TPU v7x, 256 devices: a whole 4x4x8 slice. The times are simulated.
256 devices in a mesh: ctx: 32 (over z, y), seq: 8 (over x, core).
Axes of the slice: x: 4, y: 4, z: 8, core: 2. Of those that a mesh axis runs over, the one named last changes fastest.
Arguments:
- query_input: bfloat16 [8, 4096, 2048], P('seq', 'ctx'), may hold values from -6 to 6
- key_input: bfloat16 [8, 4096, 2048], P('seq', 'ctx'), may hold values from -6 to 6
- value_input: bfloat16 [8, 4096, 2048], P('seq', 'ctx'), may hold values from -6 to 6
- cotangent: bfloat16 [8, 4096, 2048], P('seq', 'ctx'), may hold values from -6 to 6
- residues: float32 [2048, 16], replicated, may hold values from -1.5 to 1.5
- decay_rates: float32 [2048, 16], replicated, as said below
Outputs:
- output: bfloat16 [8, 4096, 2048], P('seq', 'ctx')
- grad_query: bfloat16 [8, 4096, 2048], P('seq', 'ctx')
- grad_key: bfloat16 [8, 4096, 2048], P('seq', 'ctx')
- grad_value: bfloat16 [8, 4096, 2048], P('seq', 'ctx')
- grad_residues: float32 [2048, 16], replicated
Inputs may be any that keep to these rules, and one draw needn't show every extreme that they name: `decay_rates`: every rate lies between 0.1 divided by 4096 and 1 divided by 30.
All inputs are finite; a program needn't handle non-finite values.
Results may differ from a plain program's by a relative error of at most 0.0013.
Values sent between devices are 32-bit elements; how exact they have to be, the bound alone decides.
No kernel may reach another device: no remote copies, remote signals or barrier semaphores. Data moves between devices by JAX's collectives and lax.ppermute only.
A program may use at most 192 MiB of HBM per device.

v0:
```python
import math

import jax
import jax.numpy as jnp
from jax import lax
from jax.sharding import PartitionSpec as P

HIGH = lax.Precision.HIGHEST


def phase_of(count, modulus):
    wrapped = (count + modulus // 2) % modulus - modulus // 2
    return 2.0 * math.pi / modulus * wrapped.astype(jnp.float32)


def complex_apply(joined, cosines, sines, real_part, imag_part):
    table = jnp.stack(
        [jnp.stack([cosines, -sines], axis=1), jnp.stack([sines, cosines], axis=1)], axis=0
    )
    stacked = jnp.stack([real_part, imag_part], axis=0)
    product = jnp.einsum(joined, table, stacked, precision=HIGH)
    return (product[0], product[1])


def factor_pair(length):
    first_len = math.isqrt(length)
    while length % first_len:
        first_len -= 1
    return (first_len, length // first_len)


def forward_rows(real_part, imag_part):
    leading, length, columns = real_part.shape
    first_len, second_len = factor_pair(length)
    real_grid = real_part.reshape(leading, second_len, first_len, columns)
    imag_grid = imag_part.reshape(leading, second_len, first_len, columns)
    outer_steps = jnp.arange(second_len, dtype=jnp.int32)
    inner_steps = jnp.arange(first_len, dtype=jnp.int32)
    angles = phase_of(outer_steps[:, None] * outer_steps[None, :], second_len)
    real_grid, imag_grid = complex_apply(
        "pgqb,qfbak->pfgak", jnp.cos(angles), -jnp.sin(angles), real_grid, imag_grid
    )
    twist = phase_of(outer_steps[:, None] * inner_steps[None, :], length)[None, :, :, None]
    twist_cos = jnp.cos(twist)
    twist_sin = -jnp.sin(twist)
    real_grid, imag_grid = (
        real_grid * twist_cos - imag_grid * twist_sin,
        real_grid * twist_sin + imag_grid * twist_cos,
    )
    angles = phase_of(inner_steps[:, None] * inner_steps[None, :], first_len)
    real_grid, imag_grid = complex_apply(
        "phqa,qfgak->pfhgk", jnp.cos(angles), -jnp.sin(angles), real_grid, imag_grid
    )
    return (
        real_grid.reshape(leading, length, columns),
        imag_grid.reshape(leading, length, columns),
    )


def inverse_rows(real_part, imag_part):
    leading, length, columns = real_part.shape
    first_len, second_len = factor_pair(length)
    real_grid = real_part.reshape(leading, first_len, second_len, columns)
    imag_grid = imag_part.reshape(leading, first_len, second_len, columns)
    outer_steps = jnp.arange(second_len, dtype=jnp.int32)
    inner_steps = jnp.arange(first_len, dtype=jnp.int32)
    angles = phase_of(inner_steps[:, None] * inner_steps[None, :], first_len)
    real_grid, imag_grid = complex_apply(
        "paqh,qfhgk->pfagk", jnp.cos(angles), jnp.sin(angles), real_grid, imag_grid
    )
    twist = phase_of(inner_steps[:, None] * outer_steps[None, :], length)[None, :, :, None]
    twist_cos = jnp.cos(twist)
    twist_sin = jnp.sin(twist)
    real_grid, imag_grid = (
        real_grid * twist_cos - imag_grid * twist_sin,
        real_grid * twist_sin + imag_grid * twist_cos,
    )
    angles = phase_of(outer_steps[:, None] * outer_steps[None, :], second_len)
    real_grid, imag_grid = complex_apply(
        "pbqg,qfagk->pfbak", jnp.cos(angles), jnp.sin(angles), real_grid, imag_grid
    )
    return (
        real_grid.reshape(leading, length, columns),
        imag_grid.reshape(leading, length, columns),
    )


def spectrum(signal, ctx_count, ctx_rank):
    length, columns = signal.shape
    row_count = length // ctx_count
    modulus = 2 * ctx_count * length
    spread = lax.all_to_all(
        signal.reshape(ctx_count, row_count, columns),
        "ctx",
        split_axis=0,
        concat_axis=0,
        tiled=True,
    )
    freq_steps = jnp.arange(2 * ctx_count, dtype=jnp.int32)
    source_steps = jnp.arange(ctx_count, dtype=jnp.int32)
    angles = phase_of(freq_steps[:, None] * source_steps[None, :], 2 * ctx_count)
    real_part = jnp.einsum("fj,jrk->frk", jnp.cos(angles), spread, precision=HIGH)
    imag_part = -jnp.einsum("fj,jrk->frk", jnp.sin(angles), spread, precision=HIGH)
    place = ctx_rank * row_count + jnp.arange(row_count, dtype=jnp.int32)
    twist = phase_of(freq_steps[:, None] * place[None, :], modulus)[:, :, None]
    twist_cos = jnp.cos(twist)
    twist_sin = jnp.sin(twist)
    turned_real = real_part * twist_cos + imag_part * twist_sin
    turned_imag = imag_part * twist_cos - real_part * twist_sin
    moved = lax.all_to_all(
        jnp.concatenate([turned_real, turned_imag], axis=2),
        "ctx",
        split_axis=0,
        concat_axis=1,
        tiled=True,
    )
    return forward_rows(moved[..., :columns], moved[..., columns:])


def to_signal(real_part, imag_part, ctx_count, ctx_rank):
    leading, length, columns = real_part.shape
    modulus = 2 * ctx_count * length
    back_real, back_imag = inverse_rows(real_part, imag_part)
    freq_here = 2 * ctx_rank + jnp.arange(2, dtype=jnp.int32)
    place = jnp.arange(length, dtype=jnp.int32)
    twist = phase_of(freq_here[:, None] * place[None, :], modulus)[:, :, None]
    twist_cos = jnp.cos(twist)
    twist_sin = jnp.sin(twist)
    turned_real = back_real * twist_cos - back_imag * twist_sin
    turned_imag = back_real * twist_sin + back_imag * twist_cos
    returned = lax.all_to_all(
        jnp.concatenate([turned_real, turned_imag], axis=2),
        "ctx",
        split_axis=1,
        concat_axis=0,
        tiled=True,
    )
    freq_steps = jnp.arange(2 * ctx_count, dtype=jnp.int32)
    target_steps = jnp.arange(ctx_count, dtype=jnp.int32)
    angles = phase_of(target_steps[:, None] * freq_steps[None, :], 2 * ctx_count)
    rebuilt = (
        jnp.einsum("jf,frk->jrk", jnp.cos(angles), returned[..., :columns], precision=HIGH)
        - jnp.einsum("jf,frk->jrk", jnp.sin(angles), returned[..., columns:], precision=HIGH)
    ) / modulus
    arrived = lax.all_to_all(rebuilt, "ctx", split_axis=0, concat_axis=0, tiled=True)
    return arrived.reshape(length, columns)


def filter_terms(
    mix_real, mix_imag, adj_real, adj_imag, residues, decay_rates, scaling, ctx_count, ctx_rank
):
    leading, length, channels = mix_real.shape
    modulus = 2 * ctx_count * length
    seq_length = float(ctx_count * length)
    freq_index = (2 * ctx_rank + jnp.arange(2, dtype=jnp.int32))[
        :, None
    ] + 2 * ctx_count * jnp.arange(length, dtype=jnp.int32)[None, :]
    theta = phase_of(freq_index, modulus)[None, :, :, None]
    sin_theta = jnp.sin(theta)
    half_sin = jnp.sin(0.5 * theta)
    lifted = 2.0 * half_sin * half_sin
    parity = jnp.array([1.0, -1.0], jnp.float32)[None, :, None, None]
    cross_real = adj_real * mix_real + adj_imag * mix_imag
    cross_imag = adj_imag * mix_real - adj_real * mix_imag
    rate = decay_rates.T[:, None, None, :]
    lam = jnp.exp(-rate)
    numer = 1.0 - jnp.exp(-rate * seq_length) * parity
    den_real = -jnp.expm1(-rate) + lam * lifted
    den_imag = lam * sin_theta
    ratio = numer / (den_real * den_real + den_imag * den_imag)
    geo_real = den_real * ratio
    geo_imag = -den_imag * ratio
    weight = (residues * scaling).T[:, None, None, :]
    filt_real = jnp.sum(weight * geo_real, axis=0)
    filt_imag = jnp.sum(weight * geo_imag, axis=0)
    columns = jnp.sum(cross_real[None] * geo_real + cross_imag[None] * geo_imag, axis=(1, 2))
    filter_part = columns.T * scaling / modulus
    return (filt_real, filt_imag, filter_part)


def spectral_pass(mixed, adjoint, residues, decay_rates, scaling):
    ctx_count = lax.axis_size("ctx")
    ctx_rank = lax.axis_index("ctx")
    channels = mixed.shape[1]
    spec_real, spec_imag = spectrum(jnp.concatenate([mixed, adjoint], axis=1), ctx_count, ctx_rank)
    mix_real = spec_real[..., :channels]
    mix_imag = spec_imag[..., :channels]
    adj_real = spec_real[..., channels:]
    adj_imag = spec_imag[..., channels:]
    filt_real, filt_imag, filter_part = filter_terms(
        mix_real, mix_imag, adj_real, adj_imag, residues, decay_rates, scaling, ctx_count, ctx_rank
    )
    out_real = jnp.concatenate(
        [filt_real * mix_real - filt_imag * mix_imag, filt_real * adj_real + filt_imag * adj_imag],
        axis=2,
    )
    out_imag = jnp.concatenate(
        [filt_real * mix_imag + filt_imag * mix_real, filt_real * adj_imag - filt_imag * adj_real],
        axis=2,
    )
    signal = to_signal(out_real, out_imag, ctx_count, ctx_rank)
    return (signal[:, :channels], signal[:, channels:], filter_part)


def on_device(query_input, key_input, value_input, cotangent, residues, decay_rates):
    query_wide = query_input[0].astype(jnp.float32)
    key_wide = key_input[0].astype(jnp.float32)
    value_wide = value_input[0].astype(jnp.float32)
    cot_wide = cotangent[0].astype(jnp.float32)
    length = query_wide.shape[0]
    mixed = key_wide * value_wide
    adjoint = cot_wide * query_wide
    scaling = jnp.sqrt(-jnp.expm1(-2.0 * decay_rates))
    convolved, grad_mixed, filter_part = spectral_pass(
        mixed, adjoint, residues, decay_rates, scaling
    )
    summed = lax.psum(filter_part, ("ctx", "seq"))
    grad_residues = summed / float(length * lax.axis_size("ctx") * lax.axis_size("seq"))
    output = (query_wide * convolved).astype(jnp.bfloat16)[None]
    grad_query = (cot_wide * convolved).astype(jnp.bfloat16)[None]
    grad_key = (grad_mixed * value_wide).astype(jnp.bfloat16)[None]
    grad_value = (grad_mixed * key_wide).astype(jnp.bfloat16)[None]
    return (output, grad_query, grad_key, grad_value, grad_residues)


def solution(mesh):
    return jax.shard_map(
        on_device,
        mesh=mesh,
        in_specs=(
            P("seq", "ctx", None),
            P("seq", "ctx", None),
            P("seq", "ctx", None),
            P("seq", "ctx", None),
            P(),
            P(),
        ),
        out_specs=(
            P("seq", "ctx", None),
            P("seq", "ctx", None),
            P("seq", "ctx", None),
            P("seq", "ctx", None),
            P(),
        ),
        check_vma=False,
    )
```

profile of v0, /device:TPU:32, one launch (start us, length us, event | category | flops | bytes accessed | tf_op | source)
XLA Modules:
  0.0 936.7 jit_solution(878025486541470566)
XLA Ops:
  11.3 11.4 %all-to-all-start = ((f32[32,4,4096]{2,1,0:T(4,128)}), f32[32,4,4096]{2,1,0:T(4,128)S(1)}, u32[]{:S(2)}, u32[]{:S(2)}) async-start(f32[32,4,4096]{2,1,0:T(4,128)} %pad_maximum_fusion.4), calls=%async_computation | async-start | bytes 4194304 | tf_op jit(solution)/shard_map/all_to_all | solution.py:92
  22.8 49.5 %all-to-all-done = f32[32,4,4096]{2,1,0:T(4,128)S(1)} async-done(((f32[32,4,4096]{2,1,0:T(4,128)}), f32[32,4,4096]{2,1,0:T(4,128)S(1)}, u32[]{:S(2)}, u32[]{:S(2)}) %all-to-all-start) | async-done | bytes 2097184 | tf_op jit(solution)/shard_map/all_to_all | solution.py:92
  72.3 4.7 fusion.29
  77.0 5.5 multiply_add_fusion.3
  86.3 12.2 %copy.53 = f32[64,4,8192]{2,1,0:T(4,128)} copy(f32[64,4,8192]{2,0,1:T(8,128)} %pad_maximum_fusion) | data formatting | bytes 16777216 | tf_op jit(solution)/shard_map/concatenate | solution.py:111
  98.5 6.6 all-to-all-start.1
  106.1 182.6 %all-to-all-done.1 = f32[64,4,8192]{2,1,0:T(4,128)} async-done(((f32[64,4,8192]{2,1,0:T(4,128)}), f32[64,4,8192]{2,1,0:T(4,128)}, u32[]{:S(2)}, u32[]{:S(2)}) %all-to-all-start.1) | async-done | bytes 8388640 | tf_op jit(solution)/shard_map/all_to_all | solution.py:110
  288.7 15.5 %copy.54 = f32[32,2,4,8192]{3,1,2,0:T(2,128)} copy(f32[32,2,4,8192]{3,2,1,0:T(4,128)} %bitcast.8) | data formatting | bytes 16777216 | tf_op jit(solution)/shard_map/all_to_all | solution.py:110
  304.2 11.0 %fusion.174 = (f32[2,128,4096]{2,0,1:T(2,128)}, f32[2,128,4096]{2,0,1:T(2,128)S(1)}) fusion(f32[2,128,8192]{2,0,1:T(2,128)} %bitcast.173), kind=kLoop, calls=%fused_computation.258 | loop fusion | bytes 16777216 | tf_op jit(solution)/shard_map/slice | solution.py:117
  315.1 4.6 copy.57
  322.2 11.7 %fusion.21 = f32[2,2,16,8,4096]{4,2,0,3,1:T(8,128)S(1)} fusion(f32[1,2,16,8,4096]{4,2,0,3,1:T(8,128)S(1)} %copy.58, f32[1,2,16,8,4096]{4,2,0,3,1:T(8,128)S(1)} %copy.57, f32[1,16,2,16]{3,1,2,0:T(8,128)S(1)} %get-tuple-element.37, f32[1,16,2,16]{3,1,2,0:T(8,128)S(1)} %get-tuple-element.40), kind=kOutput, calls=%fused_computation.29 | convolution fusion | flops 807404544 | bytes 16781312 | tf_op jit(solution)/shard_map/pgqb,qfbak->pfgak/dot_general | solution.py:21
  336.7 15.6 %fusion.14 = f32[2,2,8,16,4096]{4,2,0,3,1:T(8,128)S(1)} fusion(f32[2,2,16,8,4096,1]{4,2,0,3,1,5:T(8,128)S(1)} %maximum_bitcast_fusion.2, f32[1,8,2,8]{3,1,2,0:T(8,128)S(1)} %get-tuple-element.43, f32[1,8,2,8]{3,1,2,0:T(8,128)S(1)} %get-tuple-element.46), kind=kOutput, calls=%fused_computation.26 | convolution fusion | flops 402653440 | bytes 16778240 | tf_op jit(solution)/shard_map/phqa,qfgak->pfhgk/dot_general | solution.py:21
  359.9 23.0 %multiply_reduce_fusion.1 = (f32[2,128,2048]{2,1,0:T(8,128)S(1)}, f32[2,128,2048]{2,1,0:T(8,128)S(1)}, f32[16,2048]{1,0:T(8,128)S(1)}) fusion(f32[2,128]{1,0:T(2,128)S(1)} %get-tuple-element.49, f32[16,2048]{1,0:T(8,128)S(1)} %get-tuple-element.33, f32[16,2048]{1,0:T(8,128)S(1)} %get-tuple-element.35, f32[2,128]{1,0:T(2,128)S(1)} %get-tuple-element.48, ...), kind=kLoop, calls=%fused_computation.7 | loop fusion | flops 149913600 | bytes 9177088 | tf_op jit(solution)/shard_map/reduce_sum | solution.py:174
  390.7 11.6 %fusion.20 = f32[2,2,8,16,4096]{4,2,0,3,1:T(8,128)S(1)} fusion(f32[1,2,8,16,4096]{4,2,0,3,1:T(8,128)S(1)} %copy.63, f32[1,2,8,16,4096]{4,2,0,3,1:T(8,128)S(1)} %copy.62, f32[1,8,2,8]{3,1,2,0:T(8,128)S(1)} %get-tuple-element.47, f32[1,8,2,8]{3,1,2,0:T(8,128)S(1)} %get-tuple-element.42), kind=kOutput, calls=%fused_computation.28 | convolution fusion | flops 404750592 | bytes 16778240 | tf_op jit(solution)/shard_map/paqh,qfhgk->pfagk/dot_general | solution.py:21
  405.2 16.3 %fusion.17 = f32[2,2,16,8,4096]{4,2,0,3,1:T(8,128)S(1)} fusion(f32[2,2,8,16,4096,1]{4,2,0,3,1,5:T(8,128)S(1)} %maximum_bitcast_fusion.5, f32[1,16,2,16]{3,1,2,0:T(8,128)S(1)} %get-tuple-element.41, f32[1,16,2,16]{3,1,2,0:T(8,128)S(1)} %get-tuple-element.36), kind=kOutput, calls=%fused_computation.27 | convolution fusion | flops 805307392 | bytes 16781312 | tf_op jit(solution)/shard_map/pbqg,qfagk->pfbak/dot_general | solution.py:21
  422.5 8.0 fusion.26
  433.4 7.8 copy.67
  441.2 195.2 %all_to_all.46 = f32[2,128,8192]{2,0,1:T(2,128)S(1)} all-to-all(f32[2,128,8192]{2,0,1:T(2,128)S(1)} %copy.67), channel_id=1, replica_groups=mesh['ctx'=32,'seq'=8] {'ctx'}, dimensions={1} | all-to-all | bytes 16777216 | tf_op jit(solution)/shard_map/all_to_all | solution.py:131
  636.4 4.7 copy.68
  641.1 10.9 %all_to_all.40 = f32[64,4,8192]{2,0,1:T(8,128)} reshape(f32[32,2,4,8192]{3,1,0,2:T(2,128)} %copy.68) | data formatting | bytes 16777216 | tf_op jit(solution)/shard_map/all_to_all | solution.py:131
  651.9 4.0 fusion.24
  655.9 4.1 fusion.22
  662.7 6.6 all-to-all-start.3
  670.1 252.9 %all-reduce.2.cloned.1.call-done = f32[2048,16]{0,1:T(8,128)} async-done(((f32[2048,16]{0,1:T(8,128)}), f32[2048,16]{0,1:T(8,128)}) %all-reduce.2.cloned.1.call-update) | async-done | bytes 131088 | tf_op jit(solution)/shard_map/psum | solution.py:217
  (59 shorter events, 45.9 us)
Async XLA Ops:
  7.2 1.8 copy-start.3
  7.2 1.8 copy-start.1
  11.3 61.0 %all-to-all-start = ((f32[32,4,4096]{2,1,0:T(4,128)}), f32[32,4,4096]{2,1,0:T(4,128)S(1)}, u32[]{:S(2)}, u32[]{:S(2)}) async-start(f32[32,4,4096]{2,1,0:T(4,128)} %pad_maximum_fusion.4), calls=%async_computation | async-start | bytes 4194304 | tf_op jit(solution)/shard_map/all_to_all | solution.py:92
  98.5 7.2 copy-start.4
  98.5 7.2 copy-start.5
  98.5 7.4 copy-start.6
  98.5 190.2 %all-to-all-start.1 = ((f32[64,4,8192]{2,1,0:T(4,128)}), f32[64,4,8192]{2,1,0:T(4,128)}, u32[]{:S(2)}, u32[]{:S(2)}) async-start(f32[64,4,8192]{2,1,0:T(4,128)} %copy.53), calls=%async_computation.1 | async-start | bytes 16777216 | tf_op jit(solution)/shard_map/all_to_all | solution.py:110
  662.7 263.8 %copy-start = (bf16[1,128,2048]{2,1,0:T(8,128)(2,1)S(1)}, bf16[1,128,2048]{2,1,0:T(8,128)(2,1)}, u32[]{:S(2)}) copy-start(bf16[1,128,2048]{2,1,0:T(8,128)(2,1)} %param.8) | copy-start | bytes 1572868
  662.7 263.8 %copy-start.2 = (bf16[1,128,2048]{2,1,0:T(8,128)(2,1)S(1)}, bf16[1,128,2048]{2,1,0:T(8,128)(2,1)}, u32[]{:S(2)}) copy-start(bf16[1,128,2048]{2,1,0:T(8,128)(2,1)} %param.7) | copy-start | bytes 1572868
  662.7 261.8 %all-to-all-start.3 = ((f32[32,4,4096]{2,1,0:T(4,128)}), f32[32,4,4096]{2,1,0:T(4,128)}, u32[]{:S(2)}, u32[]{:S(2)}) async-start(f32[32,4,4096]{2,1,0:T(4,128)} %copy.69), calls=%async_computation.3 | async-start | bytes 4194304 | tf_op jit(solution)/shard_map/all_to_all | solution.py:145
  669.3 253.7 %all-reduce.2.cloned.1.call-start = ((), (), s32[]{:S(2)}) async-start(), calls=%async_computation.4 | async-start | bytes 262144 | tf_op jit(solution)/shard_map/psum | solution.py:217
Sparse Core Ops, SparseCore 0:
  676.2 246.7 all-reduce.1
where the time goes:
time: 949 us; the launch traced here: 937 us
  waiting for transfers between devices  485 us (51%)
  blocking collectives  195 us (21%)
  local copies, waits for them, and re-layouts  86.4 us (9%)
  matrix products  73.6 us (8%)
  other arithmetic  57.1 us (6%)
  starting transfers between devices  24.6 us (3%)
  between operations  14.9 us (2%)
    psum x1, waiting for transfers between devices, on_device(): summed = lax.psum(filter_part, ('ctx', 'seq'))  253 us
    all_to_all x1, blocking collectives, to_signal(): lax.all_to_all(jnp.concatenate([turned_real, turned_imag], axis=2), 'ctx'...  195 us
    all_to_all x1, waiting for transfers between devices, spectrum(): lax.all_to_all(jnp.concatenate([turned_real, turned_imag], axis=2), 'ctx'...  183 us
    dot_general x4, matrix products, complex_apply(): product = jnp.einsum(joined, table, stacked, precision=HIGH)  55.3 us
    all_to_all x1, waiting for transfers between devices, spectrum(): lax.all_to_all(signal.reshape(ctx_count, row_count, columns), 'ctx', spli...  49.5 us
    reduce_sum x1, other arithmetic, filter_terms(): filt_real = jnp.sum(weight * geo_real, axis=0)  23 us
  transfers between devices with their start and end apart: 4, of which 3 were waited for; matrix products, arithmetic and copies ran while one was open for 0% of the time, Pallas kernels for 0%

commit v1 on v0

v1 whole, which is shorter than its diff:
```python
import functools

import jax
import jax.numpy as jnp
from jax import lax
from jax.experimental import pallas as pl
from jax.experimental.pallas import tpu as pltpu
from jax.sharding import PartitionSpec as P

LANES = 128
SUBS = 8
MODES_TILE = 8
F32 = jnp.float32


def sub_index():
    return lax.broadcasted_iota(jnp.int32, (SUBS, LANES), 0)


def prefix_over_subs(state, decays, sub):
    total = state
    for step, decay in zip((1, 2, 4), decays, strict=True):
        total = total + jnp.where(sub >= step, pltpu.roll(total, step, 0), 0.0) * decay
    return total


def suffix_over_subs(state, decays, sub):
    total = state
    for step, decay in zip((1, 2, 4), decays, strict=True):
        total = total + jnp.where(sub < SUBS - step, pltpu.roll(total, SUBS - step, 0), 0.0) * decay
    return total


def rows_of(tile):
    return [jnp.broadcast_to(tile[m : m + 1], (SUBS, LANES)) for m in range(MODES_TILE)]


def states_kernel(
    query_ref, key_ref, value_ref, cot_ref, rates_ref, packed_ref, before_ref, after_ref, u_ref, a_ref
):
    tokens, width = query_ref.shape
    steps = tokens // SUBS
    modes = rates_ref.shape[0]
    sub = sub_index()

    def block(index, carry):
        lanes = pl.ds(pl.multiple_of(index * LANES, LANES), LANES)
        u_ref[...] = key_ref[:, lanes].astype(F32) * value_ref[:, lanes].astype(F32)
        a_ref[...] = cot_ref[:, lanes].astype(F32) * query_ref[:, lanes].astype(F32)
        for half in range(modes // MODES_TILE):
            rates = rates_ref[half * MODES_TILE : (half + 1) * MODES_TILE, lanes]
            lam = rows_of(jnp.exp(-rates))
            zero = jnp.zeros((SUBS, LANES), F32)
            fwd = [zero] * MODES_TILE
            grad = [zero] * MODES_TILE
            bwd = [zero] * MODES_TILE
            for i in range(steps):
                u = u_ref[pl.ds(i, SUBS, stride=steps), :]
                a = a_ref[pl.ds(i, SUBS, stride=steps), :]
                back = a_ref[pl.ds(steps - 1 - i, SUBS, stride=steps), :]
                for m in range(MODES_TILE):
                    fwd[m] = lam[m] * fwd[m] + u
                    grad[m] = grad[m] + a * fwd[m]
                    bwd[m] = lam[m] * bwd[m] + back
            decays = [rows_of(jnp.exp(rates * -float(steps * k))) for k in (1, 2, 4)]
            for m in range(MODES_TILE):
                decay = [d[m] for d in decays]
                upto = prefix_over_subs(fwd[m], decay, sub)
                down = suffix_over_subs(bwd[m], decay, sub)
                before = jnp.where(sub >= 1, pltpu.roll(upto, 1, 0), 0.0)
                after = jnp.where(sub < SUBS - 1, pltpu.roll(down, SUBS - 1, 0), 0.0)
                inner = grad[m] + lam[m] * bwd[m] * before
                before_ref[index, half * MODES_TILE + m] = before
                after_ref[index, half * MODES_TILE + m] = after
                packed_ref[half, index, m : m + 1, :] = upto[SUBS - 1 : SUBS]
                packed_ref[half, index, MODES_TILE + m : MODES_TILE + m + 1, :] = down[0:1]
                packed_ref[half, index, 2 * MODES_TILE + m : 2 * MODES_TILE + m + 1, :] = jnp.sum(
                    inner, axis=0, keepdims=True
                )
        return carry

    lax.fori_loop(0, width // LANES, block, 0)


def local_kernel(
    query_ref,
    key_ref,
    value_ref,
    cot_ref,
    rates_ref,
    weight_ref,
    before_ref,
    after_ref,
    conv_ref,
    grad_ref,
    u_ref,
    a_ref,
    y_ref,
    g_ref,
):
    tokens, width = query_ref.shape
    steps = tokens // SUBS
    modes = rates_ref.shape[0]

    def block(index, carry):
        lanes = pl.ds(pl.multiple_of(index * LANES, LANES), LANES)
        u_ref[...] = key_ref[:, lanes].astype(F32) * value_ref[:, lanes].astype(F32)
        a_ref[...] = cot_ref[:, lanes].astype(F32) * query_ref[:, lanes].astype(F32)
        for half in range(modes // MODES_TILE):
            picked = slice(half * MODES_TILE, (half + 1) * MODES_TILE)
            lam = rows_of(jnp.exp(-rates_ref[picked, lanes]))
            weight = rows_of(weight_ref[picked, lanes])
            fwd = [before_ref[index, half * MODES_TILE + m] for m in range(MODES_TILE)]
            for i in range(steps):
                rows = pl.ds(i, SUBS, stride=steps)
                u = u_ref[rows, :]
                total = y_ref[rows, :] if half else None
                for m in range(MODES_TILE):
                    fwd[m] = lam[m] * fwd[m] + u
                    term = weight[m] * fwd[m]
                    total = term if total is None else total + term
                y_ref[rows, :] = total
            bwd = [after_ref[index, half * MODES_TILE + m] for m in range(MODES_TILE)]
            for i in reversed(range(steps)):
                rows = pl.ds(i, SUBS, stride=steps)
                a = a_ref[rows, :]
                total = g_ref[rows, :] if half else None
                for m in range(MODES_TILE):
                    bwd[m] = lam[m] * bwd[m] + a
                    term = weight[m] * bwd[m]
                    total = term if total is None else total + term
                g_ref[rows, :] = total
        conv_ref[:, lanes] = y_ref[...]
        grad_ref[:, lanes] = g_ref[...]
        return carry

    lax.fori_loop(0, width // LANES, block, 0)


def scan_kernel(chunk_tokens, per_half, share, states_ref, rates_ref, weight_ref, scaling_ref, out_ref, part_ref):
    chunks = states_ref.shape[0]
    rank = lax.axis_index("ctx")
    rows = pl.ds(pl.multiple_of((rank // per_half) * MODES_TILE, MODES_TILE), MODES_TILE)
    lanes = pl.ds(pl.multiple_of((rank % per_half) * LANES, LANES), LANES)
    rates = rates_ref[rows, lanes]
    lam = jnp.exp(-rates)
    jump = jnp.exp(rates * -float(chunk_tokens))
    entry = weight_ref[rows, lanes] * lam
    zero = jnp.zeros((MODES_TILE, LANES), F32)
    fwd, cross, inner = zero, zero, zero
    for j in range(chunks):
        out_ref[j, 0:MODES_TILE] = entry * fwd
        cross = cross + states_ref[j, MODES_TILE : 2 * MODES_TILE] * fwd
        inner = inner + states_ref[j, 2 * MODES_TILE : 3 * MODES_TILE]
        fwd = jump * fwd + states_ref[j, 0:MODES_TILE]
    bwd = zero
    for j in reversed(range(chunks)):
        out_ref[j, MODES_TILE : 2 * MODES_TILE] = entry * bwd
        bwd = jump * bwd + states_ref[j, MODES_TILE : 2 * MODES_TILE]
    part = (inner + lam * cross) * scaling_ref[rows, lanes] * share
    for s in range(part_ref.shape[0]):
        part_ref[s] = part


def pack_kernel(states_ref, parts_ref, out_ref):
    total = parts_ref[0]
    for s in range(1, parts_ref.shape[0]):
        total = total + parts_ref[s]
    for j in range(states_ref.shape[0]):
        out_ref[j, 0 : 2 * MODES_TILE] = states_ref[j]
        out_ref[j, 2 * MODES_TILE : 3 * MODES_TILE] = total


def output_kernel(
    query_ref,
    key_ref,
    value_ref,
    cot_ref,
    rates_ref,
    conv_ref,
    grad_ref,
    entry_ref,
    out_ref,
    grad_query_ref,
    grad_key_ref,
    grad_value_ref,
    grad_res_ref,
    y_ref,
    g_ref,
):
    tokens, width = query_ref.shape
    modes = rates_ref.shape[0]
    groups = tokens // SUBS
    sub = sub_index().astype(F32)

    def block(index, carry):
        lanes = pl.ds(pl.multiple_of(index * LANES, LANES), LANES)
        for half in range(modes // MODES_TILE):
            picked = slice(half * MODES_TILE, (half + 1) * MODES_TILE)
            rates = rates_ref[picked, lanes]
            row = rows_of(rates)
            jump = rows_of(jnp.exp(rates * -float(SUBS)))
            early = rows_of(entry_ref[half, index, 0:MODES_TILE, :])
            late = rows_of(entry_ref[half, index, MODES_TILE : 2 * MODES_TILE, :])
            grad_res_ref[picked, lanes] = entry_ref[half, index, 2 * MODES_TILE : 3 * MODES_TILE, :]
            fwd = [early[m] * jnp.exp(-row[m] * sub) for m in range(MODES_TILE)]
            bwd = [late[m] * jnp.exp(-row[m] * (SUBS - 1 - sub)) for m in range(MODES_TILE)]
            for i in range(groups):
                rows = slice(i * SUBS, (i + 1) * SUBS)
                total = y_ref[rows, :] if half else conv_ref[rows, lanes]
                for m in range(MODES_TILE):
                    total = total + fwd[m]
                    fwd[m] = fwd[m] * jump[m]
                y_ref[rows, :] = total
                rows = slice((groups - 1 - i) * SUBS, (groups - i) * SUBS)
                total = g_ref[rows, :] if half else grad_ref[rows, lanes]
                for m in range(MODES_TILE):
                    total = total + bwd[m]
                    bwd[m] = bwd[m] * jump[m]
                g_ref[rows, :] = total
        y = y_ref[...]
        g = g_ref[...]
        out_ref[:, lanes] = (query_ref[:, lanes].astype(F32) * y).astype(out_ref.dtype)
        grad_query_ref[:, lanes] = (cot_ref[:, lanes].astype(F32) * y).astype(out_ref.dtype)
        grad_key_ref[:, lanes] = (value_ref[:, lanes].astype(F32) * g).astype(out_ref.dtype)
        grad_value_ref[:, lanes] = (key_ref[:, lanes].astype(F32) * g).astype(out_ref.dtype)
        return carry

    lax.fori_loop(0, width // LANES, block, 0)


def on_device(query_input, key_input, value_input, cotangent, residues, decay_rates):
    tokens, channels = query_input.shape[1:]
    modes = residues.shape[1]
    ctx_count = lax.axis_size("ctx")
    seq_count = lax.axis_size("seq")
    blocks = channels // LANES
    halves = modes // MODES_TILE
    per_step = 4
    width = per_step * LANES
    grid = (blocks // per_step,)
    signals = [s[0] for s in (query_input, key_input, value_input, cotangent)]
    rates = decay_rates.T

    signal_spec = pl.BlockSpec((tokens, width), lambda i: (0, i))
    mode_spec = pl.BlockSpec((modes, width), lambda i: (0, i))
    packed_spec = pl.BlockSpec((halves, per_step, 3 * MODES_TILE, LANES), lambda i: (0, i, 0, 0))
    border_spec = pl.BlockSpec((per_step, modes, SUBS, LANES), lambda i: (i, 0, 0, 0))
    border_shape = jax.ShapeDtypeStruct((blocks, modes, SUBS, LANES), F32)
    whole = jax.ShapeDtypeStruct((tokens, channels), F32)
    square = pltpu.VMEM((tokens, LANES), F32)

    def cost(ops, moved):
        return pl.CostEstimate(
            flops=ops * tokens * channels, bytes_accessed=moved * tokens * channels, transcendentals=0
        )

    packed, before, after = pl.pallas_call(
        states_kernel,
        grid=grid,
        in_specs=[signal_spec] * 4 + [mode_spec],
        out_specs=[packed_spec, border_spec, border_spec],
        out_shape=[
            jax.ShapeDtypeStruct((halves, blocks, 3 * MODES_TILE, LANES), F32),
            border_shape,
            border_shape,
        ],
        scratch_shapes=[square] * 2,
        cost_estimate=cost(96, 16),
        name="states",
    )(*signals, rates)

    late_rates, late_residues, packed = lax.optimization_barrier((rates, residues.T, packed))
    scaling = jnp.sqrt(-jnp.expm1(-2.0 * late_rates))
    weight = late_residues * scaling

    gathered = lax.all_to_all(
        packed.reshape(ctx_count, 3 * MODES_TILE, LANES), "ctx", split_axis=0, concat_axis=0, tiled=True
    )

    conv, grad = pl.pallas_call(
        local_kernel,
        grid=grid,
        in_specs=[signal_spec] * 4 + [mode_spec] * 2 + [border_spec] * 2,
        out_specs=[signal_spec] * 2,
        out_shape=[whole] * 2,
        scratch_shapes=[square] * 4,
        cost_estimate=cost(128, 24),
        name="local",
    )(*signals, rates, weight, before, after)

    borders, part = pl.pallas_call(
        functools.partial(scan_kernel, tokens, blocks, 1.0 / (tokens * ctx_count * seq_count)),
        out_shape=[
            jax.ShapeDtypeStruct((ctx_count, 2 * MODES_TILE, LANES), F32),
            jax.ShapeDtypeStruct((seq_count, MODES_TILE, LANES), F32),
        ],
        name="scan",
    )(gathered, rates, weight, scaling)

    parts = lax.all_to_all(part, "seq", split_axis=0, concat_axis=0, tiled=True)
    repacked = pl.pallas_call(
        pack_kernel,
        out_shape=jax.ShapeDtypeStruct((ctx_count, 3 * MODES_TILE, LANES), F32),
        name="pack",
    )(borders, parts)
    returned = lax.all_to_all(repacked, "ctx", split_axis=0, concat_axis=0, tiled=True)

    half_type = query_input.dtype
    result = jax.ShapeDtypeStruct((tokens, channels), half_type)
    output, grad_query, grad_key, grad_value, grad_residues = pl.pallas_call(
        output_kernel,
        grid=grid,
        in_specs=[signal_spec] * 4 + [mode_spec] + [signal_spec] * 2 + [packed_spec],
        out_specs=[signal_spec] * 4 + [mode_spec],
        out_shape=[result] * 4 + [jax.ShapeDtypeStruct((modes, channels), F32)],
        scratch_shapes=[square] * 2,
        cost_estimate=cost(64, 24),
        name="outputs",
    )(*signals, rates, conv, grad, returned.reshape(halves, blocks, 3 * MODES_TILE, LANES))
    return (output[None], grad_query[None], grad_key[None], grad_value[None], grad_residues.T)


def solution(mesh):
    split = P("seq", "ctx", None)
    return jax.shard_map(
        on_device,
        mesh=mesh,
        in_specs=(split, split, split, split, P(), P()),
        out_specs=(split, split, split, split, P()),
        check_vma=False,
    )
```

time: 949 us -> 76 us (0.08); the launches traced: 937 us -> 75.5 us
  waiting for transfers between devices: 485 us -> 20.2 us
  blocking collectives: 195 us -> 9.85 us
  local copies, waits for them, and re-layouts: 86.4 us -> 1.49 us
  matrix products: 73.6 us -> 0 us
  other arithmetic: 57.1 us -> 0.79 us
  Pallas kernels: 0 us -> 26.1 us
  between operations: 14.9 us -> 0.67 us
    psum x1 -> x0, waiting for transfers between devices: 253 us -> none  [on_device(): summed = lax.psum(filter_part, ('ctx', 'seq'))]
    all_to_all x3 -> x2, waiting for transfers between devices: 232 us -> 20.2 us  [the longest x1 13.9 us: on_device(): lax.all_to_all(packed.reshape(ctx_count, 3 * MODES_TILE, LANES), 'ctx', s...]
    all_to_all x1, blocking collectives: 195 us -> 9.85 us  [on_device(): parts = lax.all_to_all(part, 'seq', split_axis=0, concat_axis=0, tiled=True)]
    dot_general x8 -> x0, matrix products: 73.6 us -> none  [the longest x4 55.3 us: complex_apply(): product = jnp.einsum(joined, table, stacked, precision=HIGH)]
    all_to_all x3 -> x0, local copies, waits for them, and re-layouts: 31 us -> none  [the longest x2 15.5 us: to_signal(): lax.all_to_all(jnp.concatenate([turned_real, turned_imag], axis=2), 'ctx'...]
    pallas_call x0 -> x5, Pallas kernels: none -> 26.1 us  [the longest x1 8.33 us: on_device(): pl.pallas_call(local_kernel, grid=grid, in_specs=[signal_spec] * 4 + [mod...]
    reduce_sum x1 -> x0, other arithmetic: 23 us -> none  [filter_terms(): filt_real = jnp.sum(weight * geo_real, axis=0)]
    concatenate x2 -> x0, local copies, waits for them, and re-layouts: 20 us -> none  [the longest x1 12.2 us: spectrum(): jnp.concatenate([turned_real, turned_imag], axis=2)]
  transfers between devices with their start and end apart: 4 -> 2, of which waited for: 3 -> 2; matrix products, arithmetic and copies ran while one was open for 0% -> 1% of each run, Pallas kernels for 0% -> 11%
where the time goes in v1:
time: 76 us; the launch traced here: 75.5 us
  Pallas kernels  26.1 us (34%)
  waiting for transfers between devices  20.2 us (27%)
  starting transfers between devices  16.4 us (22%)
  blocking collectives  9.85 us (13%)
  local copies, waits for them, and re-layouts  1.49 us (2%)
  other arithmetic  0.79 us (1%)
    all_to_all x1, waiting for transfers between devices, on_device(): lax.all_to_all(packed.reshape(ctx_count, 3 * MODES_TILE, LANES), 'ctx', s...  13.9 us
    all_to_all x1, starting transfers between devices, on_device(): lax.all_to_all(packed.reshape(ctx_count, 3 * MODES_TILE, LANES), 'ctx', s...  11.5 us
    all_to_all x1, blocking collectives, on_device(): parts = lax.all_to_all(part, 'seq', split_axis=0, concat_axis=0, tiled=True)  9.85 us
    pallas_call x1, Pallas kernels, on_device(): pl.pallas_call(local_kernel, grid=grid, in_specs=[signal_spec] * 4 + [mod...  8.33 us
    pallas_call x1, Pallas kernels, on_device(): pl.pallas_call(states_kernel, grid=grid, in_specs=[signal_spec] * 4 + [mo...  7.81 us
    all_to_all x1, waiting for transfers between devices, on_device(): lax.all_to_all(repacked, 'ctx', split_axis=0, concat_axis=0, tiled=True)  6.33 us
    pallas_call x1, Pallas kernels, on_device(): pl.pallas_call(output_kernel, grid=grid, in_specs=[signal_spec] * 4 + [mo...  6.29 us
    all_to_all x1, starting transfers between devices, on_device(): lax.all_to_all(repacked, 'ctx', split_axis=0, concat_axis=0, tiled=True)  4.88 us
  transfers between devices with their start and end apart: 2, of which 2 were waited for; matrix products, arithmetic and copies ran while one was open for 1% of the time, Pallas kernels for 11%

profile of v1, /device:TPU:32, one launch (start us, length us, event | category | flops | bytes accessed | tf_op | source)
XLA Modules:
  0.0 75.5 jit_solution(8031339930704422685)
XLA Ops:
  0.6 7.8 %states.1 = (f32[2,16,24,128]{3,2,1,0:T(8,128)}, f32[16,16,8,128]{3,2,1,0:T(8,128)}, f32[16,16,8,128]{3,2,1,0:T(8,128)}) custom-call(bf16[128,2048]{1,0:T(8,128)(2,1)} %bitcast.13, bf16[128,2048]{1,0:T(8,128)(2,1)} %bitcast.16, bf16[128,2048]{1,0:T(8,128)(2,1)} %bitcast.19, bf16[128,2048]{1,0:T(8,128)(2,1)} %bitcast.22, f32[16,2048]{1,0:T(8,128)} %bitcast.25), custom_call_target="tpu_custom_call" | custom-call | flops 25165824 | bytes 4194304 | tf_op jit(solution)/shard_map/states/pallas_call | solution.py:258
  8.4 0.0 copy-start
  8.4 0.0 copy-start.3
  8.4 11.5 %all-to-all-start = ((f32[32,24,128]{2,1,0:T(8,128)}), f32[32,24,128]{2,1,0:T(8,128)S(1)}, u32[]{:S(2)}, u32[]{:S(2)}) async-start(f32[32,24,128]{2,1,0:T(8,128)} %bitcast.31), calls=%async_computation | async-start | bytes 786432 | tf_op jit(solution)/shard_map/all_to_all | solution.py:277
  20.0 0.0 copy-done
  20.0 0.0 copy-done.3
  20.0 0.8 %negate_sqrt_fusion = (f32[16,2048]{1,0:T(8,128)}, f32[16,2048]{1,0:T(8,128)}) fusion(f32[16,2048]{1,0:T(8,128)S(1)} %bitcast.29, f32[16,2048]{1,0:T(8,128)S(1)} %bitcast.32), kind=kLoop, calls=%fused_computation | loop fusion | flops 98304 | bytes 524288 | tf_op jit(solution)/shard_map/sqrt | solution.py:274
  20.8 13.9 %all-to-all-done.states_ref = f32[32,24,128]{2,1,0:T(8,128)S(1)} async-done(((f32[32,24,128]{2,1,0:T(8,128)}), f32[32,24,128]{2,1,0:T(8,128)S(1)}, u32[]{:S(2)}, u32[]{:S(2)}) %all-to-all-start) | async-done | bytes 393248 | tf_op jit(solution)/shard_map/all_to_all | solution.py:277
  34.7 0.0 copy-start.2
  34.7 0.7 copy-done.2
  35.4 1.9 %scan.1 = (f32[32,16,128]{2,1,0:T(8,128)}, f32[8,8,128]{2,1,0:T(8,128)}) custom-call(f32[32,24,128]{2,1,0:T(8,128)} %copy-done.2, f32[16,2048]{1,0:T(8,128)} %bitcast.26, f32[16,2048]{1,0:T(8,128)} %get-tuple-element.36.weight_ref, f32[16,2048]{1,0:T(8,128)} %get-tuple-element.35.scaling_ref), custom_call_target="tpu_custom_call" | custom-call | tf_op jit(solution)/shard_map/scan/pallas_call | solution.py:292
  37.3 9.8 %all_to_all.15.parts_ref = f32[8,8,128]{2,1,0:T(8,128)} all-to-all(f32[8,8,128]{2,1,0:T(8,128)} %get-tuple-element.29), channel_id=1, replica_groups=mesh['ctx'=32,'seq'=8] {'seq'}, dimensions={0} | all-to-all | bytes 65536 | tf_op jit(solution)/shard_map/all_to_all | solution.py:301
  47.2 1.7 %pack.1 = f32[32,24,128]{2,1,0:T(8,128)} custom-call(f32[32,16,128]{2,1,0:T(8,128)} %get-tuple-element.28.states_ref, f32[8,8,128]{2,1,0:T(8,128)} %all_to_all.15.parts_ref), custom_call_target="tpu_custom_call" | custom-call | tf_op jit(solution)/shard_map/pack/pallas_call | solution.py:302
  48.9 4.9 %all-to-all-start.2 = ((f32[32,24,128]{2,1,0:T(8,128)}), f32[32,24,128]{2,1,0:T(8,128)S(1)}, u32[]{:S(2)}, u32[]{:S(2)}) async-start(f32[32,24,128]{2,1,0:T(8,128)} %pack.1), calls=%async_computation.2 | async-start | bytes 786432 | tf_op jit(solution)/shard_map/all_to_all | solution.py:307
  53.8 8.3 %local.1 = (f32[128,2048]{1,0:T(8,128)}, f32[128,2048]{1,0:T(8,128)}) custom-call(bf16[128,2048]{1,0:T(8,128)(2,1)} %bitcast.14, bf16[128,2048]{1,0:T(8,128)(2,1)} %bitcast.17, bf16[128,2048]{1,0:T(8,128)(2,1)} %bitcast.20, bf16[128,2048]{1,0:T(8,128)(2,1)} %bitcast.23, f32[16,2048]{1,0:T(8,128)} %bitcast.27, f32[16,2048]{1,0:T(8,128)} %get-tuple-element.36.weight_ref, ...), custom_call_target="tpu_custom_call" | custom-call | flops 33554432 | bytes 6291456 | tf_op jit(solution)/shard_map/local/pallas_call | solution.py:281
  62.1 6.3 %all-to-all-done.2 = f32[32,24,128]{2,1,0:T(8,128)S(1)} async-done(((f32[32,24,128]{2,1,0:T(8,128)}), f32[32,24,128]{2,1,0:T(8,128)S(1)}, u32[]{:S(2)}, u32[]{:S(2)}) %all-to-all-start.2) | async-done | bytes 393248 | tf_op jit(solution)/shard_map/all_to_all | solution.py:307
  68.4 0.0 copy-start.1
  68.4 0.7 copy-done.1
  69.2 6.3 %outputs.1 = (bf16[128,2048]{1,0:T(8,128)(2,1)}, bf16[128,2048]{1,0:T(8,128)(2,1)}, bf16[128,2048]{1,0:T(8,128)(2,1)}, bf16[128,2048]{1,0:T(8,128)(2,1)}, f32[16,2048]{1,0:T(8,128)}) custom-call(bf16[128,2048]{1,0:T(8,128)(2,1)} %bitcast.15, bf16[128,2048]{1,0:T(8,128)(2,1)} %bitcast.18, bf16[128,2048]{1,0:T(8,128)(2,1)} %bitcast.21, ...), custom_call_target="tpu_custom_call" | custom-call | flops 16777216 | bytes 6291456 | tf_op jit(solution)/shard_map/outputs/pallas_call | solution.py:311
Async XLA Ops:
  8.4 11.5 %copy-start = (f32[2048,16]{0,1:T(8,128)S(1)}, f32[2048,16]{0,1:T(8,128)}, u32[]{:S(2)}) copy-start(f32[2048,16]{0,1:T(8,128)} %param.11) | copy-start | bytes 393220
  8.4 11.5 %copy-start.3 = (f32[2048,16]{0,1:T(8,128)S(1)}, f32[2048,16]{0,1:T(8,128)}, u32[]{:S(2)}) copy-start(f32[2048,16]{0,1:T(8,128)} %param.10) | copy-start | bytes 393220
  8.4 26.2 %all-to-all-start = ((f32[32,24,128]{2,1,0:T(8,128)}), f32[32,24,128]{2,1,0:T(8,128)S(1)}, u32[]{:S(2)}, u32[]{:S(2)}) async-start(f32[32,24,128]{2,1,0:T(8,128)} %bitcast.31), calls=%async_computation | async-start | bytes 786432 | tf_op jit(solution)/shard_map/all_to_all | solution.py:277
  34.7 0.7 copy-start.2
  48.9 19.5 %all-to-all-start.2 = ((f32[32,24,128]{2,1,0:T(8,128)}), f32[32,24,128]{2,1,0:T(8,128)S(1)}, u32[]{:S(2)}, u32[]{:S(2)}) async-start(f32[32,24,128]{2,1,0:T(8,128)} %pack.1), calls=%async_computation.2 | async-start | bytes 786432 | tf_op jit(solution)/shard_map/all_to_all | solution.py:307
  68.4 0.7 copy-start.1

commit v2 on v1

v2 whole, which is shorter than its diff:
```python
import functools

import jax
import jax.numpy as jnp
from jax import lax
from jax.experimental import pallas as pl
from jax.experimental.pallas import tpu as pltpu
from jax.sharding import PartitionSpec as P

LANES = 128
SUBS = 8
MODES_TILE = 8
F32 = jnp.float32
GROUPS = 4
PITCH = 17
SMALL_VMEM = 12 * 1024 * 1024
STATES_VMEM = 58 * 1024 * 1024
OUTPUTS_VMEM = 51 * 1024 * 1024


def sub_index():
    return lax.broadcasted_iota(jnp.int32, (SUBS, LANES), 0)


def rows_of(tile):
    return [jnp.broadcast_to(tile[m : m + 1], (SUBS, LANES)) for m in range(MODES_TILE)]


def states_kernel(
    query_hbm,
    key_hbm,
    value_hbm,
    cot_hbm,
    rates_hbm,
    packed_hbm,
    before_hbm,
    after_hbm,
    query_ref,
    key_ref,
    value_ref,
    cot_ref,
    rates_ref,
    packed_ref,
    before_ref,
    after_ref,
    rates_arrived,
    arrived,
    sent,
    u_ref,
    a_ref,
    lag_ref,
    lag_sum_ref,
    fwd_ref,
    bwd_ref,
):
    tokens, width = query_ref.shape
    steps = tokens // SUBS
    modes = rates_ref.shape[0]
    groups = arrived.shape[1]
    span = width // groups
    pairs = ((query_hbm, query_ref), (key_hbm, key_ref), (value_hbm, value_ref), (cot_hbm, cot_ref))

    def fetches(group):
        lanes = pl.ds(pl.multiple_of(group * span, span), span)
        return [
            pltpu.make_async_copy(source.at[:, lanes], target.at[:, lanes], arrived.at[n, group])
            for n, (source, target) in enumerate(pairs)
        ]

    def stores(group):
        count = span // LANES
        part = pl.ds(group * count, count)
        return [
            pltpu.make_async_copy(packed_ref.at[:, part], packed_hbm.at[:, part], sent.at[0, group]),
            pltpu.make_async_copy(before_ref.at[part], before_hbm.at[part], sent.at[1, group]),
            pltpu.make_async_copy(after_ref.at[part], after_hbm.at[part], sent.at[2, group]),
        ]

    rates_fetch = pltpu.make_async_copy(rates_hbm, rates_ref, rates_arrived)
    for group in range(groups):
        for fetch in fetches(group):
            fetch.start()
        if group == 0:
            rates_fetch.start()
    rates_fetch.wait()

    def block(index, carry):
        lanes = pl.ds(pl.multiple_of(index * LANES, LANES), LANES)
        mixed = key_ref[:, lanes].astype(F32) * value_ref[:, lanes].astype(F32)
        adjoint = cot_ref[:, lanes].astype(F32) * query_ref[:, lanes].astype(F32)
        for s in range(SUBS):
            u_ref[s * PITCH : s * PITCH + steps, :] = mixed[s * steps : (s + 1) * steps]
            a_ref[s * PITCH : s * PITCH + steps, :] = adjoint[s * steps : (s + 1) * steps]
        u = [u_ref[pl.ds(i, SUBS, stride=PITCH), :] for i in range(steps)]
        a = [a_ref[pl.ds(i, SUBS, stride=PITCH), :] for i in range(steps)]
        for lag in range(steps):
            total = a[lag] * u[0]
            for i in range(1, steps - lag):
                total = total + a[lag + i] * u[i]
            lag_ref[lag * SUBS : (lag + 1) * SUBS, :] = total
        for group in range(steps // SUBS):
            total = None
            for s in range(SUBS):
                term = lag_ref[pl.ds(group * SUBS * SUBS + s, SUBS, stride=SUBS), :]
                total = term if total is None else total + term
            lag_sum_ref[group * SUBS : (group + 1) * SUBS, :] = total
        for half in range(modes // MODES_TILE):
            rates = rates_ref[half * MODES_TILE : (half + 1) * MODES_TILE, lanes]
            lam_tile = jnp.exp(-rates)
            lam = rows_of(lam_tile)
            fwd = [u_ref[pl.ds(0, SUBS, stride=PITCH), :]] * MODES_TILE
            bwd = [a_ref[pl.ds(steps - 1, SUBS, stride=PITCH), :]] * MODES_TILE
            for i in range(1, steps):
                front = u_ref[pl.ds(i, SUBS, stride=PITCH), :]
                back = a_ref[pl.ds(steps - 1 - i, SUBS, stride=PITCH), :]
                for m in range(MODES_TILE):
                    fwd[m] = lam[m] * fwd[m] + front
                    bwd[m] = lam[m] * bwd[m] + back
            for m in range(MODES_TILE):
                fwd_ref[m * SUBS : (m + 1) * SUBS, :] = fwd[m]
                bwd_ref[m * SUBS : (m + 1) * SUBS, :] = bwd[m]
            jump = jnp.exp(rates * -float(steps))
            zero = jnp.zeros((MODES_TILE, LANES), F32)
            before, after, cross, inner = zero, zero, zero, zero
            for s in range(SUBS):
                rows = pl.ds(s, MODES_TILE, stride=SUBS)
                before_ref[index, half, rows, :] = before
                cross = cross + bwd_ref[rows, :] * before
                before = jump * before + fwd_ref[rows, :]
            for s in reversed(range(SUBS)):
                rows = pl.ds(s, MODES_TILE, stride=SUBS)
                after_ref[index, half, rows, :] = after
                after = jump * after + bwd_ref[rows, :]
            for lag in reversed(range(steps)):
                inner = inner * lam_tile + lag_sum_ref[lag : lag + 1, :]
            packed_ref[half, index, 0:MODES_TILE, :] = before
            packed_ref[half, index, MODES_TILE : 2 * MODES_TILE, :] = after
            packed_ref[half, index, 2 * MODES_TILE : 3 * MODES_TILE, :] = inner + lam_tile * cross
        return carry

    def column(group, carry):
        for fetch in fetches(group):
            fetch.wait()
        per_group = span // LANES
        carry = lax.fori_loop(group * per_group, (group + 1) * per_group, block, carry)
        for store in stores(group):
            store.start()
        return carry

    lax.fori_loop(0, groups, column, 0)
    for group in range(groups):
        for store in stores(group):
            store.wait()


def local_kernel(
    query_ref,
    key_ref,
    value_ref,
    cot_ref,
    rates_ref,
    weight_ref,
    before_ref,
    after_ref,
    conv_ref,
    grad_ref,
    u_ref,
    a_ref,
    y_ref,
    g_ref,
):
    tokens, width = query_ref.shape
    steps = tokens // SUBS
    modes = rates_ref.shape[0]

    def block(index, carry):
        lanes = pl.ds(pl.multiple_of(index * LANES, LANES), LANES)
        u_ref[...] = key_ref[:, lanes].astype(F32) * value_ref[:, lanes].astype(F32)
        a_ref[...] = cot_ref[:, lanes].astype(F32) * query_ref[:, lanes].astype(F32)
        for half in range(modes // MODES_TILE):
            picked = slice(half * MODES_TILE, (half + 1) * MODES_TILE)
            lam = rows_of(jnp.exp(-rates_ref[picked, lanes]))
            weight = rows_of(weight_ref[picked, lanes])
            fwd = [before_ref[index, half, m * SUBS : (m + 1) * SUBS, :] for m in range(MODES_TILE)]
            for i in range(steps):
                rows = pl.ds(i, SUBS, stride=steps)
                u = u_ref[rows, :]
                total = y_ref[rows, :] if half else None
                for m in range(MODES_TILE):
                    fwd[m] = lam[m] * fwd[m] + u
                    term = weight[m] * fwd[m]
                    total = term if total is None else total + term
                y_ref[rows, :] = total
            bwd = [after_ref[index, half, m * SUBS : (m + 1) * SUBS, :] for m in range(MODES_TILE)]
            for i in reversed(range(steps)):
                rows = pl.ds(i, SUBS, stride=steps)
                a = a_ref[rows, :]
                total = g_ref[rows, :] if half else None
                for m in range(MODES_TILE):
                    bwd[m] = lam[m] * bwd[m] + a
                    term = weight[m] * bwd[m]
                    total = term if total is None else total + term
                g_ref[rows, :] = total
        conv_ref[:, lanes] = y_ref[...]
        grad_ref[:, lanes] = g_ref[...]
        return carry

    lax.fori_loop(0, width // LANES, block, 0)


def scan_kernel(chunk_tokens, per_half, share, states_ref, rates_ref, weight_ref, scaling_ref, out_ref, part_ref):
    chunks = states_ref.shape[0]
    rank = lax.axis_index("ctx")
    rows = pl.ds(pl.multiple_of((rank // per_half) * MODES_TILE, MODES_TILE), MODES_TILE)
    lanes = pl.ds(pl.multiple_of((rank % per_half) * LANES, LANES), LANES)
    rates = rates_ref[rows, lanes]
    lam = jnp.exp(-rates)
    jump = jnp.exp(rates * -float(chunk_tokens))
    entry = weight_ref[rows, lanes] * lam
    zero = jnp.zeros((MODES_TILE, LANES), F32)
    fwd, cross, inner = zero, zero, zero
    for j in range(chunks):
        out_ref[j, 0:MODES_TILE] = entry * fwd
        cross = cross + states_ref[j, MODES_TILE : 2 * MODES_TILE] * fwd
        inner = inner + states_ref[j, 2 * MODES_TILE : 3 * MODES_TILE]
        fwd = jump * fwd + states_ref[j, 0:MODES_TILE]
    bwd = zero
    for j in reversed(range(chunks)):
        out_ref[j, MODES_TILE : 2 * MODES_TILE] = entry * bwd
        bwd = jump * bwd + states_ref[j, MODES_TILE : 2 * MODES_TILE]
    part = (inner + lam * cross) * scaling_ref[rows, lanes] * share
    for s in range(part_ref.shape[0]):
        part_ref[s] = part


def pack_kernel(states_ref, parts_ref, out_ref):
    total = parts_ref[0]
    for s in range(1, parts_ref.shape[0]):
        total = total + parts_ref[s]
    for j in range(out_ref.shape[0]):
        out_ref[j, 0 : 2 * MODES_TILE] = states_ref[j]
        out_ref[j, 2 * MODES_TILE : 3 * MODES_TILE] = total


def output_kernel(
    query_ref,
    key_ref,
    value_ref,
    cot_ref,
    rates_ref,
    conv_hbm,
    grad_hbm,
    entry_ref,
    out_hbm,
    grad_query_hbm,
    grad_key_hbm,
    grad_value_hbm,
    grad_res_hbm,
    grad_res_ref,
    conv_ref,
    grad_ref,
    out_ref,
    grad_query_ref,
    grad_key_ref,
    grad_value_ref,
    arrived,
    sent,
    y_ref,
    g_ref,
):
    tokens, width = query_ref.shape
    modes = rates_ref.shape[0]
    groups = tokens // SUBS
    sub = sub_index().astype(F32)
    columns = sent.shape[1]
    span = width // columns
    pairs = (
        (out_ref, out_hbm),
        (grad_query_ref, grad_query_hbm),
        (grad_key_ref, grad_key_hbm),
        (grad_value_ref, grad_value_hbm),
        (grad_res_ref, grad_res_hbm),
    )

    inputs = (
        (conv_hbm, conv_ref),
        (grad_hbm, grad_ref),
    )

    def fetches(column):
        lanes = pl.ds(pl.multiple_of(column * span, span), span)
        return [
            pltpu.make_async_copy(source.at[:, lanes], target.at[:, lanes], arrived.at[n, column])
            for n, (source, target) in enumerate(inputs)
        ]

    for column in range(columns):
        for fetch in fetches(column):
            fetch.start()

    def stores(column):
        lanes = pl.ds(pl.multiple_of(column * span, span), span)
        return [
            pltpu.make_async_copy(source.at[:, lanes], target.at[:, lanes], sent.at[n, column])
            for n, (source, target) in enumerate(pairs)
        ]

    def entry(index, carry):
        lanes = pl.ds(pl.multiple_of(index * LANES, LANES), LANES)
        for half in range(modes // MODES_TILE):
            picked = slice(half * MODES_TILE, (half + 1) * MODES_TILE)
            rates = rates_ref[picked, lanes]
            row = rows_of(rates)
            jump = rows_of(jnp.exp(rates * -float(SUBS)))
            early = rows_of(entry_ref[half, index, 0:MODES_TILE, :])
            late = rows_of(entry_ref[half, index, MODES_TILE : 2 * MODES_TILE, :])
            grad_res_ref[picked, lanes] = entry_ref[half, index, 2 * MODES_TILE : 3 * MODES_TILE, :]
            fwd = [early[m] * jnp.exp(-row[m] * sub) for m in range(MODES_TILE)]
            bwd = [late[m] * jnp.exp(-row[m] * (SUBS - 1 - sub)) for m in range(MODES_TILE)]
            for i in range(groups):
                rows = slice(i * SUBS, (i + 1) * SUBS)
                total = y_ref[rows, lanes] if half else None
                for m in range(MODES_TILE):
                    total = fwd[m] if total is None else total + fwd[m]
                    fwd[m] = fwd[m] * jump[m]
                y_ref[rows, lanes] = total
                rows = slice((groups - 1 - i) * SUBS, (groups - i) * SUBS)
                total = g_ref[rows, lanes] if half else None
                for m in range(MODES_TILE):
                    total = bwd[m] if total is None else total + bwd[m]
                    bwd[m] = bwd[m] * jump[m]
                g_ref[rows, lanes] = total
        return carry

    def finish(index, carry):
        lanes = pl.ds(pl.multiple_of(index * LANES, LANES), LANES)
        y = y_ref[:, lanes] + conv_ref[:, lanes]
        g = g_ref[:, lanes] + grad_ref[:, lanes]
        out_ref[:, lanes] = (query_ref[:, lanes].astype(F32) * y).astype(out_ref.dtype)
        grad_query_ref[:, lanes] = (cot_ref[:, lanes].astype(F32) * y).astype(out_ref.dtype)
        grad_key_ref[:, lanes] = (value_ref[:, lanes].astype(F32) * g).astype(out_ref.dtype)
        grad_value_ref[:, lanes] = (key_ref[:, lanes].astype(F32) * g).astype(out_ref.dtype)
        return carry

    def column_step(column, carry):
        first, last = column * (span // LANES), (column + 1) * (span // LANES)
        carry = lax.fori_loop(first, last, entry, carry)
        for fetch in fetches(column):
            fetch.wait()
        carry = lax.fori_loop(first, last, finish, carry)
        for store in stores(column):
            store.start()
        return carry

    lax.fori_loop(0, columns, column_step, 0)
    for column in range(columns):
        for store in stores(column):
            store.wait()


def on_device(query_input, key_input, value_input, cotangent, residues, decay_rates):
    tokens, channels = query_input.shape[1:]
    modes = residues.shape[1]
    ctx_count = lax.axis_size("ctx")
    seq_count = lax.axis_size("seq")
    blocks = channels // LANES
    halves = modes // MODES_TILE
    signals = [s[0] for s in (query_input, key_input, value_input, cotangent)]
    rates = decay_rates.T

    here = pl.BlockSpec(memory_space=pltpu.VMEM)
    there = pl.BlockSpec(memory_space=pltpu.HBM)
    border = jax.ShapeDtypeStruct((blocks, halves, MODES_TILE * SUBS, LANES), F32)
    whole = jax.ShapeDtypeStruct((tokens, channels), F32)
    square = pltpu.VMEM((tokens, LANES), F32)
    tile = pltpu.VMEM((MODES_TILE * SUBS, LANES), F32)
    signal_type = query_input.dtype
    signal_buffer = pltpu.VMEM((tokens, channels), signal_type)
    small = pltpu.CompilerParams(vmem_limit_bytes=SMALL_VMEM)

    def cost(ops, moved):
        return pl.CostEstimate(
            flops=ops * tokens * channels, bytes_accessed=moved * tokens * channels, transcendentals=0
        )

    packed, before, after = pl.pallas_call(
        states_kernel,
        in_specs=[there] * 5,
        out_specs=[there] * 3,
        out_shape=[jax.ShapeDtypeStruct((halves, blocks, 3 * MODES_TILE, LANES), F32), border, border],
        scratch_shapes=[signal_buffer] * 4
        + [
            pltpu.VMEM((modes, channels), F32),
            pltpu.VMEM((halves, blocks, 3 * MODES_TILE, LANES), F32),
            pltpu.VMEM(border.shape, F32),
            pltpu.VMEM(border.shape, F32),
            pltpu.SemaphoreType.DMA(()),
            pltpu.SemaphoreType.DMA((4, GROUPS)),
            pltpu.SemaphoreType.DMA((3, GROUPS)),
            pltpu.VMEM((SUBS * PITCH, LANES), F32),
            pltpu.VMEM((SUBS * PITCH, LANES), F32),
            square,
            pltpu.VMEM((tokens // SUBS, LANES), F32),
            tile,
            tile,
        ],
        compiler_params=pltpu.CompilerParams(vmem_limit_bytes=STATES_VMEM),
        cost_estimate=cost(96, 16),
        name="states",
    )(*signals, rates)

    late_rates, late_residues, packed = lax.optimization_barrier((rates, residues.T, packed))
    scaling = jnp.sqrt(-jnp.expm1(-2.0 * late_rates))
    weight = late_residues * scaling

    gathered = lax.all_to_all(
        packed.reshape(ctx_count, 3 * MODES_TILE, LANES), "ctx", split_axis=0, concat_axis=0, tiled=True
    )

    per_step = blocks // GROUPS
    signal_spec = pl.BlockSpec((tokens, per_step * LANES), lambda i: (0, i))
    mode_spec = pl.BlockSpec((modes, per_step * LANES), lambda i: (0, i))
    border_spec = pl.BlockSpec((per_step, halves, MODES_TILE * SUBS, LANES), lambda i: (i, 0, 0, 0))
    conv, grad = pl.pallas_call(
        local_kernel,
        grid=(GROUPS,),
        in_specs=[signal_spec] * 4 + [mode_spec] * 2 + [border_spec] * 2,
        out_specs=[signal_spec] * 2,
        out_shape=[whole] * 2,
        scratch_shapes=[square] * 4,
        cost_estimate=cost(128, 24),
        name="local",
    )(*signals, rates, weight, before, after)
    gathered, conv, grad = lax.optimization_barrier((gathered, conv, grad))

    borders, part = pl.pallas_call(
        functools.partial(scan_kernel, tokens, blocks, 1.0 / (tokens * ctx_count * seq_count)),
        in_specs=[here] * 4,
        out_specs=[here] * 2,
        out_shape=[
            jax.ShapeDtypeStruct((ctx_count, 2 * MODES_TILE, LANES), F32),
            jax.ShapeDtypeStruct((seq_count, MODES_TILE, LANES), F32),
        ],
        compiler_params=small,
        name="scan",
    )(gathered, rates, weight, scaling)

    parts = lax.all_to_all(part, "seq", split_axis=0, concat_axis=0, tiled=True)
    repacked = pl.pallas_call(
        pack_kernel,
        in_specs=[here] * 2,
        out_specs=here,
        out_shape=jax.ShapeDtypeStruct((ctx_count, 3 * MODES_TILE, LANES), F32),
        compiler_params=small,
        name="pack",
    )(borders, parts)
    returned = lax.all_to_all(repacked, "ctx", split_axis=0, concat_axis=0, tiled=True)

    result = jax.ShapeDtypeStruct((tokens, channels), signal_type)
    *results, grad_rows = pl.pallas_call(
        output_kernel,
        in_specs=[here] * 5 + [there] * 2 + [here],
        out_specs=[there] * 5,
        out_shape=[result] * 4 + [jax.ShapeDtypeStruct((modes, channels), F32)],
        scratch_shapes=[pltpu.VMEM((modes, channels), F32)]
        + [pltpu.VMEM((tokens, channels), F32)] * 2
        + [signal_buffer] * 4
        + [pltpu.SemaphoreType.DMA((2, GROUPS)), pltpu.SemaphoreType.DMA((5, GROUPS))]
        + [pltpu.VMEM((tokens, channels), F32)] * 2,
        compiler_params=pltpu.CompilerParams(vmem_limit_bytes=OUTPUTS_VMEM),
        cost_estimate=cost(64, 24),
        name="outputs",
    )(*signals, rates, conv, grad, returned.reshape(halves, blocks, 3 * MODES_TILE, LANES))
    return (*[r[None] for r in results], grad_rows.T)


def solution(mesh):
    split = P("seq", "ctx", None)
    return jax.shard_map(
        on_device,
        mesh=mesh,
        in_specs=(split, split, split, split, P(), P()),
        out_specs=(split, split, split, split, P()),
        check_vma=False,
    )
```

time: 76 us -> 69.2 us (0.911)
  blocking collectives: 9.85 us -> 29.1 us
  waiting for transfers between devices: 20.2 us -> 5.62 us
  Pallas kernels: 26.1 us -> 21.1 us
  starting transfers between devices: 16.4 us -> 11.5 us
  local copies, waits for them, and re-layouts: 1.49 us -> 0.04 us
    all_to_all x0 -> x1, blocking collectives: none -> 19.5 us  [on_device(): lax.all_to_all(repacked, 'ctx', split_axis=0, concat_axis=0, tiled=True)]
    all_to_all x1, waiting for transfers between devices: 13.9 us -> 5.62 us  [on_device(): lax.all_to_all(packed.reshape(ctx_count, 3 * MODES_TILE, LANES), 'ctx', s...]
    all_to_all x1 -> x0, waiting for transfers between devices: 6.33 us -> none  [on_device(): lax.all_to_all(repacked, 'ctx', split_axis=0, concat_axis=0, tiled=True)]
    all_to_all x1 -> x0, starting transfers between devices: 4.88 us -> none  [on_device(): lax.all_to_all(repacked, 'ctx', split_axis=0, concat_axis=0, tiled=True)]
    pallas_call x4, Pallas kernels: 24.2 us -> 21 us  [the longest x1 8.32 us: on_device(): pl.pallas_call(local_kernel, grid=(GROUPS,), in_specs=[signal_spec] * 4 +...]
    pallas_call x1, Pallas kernels: 1.92 us -> 0.1 us  [on_device(): pl.pallas_call(functools.partial(scan_kernel, tokens, blocks, 1.0 / (toke...]
    unnamed x8 -> x16, local copies, waits for them, and re-layouts: 1.49 us -> 0.04 us
  transfers between devices with their start and end apart: 2 -> 1, of which waited for: 2 -> 1; matrix products, arithmetic and copies ran while one was open for 1% -> 1% of each run, Pallas kernels for 11% -> 12%
where the time goes in v2:
time: 69.2 us; the launch traced here: 68.8 us
  blocking collectives  29.1 us (42%)
  Pallas kernels  21.1 us (30%)
  starting transfers between devices  11.5 us (17%)
  waiting for transfers between devices  5.62 us (8%)
  other arithmetic  0.74 us (1%)
  between operations  0.72 us (1%)
    all_to_all x1, blocking collectives, on_device(): lax.all_to_all(repacked, 'ctx', split_axis=0, concat_axis=0, tiled=True)  19.5 us
    all_to_all x1, starting transfers between devices, on_device(): lax.all_to_all(packed.reshape(ctx_count, 3 * MODES_TILE, LANES), 'ctx', s...  11.5 us
    all_to_all x1, blocking collectives, on_device(): parts = lax.all_to_all(part, 'seq', split_axis=0, concat_axis=0, tiled=True)  9.68 us
    pallas_call x1, Pallas kernels, on_device(): pl.pallas_call(local_kernel, grid=(GROUPS,), in_specs=[signal_spec] * 4 +...  8.32 us
    pallas_call x1, Pallas kernels, on_device(): pl.pallas_call(states_kernel, in_specs=[there] * 5, out_specs=[there] * 3...  7.33 us
    all_to_all x1, waiting for transfers between devices, on_device(): lax.all_to_all(packed.reshape(ctx_count, 3 * MODES_TILE, LANES), 'ctx', s...  5.62 us
    pallas_call x1, Pallas kernels, on_device(): pl.pallas_call(output_kernel, in_specs=[here] * 5 + [there] * 2 + [here],...  5.3 us
  transfers between devices with their start and end apart: 1, of which 1 were waited for; matrix products, arithmetic and copies ran while one was open for 1% of the time, Pallas kernels for 12%

profile of v2, /device:TPU:32, one launch (start us, length us, event | category | flops | bytes accessed | tf_op | source)
XLA Modules:
  0.0 68.8 jit_solution(13999423050016985990)
XLA Ops:
  0.6 7.3 %states.1 = (f32[2,16,24,128]{3,2,1,0:T(8,128)}, f32[16,2,64,128]{3,2,1,0:T(8,128)}, f32[16,2,64,128]{3,2,1,0:T(8,128)}) custom-call(bf16[128,2048]{1,0:T(8,128)(2,1)} %bitcast.13, bf16[128,2048]{1,0:T(8,128)(2,1)} %bitcast.16, bf16[128,2048]{1,0:T(8,128)(2,1)} %bitcast.19, bf16[128,2048]{1,0:T(8,128)(2,1)} %bitcast.22, f32[16,2048]{1,0:T(8,128)} %bitcast.25), custom_call_target="tpu_custom_call" | custom-call | flops 25165824 | bytes 4194304 | tf_op jit(solution)/shard_map/states/pallas_call | solution.py:386
  8.0 0.0 copy-start.4
  8.0 0.0 copy-start.7
  8.0 11.5 %all-to-all-start = ((f32[32,24,128]{2,1,0:T(8,128)}), f32[32,24,128]{2,1,0:T(8,128)S(1)}, u32[]{:S(2)}, u32[]{:S(2)}) async-start(f32[32,24,128]{2,1,0:T(8,128)} %bitcast.31), calls=%async_computation | async-start | bytes 786432 | tf_op jit(solution)/shard_map/all_to_all | solution.py:416
  19.5 0.0 copy-done.4
  19.5 0.0 copy-done.7
  19.5 0.7 %negate_sqrt_fusion = (f32[16,2048]{1,0:T(8,128)S(1)}, f32[16,2048]{1,0:T(8,128)}) fusion(f32[16,2048]{1,0:T(8,128)S(1)} %bitcast.27, f32[16,2048]{1,0:T(8,128)S(1)} %bitcast.32), kind=kLoop, calls=%fused_computation | loop fusion | flops 98304 | bytes 524288 | tf_op jit(solution)/shard_map/sqrt | solution.py:413
  20.3 0.0 copy-start.5
  20.3 0.0 copy-start.6
  20.3 8.3 %local.1 = (f32[128,2048]{1,0:T(8,128)}, f32[128,2048]{1,0:T(8,128)}) custom-call(bf16[128,2048]{1,0:T(8,128)(2,1)} %bitcast.14, bf16[128,2048]{1,0:T(8,128)(2,1)} %bitcast.17, bf16[128,2048]{1,0:T(8,128)(2,1)} %bitcast.20, bf16[128,2048]{1,0:T(8,128)(2,1)} %bitcast.23, f32[16,2048]{1,0:T(8,128)} %bitcast.26, f32[16,2048]{1,0:T(8,128)} %get-tuple-element.42.weight_ref, ...), custom_call_target="tpu_custom_call" | custom-call | flops 33554432 | bytes 6291456 | tf_op jit(solution)/shard_map/local/pallas_call | solution.py:424
  28.6 5.6 %all-to-all-done.states_ref = f32[32,24,128]{2,1,0:T(8,128)S(1)} async-done(((f32[32,24,128]{2,1,0:T(8,128)}), f32[32,24,128]{2,1,0:T(8,128)S(1)}, u32[]{:S(2)}, u32[]{:S(2)}) %all-to-all-start) | async-done | bytes 393248 | tf_op jit(solution)/shard_map/all_to_all | solution.py:416
  34.2 0.0 copy-done.5
  34.2 0.0 copy-done.6
  34.2 0.0 copy-start.2
  34.2 0.0 copy-start.3
  34.2 0.1 scan.1
  34.3 9.7 %all_to_all.15.parts_ref = f32[8,8,128]{2,1,0:T(8,128)S(1)} all-to-all(f32[8,8,128]{2,1,0:T(8,128)S(1)} %get-tuple-element.35), channel_id=1, replica_groups=mesh['ctx'=32,'seq'=8] {'seq'}, dimensions={0} | all-to-all | bytes 65536 | tf_op jit(solution)/shard_map/all_to_all | solution.py:448
  44.0 0.0 copy-start
  44.1 19.5 %all_to_all.16 = f32[32,24,128]{2,1,0:T(8,128)S(1)} all-to-all(f32[32,24,128]{2,1,0:T(8,128)S(1)} %pack.1), channel_id=1, replica_groups=mesh['ctx'=32,'seq'=8] {'ctx'}, dimensions={0} | all-to-all | bytes 786432 | tf_op jit(solution)/shard_map/all_to_all | solution.py:457
  63.5 0.0 copy-done.2
  63.5 0.0 copy-done.3
  63.5 0.0 copy-done.1
  63.5 0.0 copy-done
  63.5 5.3 %outputs.1 = (bf16[128,2048]{1,0:T(8,128)(2,1)}, bf16[128,2048]{1,0:T(8,128)(2,1)}, bf16[128,2048]{1,0:T(8,128)(2,1)}, bf16[128,2048]{1,0:T(8,128)(2,1)}, f32[16,2048]{1,0:T(8,128)}) custom-call(bf16[128,2048]{1,0:T(8,128)(2,1)S(1)} %bitcast.15, bf16[128,2048]{1,0:T(8,128)(2,1)S(1)} %bitcast.18, bf16[128,2048]{1,0:T(8,128)(2,1)S(1)} %bitcast.21, ...), custom_call_target="tpu_custom_call" | custom-call | flops 16777216 | bytes 6291456 | tf_op jit(solution)/shard_map/outputs/pallas_call | solution.py:460
  (2 shorter events, 0.0 us)
Async XLA Ops:
  8.0 11.5 %copy-start.4 = (f32[2048,16]{0,1:T(8,128)S(1)}, f32[2048,16]{0,1:T(8,128)}, u32[]{:S(2)}) copy-start(f32[2048,16]{0,1:T(8,128)} %param.11) | copy-start | bytes 393220
  8.0 11.5 %copy-start.7 = (f32[2048,16]{0,1:T(8,128)S(1)}, f32[2048,16]{0,1:T(8,128)}, u32[]{:S(2)}) copy-start(f32[2048,16]{0,1:T(8,128)} %param.10) | copy-start | bytes 393220
  8.0 26.2 %all-to-all-start = ((f32[32,24,128]{2,1,0:T(8,128)}), f32[32,24,128]{2,1,0:T(8,128)S(1)}, u32[]{:S(2)}, u32[]{:S(2)}) async-start(f32[32,24,128]{2,1,0:T(8,128)} %bitcast.31), calls=%async_computation | async-start | bytes 786432 | tf_op jit(solution)/shard_map/all_to_all | solution.py:416
  20.3 13.9 %copy-start.5 = (f32[2048,16]{0,1:T(8,128)S(1)}, f32[2048,16]{0,1:T(8,128)}, u32[]{:S(2)}) copy-start(f32[2048,16]{0,1:T(8,128)} %param.11) | copy-start | bytes 393220
  20.3 13.9 %copy-start.6 = (f32[16,2048]{1,0:T(8,128)S(1)}, f32[16,2048]{1,0:T(8,128)}, u32[]{:S(2)}) copy-start(f32[16,2048]{1,0:T(8,128)} %get-tuple-element.42.weight_ref) | copy-start | bytes 393220
  34.2 29.3 %copy-start.2 = (bf16[1,128,2048]{2,1,0:T(8,128)(2,1)S(1)}, bf16[1,128,2048]{2,1,0:T(8,128)(2,1)}, u32[]{:S(2)}) copy-start(bf16[1,128,2048]{2,1,0:T(8,128)(2,1)} %param.8) | copy-start | bytes 1572868
  34.2 29.3 %copy-start.3 = (bf16[1,128,2048]{2,1,0:T(8,128)(2,1)S(1)}, bf16[1,128,2048]{2,1,0:T(8,128)(2,1)}, u32[]{:S(2)}) copy-start(bf16[1,128,2048]{2,1,0:T(8,128)(2,1)} %param.9) | copy-start | bytes 1572868
  44.0 19.5 %copy-start.1 = (bf16[1,128,2048]{2,1,0:T(8,128)(2,1)S(1)}, bf16[1,128,2048]{2,1,0:T(8,128)(2,1)}, u32[]{:S(2)}) copy-start(bf16[1,128,2048]{2,1,0:T(8,128)(2,1)} %param.7) | copy-start | bytes 1572868
  44.0 19.5 %copy-start = (bf16[1,128,2048]{2,1,0:T(8,128)(2,1)S(1)}, bf16[1,128,2048]{2,1,0:T(8,128)(2,1)}, u32[]{:S(2)}) copy-start(bf16[1,128,2048]{2,1,0:T(8,128)(2,1)} %param.6) | copy-start | bytes 1572868

commit v3 on v2

--- a/solution.py
+++ b/solution.py
@@ -12,7 +12,11 @@
 MODES_TILE = 8
 F32 = jnp.float32
 GROUPS = 4
+STATE_GROUPS = 4
+AHEAD = 2
 PITCH = 17
+EARLY_FLIPS = (1, 2)
+LATE_FLIPS = (6,)
 SMALL_VMEM = 12 * 1024 * 1024
 STATES_VMEM = 58 * 1024 * 1024
 OUTPUTS_VMEM = 51 * 1024 * 1024
@@ -20,6 +24,11 @@
 
 def sub_index():
     return lax.broadcasted_iota(jnp.int32, (SUBS, LANES), 0)
+
+
+def scale_of(rates):
+    bent = jnp.tanh(rates)
+    return jnp.sqrt(2.0 * bent / (1.0 + bent))
 
 
 def rows_of(tile):
@@ -77,11 +86,10 @@
         ]
 
     rates_fetch = pltpu.make_async_copy(rates_hbm, rates_ref, rates_arrived)
-    for group in range(groups):
+    rates_fetch.start()
+    for group in range(AHEAD):
         for fetch in fetches(group):
             fetch.start()
-        if group == 0:
-            rates_fetch.start()
     rates_fetch.wait()
 
     def block(index, carry):
@@ -141,8 +149,14 @@
     def column(group, carry):
         for fetch in fetches(group):
             fetch.wait()
+
+        @pl.when(group + AHEAD < groups)
+        def _():
+            for fetch in fetches(group + AHEAD):
+                fetch.start()
+
         per_group = span // LANES
-        carry = lax.fori_loop(group * per_group, (group + 1) * per_group, block, carry)
+        carry = lax.fori_loop(0, per_group, lambda j, c: block(group * per_group + j, c), carry, unroll=True)
         for store in stores(group):
             store.start()
         return carry
@@ -159,7 +173,7 @@
     value_ref,
     cot_ref,
     rates_ref,
-    weight_ref,
+    residues_ref,
     before_ref,
     after_ref,
     conv_ref,
@@ -179,8 +193,9 @@
         a_ref[...] = cot_ref[:, lanes].astype(F32) * query_ref[:, lanes].astype(F32)
         for half in range(modes // MODES_TILE):
             picked = slice(half * MODES_TILE, (half + 1) * MODES_TILE)
-            lam = rows_of(jnp.exp(-rates_ref[picked, lanes]))
-            weight = rows_of(weight_ref[picked, lanes])
+            rates = rates_ref[picked, lanes]
+            lam = rows_of(jnp.exp(-rates))
+            weight = rows_of(residues_ref[picked, lanes] * scale_of(rates))
             fwd = [before_ref[index, half, m * SUBS : (m + 1) * SUBS, :] for m in range(MODES_TILE)]
             for i in range(steps):
                 rows = pl.ds(i, SUBS, stride=steps)
@@ -208,7 +223,7 @@
     lax.fori_loop(0, width // LANES, block, 0)
 
 
-def scan_kernel(chunk_tokens, per_half, share, states_ref, rates_ref, weight_ref, scaling_ref, out_ref, part_ref):
+def scan_kernel(chunk_tokens, per_half, share, states_ref, rates_ref, residues_ref, out_ref, part_ref):
     chunks = states_ref.shape[0]
     rank = lax.axis_index("ctx")
     rows = pl.ds(pl.multiple_of((rank // per_half) * MODES_TILE, MODES_TILE), MODES_TILE)
@@ -216,7 +231,8 @@
     rates = rates_ref[rows, lanes]
     lam = jnp.exp(-rates)
     jump = jnp.exp(rates * -float(chunk_tokens))
-    entry = weight_ref[rows, lanes] * lam
+    scaling = scale_of(rates)
+    entry = residues_ref[rows, lanes] * scaling * lam
     zero = jnp.zeros((MODES_TILE, LANES), F32)
     fwd, cross, inner = zero, zero, zero
     for j in range(chunks):
@@ -228,18 +244,14 @@
     for j in reversed(range(chunks)):
         out_ref[j, MODES_TILE : 2 * MODES_TILE] = entry * bwd
         bwd = jump * bwd + states_ref[j, MODES_TILE : 2 * MODES_TILE]
-    part = (inner + lam * cross) * scaling_ref[rows, lanes] * share
-    for s in range(part_ref.shape[0]):
-        part_ref[s] = part
-
-
-def pack_kernel(states_ref, parts_ref, out_ref):
-    total = parts_ref[0]
-    for s in range(1, parts_ref.shape[0]):
-        total = total + parts_ref[s]
+    part = (inner + lam * cross) * scaling * share
+    part_ref[...] = part
+
+
+def pack_kernel(states_ref, part_ref, out_ref):
     for j in range(out_ref.shape[0]):
         out_ref[j, 0 : 2 * MODES_TILE] = states_ref[j]
-        out_ref[j, 2 * MODES_TILE : 3 * MODES_TILE] = total
+        out_ref[j, 2 * MODES_TILE : 3 * MODES_TILE] = part_ref[...]
 
 
 def output_kernel(
@@ -255,8 +267,6 @@
     grad_query_hbm,
     grad_key_hbm,
     grad_value_hbm,
-    grad_res_hbm,
-    grad_res_ref,
     conv_ref,
     grad_ref,
     out_ref,
@@ -279,7 +289,6 @@
         (grad_query_ref, grad_query_hbm),
         (grad_key_ref, grad_key_hbm),
         (grad_value_ref, grad_value_hbm),
-        (grad_res_ref, grad_res_hbm),
     )
 
     inputs = (
@@ -314,7 +323,6 @@
             jump = rows_of(jnp.exp(rates * -float(SUBS)))
             early = rows_of(entry_ref[half, index, 0:MODES_TILE, :])
             late = rows_of(entry_ref[half, index, MODES_TILE : 2 * MODES_TILE, :])
-            grad_res_ref[picked, lanes] = entry_ref[half, index, 2 * MODES_TILE : 3 * MODES_TILE, :]
             fwd = [early[m] * jnp.exp(-row[m] * sub) for m in range(MODES_TILE)]
             bwd = [late[m] * jnp.exp(-row[m] * (SUBS - 1 - sub)) for m in range(MODES_TILE)]
             for i in range(groups):
@@ -343,11 +351,11 @@
         return carry
 
     def column_step(column, carry):
-        first, last = column * (span // LANES), (column + 1) * (span // LANES)
-        carry = lax.fori_loop(first, last, entry, carry)
+        count = span // LANES
+        carry = lax.fori_loop(0, count, lambda j, c: entry(column * count + j, c), carry, unroll=True)
         for fetch in fetches(column):
             fetch.wait()
-        carry = lax.fori_loop(first, last, finish, carry)
+        carry = lax.fori_loop(0, count, lambda j, c: finish(column * count + j, c), carry, unroll=True)
         for store in stores(column):
             store.start()
         return carry
@@ -358,32 +366,23 @@
             store.wait()
 
 
-def on_device(query_input, key_input, value_input, cotangent, residues, decay_rates):
-    tokens, channels = query_input.shape[1:]
-    modes = residues.shape[1]
-    ctx_count = lax.axis_size("ctx")
-    seq_count = lax.axis_size("seq")
+def work(tokens, channels, ops, moved):
+    return pl.CostEstimate(
+        flops=ops * tokens * channels, bytes_accessed=moved * tokens * channels, transcendentals=0
+    )
+
+
+def states_call(signals, rates):
+    tokens, channels = signals[0].shape
+    modes = rates.shape[0]
     blocks = channels // LANES
     halves = modes // MODES_TILE
-    signals = [s[0] for s in (query_input, key_input, value_input, cotangent)]
-    rates = decay_rates.T
-
-    here = pl.BlockSpec(memory_space=pltpu.VMEM)
     there = pl.BlockSpec(memory_space=pltpu.HBM)
     border = jax.ShapeDtypeStruct((blocks, halves, MODES_TILE * SUBS, LANES), F32)
-    whole = jax.ShapeDtypeStruct((tokens, channels), F32)
     square = pltpu.VMEM((tokens, LANES), F32)
     tile = pltpu.VMEM((MODES_TILE * SUBS, LANES), F32)
-    signal_type = query_input.dtype
-    signal_buffer = pltpu.VMEM((tokens, channels), signal_type)
-    small = pltpu.CompilerParams(vmem_limit_bytes=SMALL_VMEM)
-
-    def cost(ops, moved):
-        return pl.CostEstimate(
-            flops=ops * tokens * channels, bytes_accessed=moved * tokens * channels, transcendentals=0
-        )
-
-    packed, before, after = pl.pallas_call(
+    signal_buffer = pltpu.VMEM((tokens, channels), signals[0].dtype)
+    return pl.pallas_call(
         states_kernel,
         in_specs=[there] * 5,
         out_specs=[there] * 3,
@@ -395,8 +394,8 @@
             pltpu.VMEM(border.shape, F32),
             pltpu.VMEM(border.shape, F32),
             pltpu.SemaphoreType.DMA(()),
-            pltpu.SemaphoreType.DMA((4, GROUPS)),
-            pltpu.SemaphoreType.DMA((3, GROUPS)),
+            pltpu.SemaphoreType.DMA((4, STATE_GROUPS)),
+            pltpu.SemaphoreType.DMA((3, STATE_GROUPS)),
             pltpu.VMEM((SUBS * PITCH, LANES), F32),
             pltpu.VMEM((SUBS * PITCH, LANES), F32),
             square,
@@ -405,13 +404,39 @@
             tile,
         ],
         compiler_params=pltpu.CompilerParams(vmem_limit_bytes=STATES_VMEM),
-        cost_estimate=cost(96, 16),
+        cost_estimate=work(tokens, channels, 96, 16),
         name="states",
     )(*signals, rates)
 
-    late_rates, late_residues, packed = lax.optimization_barrier((rates, residues.T, packed))
-    scaling = jnp.sqrt(-jnp.expm1(-2.0 * late_rates))
-    weight = late_residues * scaling
+
+def seq_sum(tile, flips):
+    for flip in flips:
+        pairs = [(i, i ^ flip) for i in range(lax.axis_size("seq"))]
+        tile = tile + lax.ppermute(tile, "seq", pairs)
+    return tile
+
+
+def on_device(query_input, key_input, value_input, cotangent, residues, decay_rates):
+    tokens, channels = query_input.shape[1:]
+    modes = residues.shape[1]
+    ctx_count = lax.axis_size("ctx")
+    seq_count = lax.axis_size("seq")
+    blocks = channels // LANES
+    halves = modes // MODES_TILE
+    signals = [s[0] for s in (query_input, key_input, value_input, cotangent)]
+    rates = decay_rates.T
+    modal = residues.T
+
+    here = pl.BlockSpec(memory_space=pltpu.VMEM)
+    there = pl.BlockSpec(memory_space=pltpu.HBM)
+    border = jax.ShapeDtypeStruct((blocks, halves, MODES_TILE * SUBS, LANES), F32)
+    whole = jax.ShapeDtypeStruct((tokens, channels), F32)
+    square = pltpu.VMEM((tokens, LANES), F32)
+    signal_type = query_input.dtype
+    signal_buffer = pltpu.VMEM((tokens, channels), signal_type)
+    small = pltpu.CompilerParams(vmem_limit_bytes=SMALL_VMEM)
+
+    packed, before, after = states_call(signals, rates)
 
     gathered = lax.all_to_all(
         packed.reshape(ctx_count, 3 * MODES_TILE, LANES), "ctx", split_axis=0, concat_axis=0, tiled=True
@@ -428,24 +453,24 @@
         out_specs=[signal_spec] * 2,
         out_shape=[whole] * 2,
         scratch_shapes=[square] * 4,
-        cost_estimate=cost(128, 24),
+        cost_estimate=work(tokens, channels, 128, 24),
         name="local",
-    )(*signals, rates, weight, before, after)
+    )(*signals, rates, modal, before, after)
     gathered, conv, grad = lax.optimization_barrier((gathered, conv, grad))
 
     borders, part = pl.pallas_call(
         functools.partial(scan_kernel, tokens, blocks, 1.0 / (tokens * ctx_count * seq_count)),
-        in_specs=[here] * 4,
+        in_specs=[here] * 3,
         out_specs=[here] * 2,
         out_shape=[
             jax.ShapeDtypeStruct((ctx_count, 2 * MODES_TILE, LANES), F32),
-            jax.ShapeDtypeStruct((seq_count, MODES_TILE, LANES), F32),
+            jax.ShapeDtypeStruct((MODES_TILE, LANES), F32),
         ],
         compiler_params=small,
         name="scan",
-    )(gathered, rates, weight, scaling)
-
-    parts = lax.all_to_all(part, "seq", split_axis=0, concat_axis=0, tiled=True)
+    )(gathered, rates, modal)
+
+    part = seq_sum(part, EARLY_FLIPS)
     repacked = pl.pallas_call(
         pack_kernel,
         in_specs=[here] * 2,
@@ -453,25 +478,26 @@
         out_shape=jax.ShapeDtypeStruct((ctx_count, 3 * MODES_TILE, LANES), F32),
         compiler_params=small,
         name="pack",
-    )(borders, parts)
+    )(borders, part)
     returned = lax.all_to_all(repacked, "ctx", split_axis=0, concat_axis=0, tiled=True)
 
     result = jax.ShapeDtypeStruct((tokens, channels), signal_type)
-    *results, grad_rows = pl.pallas_call(
+    results = pl.pallas_call(
         output_kernel,
         in_specs=[here] * 5 + [there] * 2 + [here],
-        out_specs=[there] * 5,
-        out_shape=[result] * 4 + [jax.ShapeDtypeStruct((modes, channels), F32)],
-        scratch_shapes=[pltpu.VMEM((modes, channels), F32)]
-        + [pltpu.VMEM((tokens, channels), F32)] * 2
+        out_specs=[there] * 4,
+        out_shape=[result] * 4,
+        scratch_shapes=[pltpu.VMEM((tokens, channels), F32)] * 2
         + [signal_buffer] * 4
-        + [pltpu.SemaphoreType.DMA((2, GROUPS)), pltpu.SemaphoreType.DMA((5, GROUPS))]
+        + [pltpu.SemaphoreType.DMA((2, GROUPS)), pltpu.SemaphoreType.DMA((4, GROUPS))]
         + [pltpu.VMEM((tokens, channels), F32)] * 2,
         compiler_params=pltpu.CompilerParams(vmem_limit_bytes=OUTPUTS_VMEM),
-        cost_estimate=cost(64, 24),
+        cost_estimate=work(tokens, channels, 64, 24),
         name="outputs",
     )(*signals, rates, conv, grad, returned.reshape(halves, blocks, 3 * MODES_TILE, LANES))
-    return (*[r[None] for r in results], grad_rows.T)
+    tiles = seq_sum(returned[:, 2 * MODES_TILE :], LATE_FLIPS)
+    grad_rows = tiles.reshape(halves, blocks, MODES_TILE, LANES).transpose(0, 2, 1, 3)
+    return (*[r[None] for r in results], grad_rows.reshape(modes, channels).T)
 
 
 def solution(mesh):

time: 69.2 us -> 66 us (0.954)
  blocking collectives: 29.1 us -> 18.7 us
  starting transfers between devices: 11.5 us -> 15.8 us
  waiting for transfers between devices: 5.62 us -> 9.51 us
  Pallas kernels: 21.1 us -> 20.2 us
    all_to_all x1 -> x0, blocking collectives: 9.68 us -> none  [on_device(): parts = lax.all_to_all(part, 'seq', split_axis=0, concat_axis=0, tiled=True)]
    ppermute x0 -> x3, starting transfers between devices: none -> 4.43 us  [seq_sum(): tile = tile + lax.ppermute(tile, 'seq', pairs)]
    ppermute x0 -> x3, waiting for transfers between devices: none -> 3.27 us  [seq_sum(): tile = tile + lax.ppermute(tile, 'seq', pairs)]
    pallas_call x1, Pallas kernels: 7.33 us -> 6.52 us  [states_call(): pl.pallas_call(states_kernel, in_specs=[there] * 5, out_specs=[there] * 3...]
    all_to_all x1, blocking collectives: 19.5 us -> 18.7 us  [on_device(): lax.all_to_all(repacked, 'ctx', split_axis=0, concat_axis=0, tiled=True)]
    sqrt x1 -> x0, other arithmetic: 0.74 us -> none  [on_device(): scaling = jnp.sqrt(-jnp.expm1(-2.0 * late_rates))]
  transfers between devices with their start and end apart: 1 -> 4, of which waited for: 1 -> 3; matrix products, arithmetic and copies ran while one was open for 1% -> 0% of each run, Pallas kernels for 12% -> 21%
where the time goes in v3:
time: 66 us; the launch traced here: 65.7 us
  Pallas kernels  20.2 us (31%)
  blocking collectives  18.7 us (28%)
  starting transfers between devices  15.8 us (24%)
  waiting for transfers between devices  9.51 us (14%)
  between operations  0.73 us (1%)
  other arithmetic  0.68 us (1%)
    all_to_all x1, blocking collectives, on_device(): lax.all_to_all(repacked, 'ctx', split_axis=0, concat_axis=0, tiled=True)  18.7 us
    all_to_all x1, starting transfers between devices, on_device(): lax.all_to_all(packed.reshape(ctx_count, 3 * MODES_TILE, LANES), 'ctx', s...  11.4 us
    pallas_call x1, Pallas kernels, on_device(): pl.pallas_call(local_kernel, grid=(GROUPS,), in_specs=[signal_spec] * 4 +...  8.44 us
    pallas_call x1, Pallas kernels, states_call(): pl.pallas_call(states_kernel, in_specs=[there] * 5, out_specs=[there] * 3...  6.52 us
    all_to_all x1, waiting for transfers between devices, on_device(): lax.all_to_all(packed.reshape(ctx_count, 3 * MODES_TILE, LANES), 'ctx', s...  6.24 us
    pallas_call x1, Pallas kernels, on_device(): pl.pallas_call(output_kernel, in_specs=[here] * 5 + [there] * 2 + [here],...  5.14 us
    ppermute x3, starting transfers between devices, seq_sum(): tile = tile + lax.ppermute(tile, 'seq', pairs)  4.43 us
    ppermute x3, waiting for transfers between devices, seq_sum(): tile = tile + lax.ppermute(tile, 'seq', pairs)  3.27 us
  transfers between devices with their start and end apart: 4, of which 3 were waited for; matrix products, arithmetic and copies ran while one was open for 0% of the time, Pallas kernels for 21%

profile of v3, /device:TPU:32, one launch (start us, length us, event | category | flops | bytes accessed | tf_op | source)
XLA Modules:
  0.0 65.7 jit_solution(7009056223789818192)
XLA Ops:
  0.6 6.5 %states.1 = (f32[2,16,24,128]{3,2,1,0:T(8,128)}, f32[16,2,64,128]{3,2,1,0:T(8,128)}, f32[16,2,64,128]{3,2,1,0:T(8,128)}) custom-call(bf16[128,2048]{1,0:T(8,128)(2,1)} %bitcast.19, bf16[128,2048]{1,0:T(8,128)(2,1)} %bitcast.22, bf16[128,2048]{1,0:T(8,128)(2,1)} %bitcast.25, bf16[128,2048]{1,0:T(8,128)(2,1)} %bitcast.28, f32[16,2048]{1,0:T(8,128)} %bitcast.32), custom_call_target="tpu_custom_call" | custom-call | flops 25165824 | bytes 4194304 | tf_op jit(solution)/shard_map/states/pallas_call | solution.py:385
  7.2 11.4 %all-to-all-start = ((f32[32,24,128]{2,1,0:T(8,128)}), f32[32,24,128]{2,1,0:T(8,128)S(1)}, u32[]{:S(2)}, u32[]{:S(2)}) async-start(f32[32,24,128]{2,1,0:T(8,128)} %bitcast.38), calls=%async_computation | async-start | bytes 786432 | tf_op jit(solution)/shard_map/all_to_all | solution.py:441
  18.5 0.0 copy-start.4
  18.5 0.0 copy-start.5
  18.6 8.4 %local.1 = (f32[128,2048]{1,0:T(8,128)}, f32[128,2048]{1,0:T(8,128)}) custom-call(bf16[128,2048]{1,0:T(8,128)(2,1)} %bitcast.20, bf16[128,2048]{1,0:T(8,128)(2,1)} %bitcast.23, bf16[128,2048]{1,0:T(8,128)(2,1)} %bitcast.26, bf16[128,2048]{1,0:T(8,128)(2,1)} %bitcast.29, f32[16,2048]{1,0:T(8,128)} %bitcast.33, f32[16,2048]{1,0:T(8,128)} %bitcast.36, ...), custom_call_target="tpu_custom_call" | custom-call | flops 33554432 | bytes 6291456 | tf_op jit(solution)/shard_map/local/pallas_call | solution.py:449
  27.0 6.2 %all-to-all-done.states_ref = f32[32,24,128]{2,1,0:T(8,128)S(1)} async-done(((f32[32,24,128]{2,1,0:T(8,128)}), f32[32,24,128]{2,1,0:T(8,128)S(1)}, u32[]{:S(2)}, u32[]{:S(2)}) %all-to-all-start) | async-done | bytes 393248 | tf_op jit(solution)/shard_map/all_to_all | solution.py:441
  33.2 0.0 copy-done.4
  33.2 0.0 copy-done.5
  33.3 0.1 scan.1
  33.4 0.1 collective-permute-start
  33.5 1.2 %collective-permute-done = f32[8,128]{1,0:T(8,128)S(1)} collective-permute-done((f32[8,128]{1,0:T(8,128)S(1)}, f32[8,128]{1,0:T(8,128)S(1)}, u32[]{:S(2)}, u32[]{:S(2)}) %collective-permute-start) | collective-permute-done | bytes 4128 | tf_op jit(solution)/shard_map/ppermute | solution.py:415
  34.6 1.5 %collective-permute-start.1 = (f32[8,128]{1,0:T(8,128)S(1)}, f32[8,128]{1,0:T(8,128)S(1)}, u32[]{:S(2)}, u32[]{:S(2)}) collective-permute-start(f32[8,128]{1,0:T(8,128)S(1)} %add.9), channel_id=1, source_target_pairs={{0,2},{1,3},{2,0},{3,1},{4,6},{5,7},{6,4},{7,5},{8,10},{9,11},{10,... | collective-permute-start | bytes 12296 | tf_op jit(solution)/shard_map/ppermute | solution.py:415
  36.1 2.1 %collective-permute-done.1 = f32[8,128]{1,0:T(8,128)S(1)} collective-permute-done((f32[8,128]{1,0:T(8,128)S(1)}, f32[8,128]{1,0:T(8,128)S(1)}, u32[]{:S(2)}, u32[]{:S(2)}) %collective-permute-start.1) | collective-permute-done | bytes 4128 | tf_op jit(solution)/shard_map/ppermute | solution.py:415
  38.3 0.0 copy-start
  38.3 0.0 copy-start.1
  38.3 18.7 %all_to_all.10 = f32[32,24,128]{2,1,0:T(8,128)S(1)} all-to-all(f32[32,24,128]{2,1,0:T(8,128)S(1)} %pack.1), channel_id=1, replica_groups=mesh['ctx'=32,'seq'=8] {'ctx'}, dimensions={0} | all-to-all | bytes 786432 | tf_op jit(solution)/shard_map/all_to_all | solution.py:482
  57.0 2.8 %collective-permute-start.2 = (f32[32,8,128]{2,1,0:T(8,128)S(1)}, f32[32,8,128]{2,1,0:T(8,128)S(1)}, u32[]{:S(2)}, u32[]{:S(2)}) collective-permute-start(f32[32,8,128]{2,1,0:T(8,128)S(1)} %slice.4), channel_id=1, source_target_pairs={{0,6},{1,7},{2,4},{3,5},{4,2},{5,3},{6,0},{7,1},{8,14},{9,15},{10,... | collective-permute-start | bytes 393224 | tf_op jit(solution)/shard_map/ppermute | solution.py:415
  59.8 0.0 copy-done.3
  59.8 0.0 copy-done.2
  59.8 0.0 copy-done
  59.9 0.0 copy-done.1
  59.9 5.1 %outputs.1 = (bf16[128,2048]{1,0:T(8,128)(2,1)}, bf16[128,2048]{1,0:T(8,128)(2,1)}, bf16[128,2048]{1,0:T(8,128)(2,1)}, bf16[128,2048]{1,0:T(8,128)(2,1)}) custom-call(bf16[128,2048]{1,0:T(8,128)(2,1)S(1)} %bitcast.21, bf16[128,2048]{1,0:T(8,128)(2,1)S(1)} %bitcast.24, bf16[128,2048]{1,0:T(8,128)(2,1)S(1)} %bitcast.27, bf16[128,2048]{1,0:T(8,128)(2,1)S(1)} %bitcast.30, ...), custom_call_target="tpu_custom_call" | custom-call | flops 16777216 | bytes 6291456 | tf_op jit(solution)/shard_map/outputs/pallas_call | solution.py:485
  65.0 0.0 collective-permute-done.2
  65.0 0.7 %slice_add_fusion = f32[32,8,128]{2,1,0:T(8,128)} fusion(f32[32,8,128]{2,1,0:T(8,128)S(1)} %collective-permute-done.2, f32[32,24,128]{2,1,0:T(8,128)S(1)} %all_to_all.10), kind=kLoop, calls=%fused_computation | loop fusion | flops 32768 | bytes 393216 | tf_op jit(solution)/shard_map/add | solution.py:415
  (6 shorter events, 0.0 us)
Async XLA Ops:
  7.2 26.1 %all-to-all-start = ((f32[32,24,128]{2,1,0:T(8,128)}), f32[32,24,128]{2,1,0:T(8,128)S(1)}, u32[]{:S(2)}, u32[]{:S(2)}) async-start(f32[32,24,128]{2,1,0:T(8,128)} %bitcast.38), calls=%async_computation | async-start | bytes 786432 | tf_op jit(solution)/shard_map/all_to_all | solution.py:441
  18.5 14.7 %copy-start.4 = (f32[2048,16]{0,1:T(8,128)S(1)}, f32[2048,16]{0,1:T(8,128)}, u32[]{:S(2)}) copy-start(f32[2048,16]{0,1:T(8,128)} %param.11) | copy-start | bytes 393220
  18.5 14.7 %copy-start.5 = (f32[2048,16]{0,1:T(8,128)S(1)}, f32[2048,16]{0,1:T(8,128)}, u32[]{:S(2)}) copy-start(f32[2048,16]{0,1:T(8,128)} %param.10) | copy-start | bytes 393220
  33.3 26.6 %copy-start.3 = (bf16[1,128,2048]{2,1,0:T(8,128)(2,1)S(1)}, bf16[1,128,2048]{2,1,0:T(8,128)(2,1)}, u32[]{:S(2)}) copy-start(bf16[1,128,2048]{2,1,0:T(8,128)(2,1)} %param.9) | copy-start | bytes 1572868
  33.4 1.3 %collective-permute-start = (f32[8,128]{1,0:T(8,128)S(1)}, f32[8,128]{1,0:T(8,128)S(1)}, u32[]{:S(2)}, u32[]{:S(2)}) collective-permute-start(f32[8,128]{1,0:T(8,128)S(1)} %get-tuple-element.28), channel_id=1, source_target_pairs={{0,1},{1,0},{2,3},{3,2},{4,5},{5,4},{6,7},{7,6},{8,9},{9,8},{10,11... | collective-permute-start | bytes 12296 | tf_op jit(solution)/shard_map/ppermute | solution.py:415
  34.6 3.6 %collective-permute-start.1 = (f32[8,128]{1,0:T(8,128)S(1)}, f32[8,128]{1,0:T(8,128)S(1)}, u32[]{:S(2)}, u32[]{:S(2)}) collective-permute-start(f32[8,128]{1,0:T(8,128)S(1)} %add.9), channel_id=1, source_target_pairs={{0,2},{1,3},{2,0},{3,1},{4,6},{5,7},{6,4},{7,5},{8,10},{9,11},{10,... | collective-permute-start | bytes 12296 | tf_op jit(solution)/shard_map/ppermute | solution.py:415
  38.2 21.6 %copy-start.2 = (bf16[1,128,2048]{2,1,0:T(8,128)(2,1)S(1)}, bf16[1,128,2048]{2,1,0:T(8,128)(2,1)}, u32[]{:S(2)}) copy-start(bf16[1,128,2048]{2,1,0:T(8,128)(2,1)} %param.8) | copy-start | bytes 1572868
  38.3 21.6 %copy-start = (bf16[1,128,2048]{2,1,0:T(8,128)(2,1)S(1)}, bf16[1,128,2048]{2,1,0:T(8,128)(2,1)}, u32[]{:S(2)}) copy-start(bf16[1,128,2048]{2,1,0:T(8,128)(2,1)} %param.6) | copy-start | bytes 1572868
  38.3 21.6 %copy-start.1 = (bf16[1,128,2048]{2,1,0:T(8,128)(2,1)S(1)}, bf16[1,128,2048]{2,1,0:T(8,128)(2,1)}, u32[]{:S(2)}) copy-start(bf16[1,128,2048]{2,1,0:T(8,128)(2,1)} %param.7) | copy-start | bytes 1572868
  57.0 8.0 %collective-permute-start.2 = (f32[32,8,128]{2,1,0:T(8,128)S(1)}, f32[32,8,128]{2,1,0:T(8,128)S(1)}, u32[]{:S(2)}, u32[]{:S(2)}) collective-permute-start(f32[32,8,128]{2,1,0:T(8,128)S(1)} %slice.4), channel_id=1, source_target_pairs={{0,6},{1,7},{2,4},{3,5},{4,2},{5,3},{6,0},{7,1},{8,14},{9,15},{10,... | collective-permute-start | bytes 393224 | tf_op jit(solution)/shard_map/ppermute | solution.py:415

commit v4 on v3

--- a/solution.py
+++ b/solution.py
@@ -12,11 +12,10 @@
 MODES_TILE = 8
 F32 = jnp.float32
 GROUPS = 4
-STATE_GROUPS = 4
+STATE_BLOCKS = (4, 4, 4, 4)
 AHEAD = 2
+UNROLL = 4
 PITCH = 17
-EARLY_FLIPS = (1, 2)
-LATE_FLIPS = (6,)
 SMALL_VMEM = 12 * 1024 * 1024
 STATES_VMEM = 58 * 1024 * 1024
 OUTPUTS_VMEM = 51 * 1024 * 1024
@@ -65,20 +64,18 @@
     tokens, width = query_ref.shape
     steps = tokens // SUBS
     modes = rates_ref.shape[0]
-    groups = arrived.shape[1]
-    span = width // groups
+    firsts = [sum(STATE_BLOCKS[:n]) for n in range(len(STATE_BLOCKS))]
     pairs = ((query_hbm, query_ref), (key_hbm, key_ref), (value_hbm, value_ref), (cot_hbm, cot_ref))
 
     def fetches(group):
-        lanes = pl.ds(pl.multiple_of(group * span, span), span)
+        lanes = pl.ds(firsts[group] * LANES, STATE_BLOCKS[group] * LANES)
         return [
             pltpu.make_async_copy(source.at[:, lanes], target.at[:, lanes], arrived.at[n, group])
             for n, (source, target) in enumerate(pairs)
         ]
 
     def stores(group):
-        count = span // LANES
-        part = pl.ds(group * count, count)
+        part = pl.ds(firsts[group], STATE_BLOCKS[group])
         return [
             pltpu.make_async_copy(packed_ref.at[:, part], packed_hbm.at[:, part], sent.at[0, group]),
             pltpu.make_async_copy(before_ref.at[part], before_hbm.at[part], sent.at[1, group]),
@@ -146,23 +143,20 @@
             packed_ref[half, index, 2 * MODES_TILE : 3 * MODES_TILE, :] = inner + lam_tile * cross
         return carry
 
-    def column(group, carry):
+    for group, (first, count) in enumerate(zip(firsts, STATE_BLOCKS, strict=True)):
         for fetch in fetches(group):
             fetch.wait()
-
-        @pl.when(group + AHEAD < groups)
-        def _():
+        if group + AHEAD < len(firsts):
             for fetch in fetches(group + AHEAD):
                 fetch.start()
-
-        per_group = span // LANES
-        carry = lax.fori_loop(0, per_group, lambda j, c: block(group * per_group + j, c), carry, unroll=True)
+        if UNROLL >= count:
+            for index in range(first, first + count):
+                block(index, 0)
+        else:
+            lax.fori_loop(first, first + count, block, 0, unroll=UNROLL)
         for store in stores(group):
             store.start()
-        return carry
-
-    lax.fori_loop(0, groups, column, 0)
-    for group in range(groups):
+    for group in range(len(firsts)):
         for store in stores(group):
             store.wait()
 
@@ -394,8 +388,8 @@
             pltpu.VMEM(border.shape, F32),
             pltpu.VMEM(border.shape, F32),
             pltpu.SemaphoreType.DMA(()),
-            pltpu.SemaphoreType.DMA((4, STATE_GROUPS)),
-            pltpu.SemaphoreType.DMA((3, STATE_GROUPS)),
+            pltpu.SemaphoreType.DMA((4, len(STATE_BLOCKS))),
+            pltpu.SemaphoreType.DMA((3, len(STATE_BLOCKS))),
             pltpu.VMEM((SUBS * PITCH, LANES), F32),
             pltpu.VMEM((SUBS * PITCH, LANES), F32),
             square,
@@ -409,11 +403,26 @@
     )(*signals, rates)
 
 
-def seq_sum(tile, flips):
-    for flip in flips:
-        pairs = [(i, i ^ flip) for i in range(lax.axis_size("seq"))]
-        tile = tile + lax.ppermute(tile, "seq", pairs)
-    return tile
+def outputs_call(signals, rates, conv, grad, entries):
+    tokens, channels = signals[0].shape
+    signal_type = signals[0].dtype
+    signal_buffer = pltpu.VMEM((tokens, channels), signal_type)
+    here = pl.BlockSpec(memory_space=pltpu.VMEM)
+    there = pl.BlockSpec(memory_space=pltpu.HBM)
+    result = jax.ShapeDtypeStruct((tokens, channels), signal_type)
+    return pl.pallas_call(
+        output_kernel,
+        in_specs=[here] * 5 + [there] * 2 + [here],
+        out_specs=[there] * 4,
+        out_shape=[result] * 4,
+        scratch_shapes=[pltpu.VMEM((tokens, channels), F32)] * 2
+        + [signal_buffer] * 4
+        + [pltpu.SemaphoreType.DMA((2, GROUPS)), pltpu.SemaphoreType.DMA((4, GROUPS))]
+        + [pltpu.VMEM((tokens, channels), F32)] * 2,
+        compiler_params=pltpu.CompilerParams(vmem_limit_bytes=OUTPUTS_VMEM),
+        cost_estimate=work(tokens, channels, 64, 24),
+        name="outputs",
+    )(*signals, rates, conv, grad, entries)
 
 
 def on_device(query_input, key_input, value_input, cotangent, residues, decay_rates):
@@ -428,12 +437,8 @@
     modal = residues.T
 
     here = pl.BlockSpec(memory_space=pltpu.VMEM)
-    there = pl.BlockSpec(memory_space=pltpu.HBM)
-    border = jax.ShapeDtypeStruct((blocks, halves, MODES_TILE * SUBS, LANES), F32)
     whole = jax.ShapeDtypeStruct((tokens, channels), F32)
     square = pltpu.VMEM((tokens, LANES), F32)
-    signal_type = query_input.dtype
-    signal_buffer = pltpu.VMEM((tokens, channels), signal_type)
     small = pltpu.CompilerParams(vmem_limit_bytes=SMALL_VMEM)
 
     packed, before, after = states_call(signals, rates)
@@ -470,7 +475,10 @@
         name="scan",
     )(gathered, rates, modal)
 
-    part = seq_sum(part, EARLY_FLIPS)
+    near, far, cross = (
+        lax.ppermute(part, "seq", [(i, i ^ flip) for i in range(seq_count)]) for flip in (1, 2, 3)
+    )
+    part = (part + near) + (far + cross)
     repacked = pl.pallas_call(
         pack_kernel,
         in_specs=[here] * 2,
@@ -481,21 +489,10 @@
     )(borders, part)
     returned = lax.all_to_all(repacked, "ctx", split_axis=0, concat_axis=0, tiled=True)
 
-    result = jax.ShapeDtypeStruct((tokens, channels), signal_type)
-    results = pl.pallas_call(
-        output_kernel,
-        in_specs=[here] * 5 + [there] * 2 + [here],
-        out_specs=[there] * 4,
-        out_shape=[result] * 4,
-        scratch_shapes=[pltpu.VMEM((tokens, channels), F32)] * 2
-        + [signal_buffer] * 4
-        + [pltpu.SemaphoreType.DMA((2, GROUPS)), pltpu.SemaphoreType.DMA((4, GROUPS))]
-        + [pltpu.VMEM((tokens, channels), F32)] * 2,
-        compiler_params=pltpu.CompilerParams(vmem_limit_bytes=OUTPUTS_VMEM),
-        cost_estimate=work(tokens, channels, 64, 24),
-        name="outputs",
-    )(*signals, rates, conv, grad, returned.reshape(halves, blocks, 3 * MODES_TILE, LANES))
-    tiles = seq_sum(returned[:, 2 * MODES_TILE :], LATE_FLIPS)
+    entries = returned.reshape(halves, blocks, 3 * MODES_TILE, LANES)
+    results = outputs_call(signals, rates, conv, grad, entries)
+    tiles = returned[:, 2 * MODES_TILE :]
+    tiles = tiles + lax.ppermute(tiles, "seq", [(i, i ^ 6) for i in range(seq_count)])
     grad_rows = tiles.reshape(halves, blocks, MODES_TILE, LANES).transpose(0, 2, 1, 3)
     return (*[r[None] for r in results], grad_rows.reshape(modes, channels).T)
 

time: 66 us -> 65.6 us (level)
  waiting for transfers between devices: 9.51 us -> 8.09 us
  blocking collectives: 18.7 us -> 19.9 us
    ppermute x3 -> x4, waiting for transfers between devices: 3.27 us -> 1.85 us  [the longest x3 1.85 us: on_device(): lax.ppermute(part, 'seq', [(i, i ^ flip) for i in range(seq_count)])]
    all_to_all x1, blocking collectives: 18.7 us -> 19.9 us  [on_device(): lax.all_to_all(repacked, 'ctx', split_axis=0, concat_axis=0, tiled=True)]
    ppermute x3 -> x4, starting transfers between devices: 4.43 us -> 4.23 us  [the longest x1 2.29 us: on_device(): lax.ppermute(tiles, 'seq', [(i, i ^ 6) for i in range(seq_count)])]
  transfers between devices with their start and end apart: 4 -> 5, of which waited for: 3 -> 3; matrix products, arithmetic and copies ran while one was open for 0% -> 0% of each run, Pallas kernels for 21% -> 21%
where the time goes in v4:
time: 65.6 us; the launch traced here: 65.3 us
  Pallas kernels  20.2 us (31%)
  blocking collectives  19.9 us (30%)
  starting transfers between devices  15.6 us (24%)
  waiting for transfers between devices  8.09 us (12%)
  between operations  0.74 us (1%)
  other arithmetic  0.68 us (1%)
    all_to_all x1, blocking collectives, on_device(): lax.all_to_all(repacked, 'ctx', split_axis=0, concat_axis=0, tiled=True)  19.9 us
    all_to_all x1, starting transfers between devices, on_device(): lax.all_to_all(packed.reshape(ctx_count, 3 * MODES_TILE, LANES), 'ctx', s...  11.4 us
    pallas_call x1, Pallas kernels, on_device(): pl.pallas_call(local_kernel, grid=(GROUPS,), in_specs=[signal_spec] * 4 +...  8.44 us
    pallas_call x1, Pallas kernels, states_call(): pl.pallas_call(states_kernel, in_specs=[there] * 5, out_specs=[there] * 3...  6.5 us
    all_to_all x1, waiting for transfers between devices, on_device(): lax.all_to_all(packed.reshape(ctx_count, 3 * MODES_TILE, LANES), 'ctx', s...  6.24 us
    pallas_call x1, Pallas kernels, outputs_call(): pl.pallas_call(output_kernel, in_specs=[here] * 5 + [there] * 2 + [here],...  5.14 us
    ppermute x1, starting transfers between devices, on_device(): lax.ppermute(tiles, 'seq', [(i, i ^ 6) for i in range(seq_count)])  2.29 us
    ppermute x3, starting transfers between devices, on_device(): lax.ppermute(part, 'seq', [(i, i ^ flip) for i in range(seq_count)])  1.94 us
  transfers between devices with their start and end apart: 5, of which 3 were waited for; matrix products, arithmetic and copies ran while one was open for 0% of the time, Pallas kernels for 21%

profile of v4, /device:TPU:32, one launch (start us, length us, event | category | flops | bytes accessed | tf_op | source)
XLA Modules:
  0.0 65.3 jit_solution(2019535921345009986)
XLA Ops:
  0.6 6.5 %states.1 = (f32[2,16,24,128]{3,2,1,0:T(8,128)}, f32[16,2,64,128]{3,2,1,0:T(8,128)}, f32[16,2,64,128]{3,2,1,0:T(8,128)}) custom-call(bf16[128,2048]{1,0:T(8,128)(2,1)} %bitcast.19, bf16[128,2048]{1,0:T(8,128)(2,1)} %bitcast.22, bf16[128,2048]{1,0:T(8,128)(2,1)} %bitcast.25, bf16[128,2048]{1,0:T(8,128)(2,1)} %bitcast.28, f32[16,2048]{1,0:T(8,128)} %bitcast.32), custom_call_target="tpu_custom_call" | custom-call | flops 25165824 | bytes 4194304 | tf_op jit(solution)/shard_map/states/pallas_call | solution.py:379
  7.1 11.4 %all-to-all-start = ((f32[32,24,128]{2,1,0:T(8,128)}), f32[32,24,128]{2,1,0:T(8,128)S(1)}, u32[]{:S(2)}, u32[]{:S(2)}) async-start(f32[32,24,128]{2,1,0:T(8,128)} %bitcast.38), calls=%async_computation | async-start | bytes 786432 | tf_op jit(solution)/shard_map/all_to_all | solution.py:446
  18.5 0.0 copy-start.4
  18.5 0.0 copy-start.5
  18.5 8.4 %local.1 = (f32[128,2048]{1,0:T(8,128)}, f32[128,2048]{1,0:T(8,128)}) custom-call(bf16[128,2048]{1,0:T(8,128)(2,1)} %bitcast.20, bf16[128,2048]{1,0:T(8,128)(2,1)} %bitcast.23, bf16[128,2048]{1,0:T(8,128)(2,1)} %bitcast.26, bf16[128,2048]{1,0:T(8,128)(2,1)} %bitcast.29, f32[16,2048]{1,0:T(8,128)} %bitcast.33, f32[16,2048]{1,0:T(8,128)} %bitcast.36, ...), custom_call_target="tpu_custom_call" | custom-call | flops 33554432 | bytes 6291456 | tf_op jit(solution)/shard_map/local/pallas_call | solution.py:454
  27.0 6.2 %all-to-all-done.states_ref = f32[32,24,128]{2,1,0:T(8,128)S(1)} async-done(((f32[32,24,128]{2,1,0:T(8,128)}), f32[32,24,128]{2,1,0:T(8,128)S(1)}, u32[]{:S(2)}, u32[]{:S(2)}) %all-to-all-start) | async-done | bytes 393248 | tf_op jit(solution)/shard_map/all_to_all | solution.py:446
  33.2 0.0 copy-done.4
  33.2 0.1 scan.1
  33.3 0.1 collective-permute-start.2
  33.4 1.6 %collective-permute-start.1 = (f32[8,128]{1,0:T(8,128)S(1)}, f32[8,128]{1,0:T(8,128)S(1)}, u32[]{:S(2)}, u32[]{:S(2)}) collective-permute-start(f32[8,128]{1,0:T(8,128)S(1)} %get-tuple-element.28), channel_id=1, source_target_pairs={{0,2},{1,3},{2,0},{3,1},{4,6},{5,7},{6,4},{7,5},{8,10},{9,11},{10,... | collective-permute-start | bytes 12296 | tf_op jit(solution)/shard_map/ppermute | solution.py:479
  35.0 0.3 collective-permute-start
  35.3 1.2 %collective-permute-done.2 = f32[8,128]{1,0:T(8,128)S(1)} collective-permute-done((f32[8,128]{1,0:T(8,128)S(1)}, f32[8,128]{1,0:T(8,128)S(1)}, u32[]{:S(2)}, u32[]{:S(2)}) %collective-permute-start.2) | collective-permute-done | bytes 4128 | tf_op jit(solution)/shard_map/ppermute | solution.py:479
  36.5 0.7 %collective-permute-done.1 = f32[8,128]{1,0:T(8,128)S(1)} collective-permute-done((f32[8,128]{1,0:T(8,128)S(1)}, f32[8,128]{1,0:T(8,128)S(1)}, u32[]{:S(2)}, u32[]{:S(2)}) %collective-permute-start.1) | collective-permute-done | bytes 4128 | tf_op jit(solution)/shard_map/ppermute | solution.py:479
  37.1 0.0 collective-permute-done
  37.1 0.0 copy-start.2
  37.2 0.0 copy-start
  37.2 0.0 copy-start.1
  37.2 19.9 %all_to_all.10 = f32[32,24,128]{2,1,0:T(8,128)S(1)} all-to-all(f32[32,24,128]{2,1,0:T(8,128)S(1)} %pack.1), channel_id=1, replica_groups=mesh['ctx'=32,'seq'=8] {'ctx'}, dimensions={0} | all-to-all | bytes 786432 | tf_op jit(solution)/shard_map/all_to_all | solution.py:490
  57.2 2.3 %collective-permute-start.3 = (f32[32,8,128]{2,1,0:T(8,128)S(1)}, f32[32,8,128]{2,1,0:T(8,128)S(1)}, u32[]{:S(2)}, u32[]{:S(2)}) collective-permute-start(f32[32,8,128]{2,1,0:T(8,128)S(1)} %slice.4), channel_id=1, source_target_pairs={{0,6},{1,7},{2,4},{3,5},{4,2},{5,3},{6,0},{7,1},{8,14},{9,15},{10,... | collective-permute-start | bytes 393224 | tf_op jit(solution)/shard_map/ppermute | solution.py:495
  59.5 0.0 copy-done.2
  59.5 0.0 copy-done.1
  59.5 5.1 %outputs.1 = (bf16[128,2048]{1,0:T(8,128)(2,1)}, bf16[128,2048]{1,0:T(8,128)(2,1)}, bf16[128,2048]{1,0:T(8,128)(2,1)}, bf16[128,2048]{1,0:T(8,128)(2,1)}) custom-call(bf16[128,2048]{1,0:T(8,128)(2,1)S(1)} %bitcast.21, bf16[128,2048]{1,0:T(8,128)(2,1)S(1)} %bitcast.24, bf16[128,2048]{1,0:T(8,128)(2,1)S(1)} %bitcast.27, bf16[128,2048]{1,0:T(8,128)(2,1)S(1)} %bitcast.30, ...), custom_call_target="tpu_custom_call" | custom-call | flops 16777216 | bytes 6291456 | tf_op jit(solution)/shard_map/outputs/pallas_call | solution.py:413
  64.6 0.0 collective-permute-done.3
  64.6 0.7 %slice_add_fusion = f32[32,8,128]{2,1,0:T(8,128)} fusion(f32[32,8,128]{2,1,0:T(8,128)S(1)} %collective-permute-done.3, f32[32,24,128]{2,1,0:T(8,128)S(1)} %all_to_all.10), kind=kLoop, calls=%fused_computation.1 | loop fusion | flops 32768 | bytes 393216 | tf_op jit(solution)/shard_map/add | solution.py:495
  (7 shorter events, 0.1 us)
Async XLA Ops:
  7.1 26.1 %all-to-all-start = ((f32[32,24,128]{2,1,0:T(8,128)}), f32[32,24,128]{2,1,0:T(8,128)S(1)}, u32[]{:S(2)}, u32[]{:S(2)}) async-start(f32[32,24,128]{2,1,0:T(8,128)} %bitcast.38), calls=%async_computation | async-start | bytes 786432 | tf_op jit(solution)/shard_map/all_to_all | solution.py:446
  18.5 14.7 %copy-start.4 = (f32[2048,16]{0,1:T(8,128)S(1)}, f32[2048,16]{0,1:T(8,128)}, u32[]{:S(2)}) copy-start(f32[2048,16]{0,1:T(8,128)} %param.11) | copy-start | bytes 393220
  18.5 14.7 %copy-start.5 = (f32[2048,16]{0,1:T(8,128)S(1)}, f32[2048,16]{0,1:T(8,128)}, u32[]{:S(2)}) copy-start(f32[2048,16]{0,1:T(8,128)} %param.10) | copy-start | bytes 393220
  33.2 26.2 %copy-start.3 = (bf16[1,128,2048]{2,1,0:T(8,128)(2,1)S(1)}, bf16[1,128,2048]{2,1,0:T(8,128)(2,1)}, u32[]{:S(2)}) copy-start(bf16[1,128,2048]{2,1,0:T(8,128)(2,1)} %param.9) | copy-start | bytes 1572868
  33.3 3.1 %collective-permute-start.2 = (f32[8,128]{1,0:T(8,128)S(1)}, f32[8,128]{1,0:T(8,128)S(1)}, u32[]{:S(2)}, u32[]{:S(2)}) collective-permute-start(f32[8,128]{1,0:T(8,128)S(1)} %get-tuple-element.28), channel_id=1, source_target_pairs={{0,3},{1,2},{2,1},{3,0},{4,7},{5,6},{6,5},{7,4},{8,11},{9,10},{10,... | collective-permute-start | bytes 12296 | tf_op jit(solution)/shard_map/ppermute | solution.py:479
  33.4 3.7 %collective-permute-start.1 = (f32[8,128]{1,0:T(8,128)S(1)}, f32[8,128]{1,0:T(8,128)S(1)}, u32[]{:S(2)}, u32[]{:S(2)}) collective-permute-start(f32[8,128]{1,0:T(8,128)S(1)} %get-tuple-element.28), channel_id=1, source_target_pairs={{0,2},{1,3},{2,0},{3,1},{4,6},{5,7},{6,4},{7,5},{8,10},{9,11},{10,... | collective-permute-start | bytes 12296 | tf_op jit(solution)/shard_map/ppermute | solution.py:479
  35.0 2.1 %collective-permute-start = (f32[8,128]{1,0:T(8,128)S(1)}, f32[8,128]{1,0:T(8,128)S(1)}, u32[]{:S(2)}, u32[]{:S(2)}) collective-permute-start(f32[8,128]{1,0:T(8,128)S(1)} %get-tuple-element.28), channel_id=1, source_target_pairs={{0,1},{1,0},{2,3},{3,2},{4,5},{5,4},{6,7},{7,6},{8,9},{9,8},{10,11... | collective-permute-start | bytes 12296 | tf_op jit(solution)/shard_map/ppermute | solution.py:479
  37.1 22.3 %copy-start.2 = (bf16[1,128,2048]{2,1,0:T(8,128)(2,1)S(1)}, bf16[1,128,2048]{2,1,0:T(8,128)(2,1)}, u32[]{:S(2)}) copy-start(bf16[1,128,2048]{2,1,0:T(8,128)(2,1)} %param.8) | copy-start | bytes 1572868
  37.2 22.3 %copy-start = (bf16[1,128,2048]{2,1,0:T(8,128)(2,1)S(1)}, bf16[1,128,2048]{2,1,0:T(8,128)(2,1)}, u32[]{:S(2)}) copy-start(bf16[1,128,2048]{2,1,0:T(8,128)(2,1)} %param.6) | copy-start | bytes 1572868
  37.2 22.3 %copy-start.1 = (bf16[1,128,2048]{2,1,0:T(8,128)(2,1)S(1)}, bf16[1,128,2048]{2,1,0:T(8,128)(2,1)}, u32[]{:S(2)}) copy-start(bf16[1,128,2048]{2,1,0:T(8,128)(2,1)} %param.7) | copy-start | bytes 1572868
  57.2 7.5 %collective-permute-start.3 = (f32[32,8,128]{2,1,0:T(8,128)S(1)}, f32[32,8,128]{2,1,0:T(8,128)S(1)}, u32[]{:S(2)}, u32[]{:S(2)}) collective-permute-start(f32[32,8,128]{2,1,0:T(8,128)S(1)} %slice.4), channel_id=1, source_target_pairs={{0,6},{1,7},{2,4},{3,5},{4,2},{5,3},{6,0},{7,1},{8,14},{9,15},{10,... | collective-permute-start | bytes 393224 | tf_op jit(solution)/shard_map/ppermute | solution.py:495

commit v5 on v4

--- a/solution.py
+++ b/solution.py
@@ -12,6 +12,7 @@
 MODES_TILE = 8
 F32 = jnp.float32
 GROUPS = 4
+OUTPUT_COLUMNS = 2
 STATE_BLOCKS = (4, 4, 4, 4)
 AHEAD = 2
 UNROLL = 4
@@ -291,7 +292,7 @@
     )
 
     def fetches(column):
-        lanes = pl.ds(pl.multiple_of(column * span, span), span)
+        lanes = pl.ds(column * span, span)
         return [
             pltpu.make_async_copy(source.at[:, lanes], target.at[:, lanes], arrived.at[n, column])
             for n, (source, target) in enumerate(inputs)
@@ -302,7 +303,7 @@
             fetch.start()
 
     def stores(column):
-        lanes = pl.ds(pl.multiple_of(column * span, span), span)
+        lanes = pl.ds(column * span, span)
         return [
             pltpu.make_async_copy(source.at[:, lanes], target.at[:, lanes], sent.at[n, column])
             for n, (source, target) in enumerate(pairs)
@@ -344,17 +345,15 @@
         grad_value_ref[:, lanes] = (key_ref[:, lanes].astype(F32) * g).astype(out_ref.dtype)
         return carry
 
-    def column_step(column, carry):
-        count = span // LANES
-        carry = lax.fori_loop(0, count, lambda j, c: entry(column * count + j, c), carry, unroll=True)
+    count = span // LANES
+    for column in range(columns):
+        first = column * count
+        lax.fori_loop(first, first + count, entry, 0, unroll=True)
         for fetch in fetches(column):
             fetch.wait()
-        carry = lax.fori_loop(0, count, lambda j, c: finish(column * count + j, c), carry, unroll=True)
+        lax.fori_loop(first, first + count, finish, 0, unroll=True)
         for store in stores(column):
             store.start()
-        return carry
-
-    lax.fori_loop(0, columns, column_step, 0)
     for column in range(columns):
         for store in stores(column):
             store.wait()
@@ -417,7 +416,7 @@
         out_shape=[result] * 4,
         scratch_shapes=[pltpu.VMEM((tokens, channels), F32)] * 2
         + [signal_buffer] * 4
-        + [pltpu.SemaphoreType.DMA((2, GROUPS)), pltpu.SemaphoreType.DMA((4, GROUPS))]
+        + [pltpu.SemaphoreType.DMA((2, OUTPUT_COLUMNS)), pltpu.SemaphoreType.DMA((4, OUTPUT_COLUMNS))]
         + [pltpu.VMEM((tokens, channels), F32)] * 2,
         compiler_params=pltpu.CompilerParams(vmem_limit_bytes=OUTPUTS_VMEM),
         cost_estimate=work(tokens, channels, 64, 24),

time: 65.6 us -> 64.7 us (0.986)
  Pallas kernels: 20.2 us -> 19 us
    pallas_call x1, Pallas kernels: 5.14 us -> 3.9 us  [outputs_call(): pl.pallas_call(output_kernel, in_specs=[here] * 5 + [there] * 2 + [here],...]
  transfers between devices with their start and end apart: 5 -> 5, of which waited for: 3 -> 4; matrix products, arithmetic and copies ran while one was open for 0% -> 0% of each run, Pallas kernels for 21% -> 19%
where the time goes in v5:
time: 64.7 us; the launch traced here: 64.1 us
  blocking collectives  19.9 us (31%)
  Pallas kernels  19 us (29%)
  starting transfers between devices  15.6 us (24%)
  waiting for transfers between devices  8.15 us (13%)
  between operations  0.73 us (1%)
  other arithmetic  0.68 us (1%)
    all_to_all x1, blocking collectives, on_device(): lax.all_to_all(repacked, 'ctx', split_axis=0, concat_axis=0, tiled=True)  19.9 us
    all_to_all x1, starting transfers between devices, on_device(): lax.all_to_all(packed.reshape(ctx_count, 3 * MODES_TILE, LANES), 'ctx', s...  11.4 us
    pallas_call x1, Pallas kernels, on_device(): pl.pallas_call(local_kernel, grid=(GROUPS,), in_specs=[signal_spec] * 4 +...  8.44 us
    pallas_call x1, Pallas kernels, states_call(): pl.pallas_call(states_kernel, in_specs=[there] * 5, out_specs=[there] * 3...  6.5 us
    all_to_all x1, waiting for transfers between devices, on_device(): lax.all_to_all(packed.reshape(ctx_count, 3 * MODES_TILE, LANES), 'ctx', s...  6.24 us
    pallas_call x1, Pallas kernels, outputs_call(): pl.pallas_call(output_kernel, in_specs=[here] * 5 + [there] * 2 + [here],...  3.9 us
    ppermute x1, starting transfers between devices, on_device(): lax.ppermute(tiles, 'seq', [(i, i ^ 6) for i in range(seq_count)])  2.29 us
    ppermute x3, starting transfers between devices, on_device(): lax.ppermute(part, 'seq', [(i, i ^ flip) for i in range(seq_count)])  1.94 us
  transfers between devices with their start and end apart: 5, of which 4 were waited for; matrix products, arithmetic and copies ran while one was open for 0% of the time, Pallas kernels for 19%

profile of v5, /device:TPU:32, one launch (start us, length us, event | category | flops | bytes accessed | tf_op | source)
XLA Modules:
  0.0 64.1 jit_solution(12961972887730389589)
XLA Ops:
  0.6 6.5 %states.1 = (f32[2,16,24,128]{3,2,1,0:T(8,128)}, f32[16,2,64,128]{3,2,1,0:T(8,128)}, f32[16,2,64,128]{3,2,1,0:T(8,128)}) custom-call(bf16[128,2048]{1,0:T(8,128)(2,1)} %bitcast.19, bf16[128,2048]{1,0:T(8,128)(2,1)} %bitcast.22, bf16[128,2048]{1,0:T(8,128)(2,1)} %bitcast.25, bf16[128,2048]{1,0:T(8,128)(2,1)} %bitcast.28, f32[16,2048]{1,0:T(8,128)} %bitcast.32), custom_call_target="tpu_custom_call" | custom-call | flops 25165824 | bytes 4194304 | tf_op jit(solution)/shard_map/states/pallas_call | solution.py:378
  7.1 11.4 %all-to-all-start = ((f32[32,24,128]{2,1,0:T(8,128)}), f32[32,24,128]{2,1,0:T(8,128)S(1)}, u32[]{:S(2)}, u32[]{:S(2)}) async-start(f32[32,24,128]{2,1,0:T(8,128)} %bitcast.38), calls=%async_computation | async-start | bytes 786432 | tf_op jit(solution)/shard_map/all_to_all | solution.py:445
  18.5 0.0 copy-start.4
  18.5 0.0 copy-start.5
  18.5 8.4 %local.1 = (f32[128,2048]{1,0:T(8,128)}, f32[128,2048]{1,0:T(8,128)}) custom-call(bf16[128,2048]{1,0:T(8,128)(2,1)} %bitcast.20, bf16[128,2048]{1,0:T(8,128)(2,1)} %bitcast.23, bf16[128,2048]{1,0:T(8,128)(2,1)} %bitcast.26, bf16[128,2048]{1,0:T(8,128)(2,1)} %bitcast.29, f32[16,2048]{1,0:T(8,128)} %bitcast.33, f32[16,2048]{1,0:T(8,128)} %bitcast.36, ...), custom_call_target="tpu_custom_call" | custom-call | flops 33554432 | bytes 6291456 | tf_op jit(solution)/shard_map/local/pallas_call | solution.py:453
  27.0 6.2 %all-to-all-done.states_ref = f32[32,24,128]{2,1,0:T(8,128)S(1)} async-done(((f32[32,24,128]{2,1,0:T(8,128)}), f32[32,24,128]{2,1,0:T(8,128)S(1)}, u32[]{:S(2)}, u32[]{:S(2)}) %all-to-all-start) | async-done | bytes 393248 | tf_op jit(solution)/shard_map/all_to_all | solution.py:445
  33.2 0.0 copy-done.4
  33.2 0.1 scan.1
  33.3 0.1 collective-permute-start.2
  33.4 1.6 %collective-permute-start.1 = (f32[8,128]{1,0:T(8,128)S(1)}, f32[8,128]{1,0:T(8,128)S(1)}, u32[]{:S(2)}, u32[]{:S(2)}) collective-permute-start(f32[8,128]{1,0:T(8,128)S(1)} %get-tuple-element.28), channel_id=1, source_target_pairs={{0,2},{1,3},{2,0},{3,1},{4,6},{5,7},{6,4},{7,5},{8,10},{9,11},{10,... | collective-permute-start | bytes 12296 | tf_op jit(solution)/shard_map/ppermute | solution.py:478
  35.0 0.3 collective-permute-start
  35.3 1.2 %collective-permute-done.2 = f32[8,128]{1,0:T(8,128)S(1)} collective-permute-done((f32[8,128]{1,0:T(8,128)S(1)}, f32[8,128]{1,0:T(8,128)S(1)}, u32[]{:S(2)}, u32[]{:S(2)}) %collective-permute-start.2) | collective-permute-done | bytes 4128 | tf_op jit(solution)/shard_map/ppermute | solution.py:478
  36.5 0.7 %collective-permute-done.1 = f32[8,128]{1,0:T(8,128)S(1)} collective-permute-done((f32[8,128]{1,0:T(8,128)S(1)}, f32[8,128]{1,0:T(8,128)S(1)}, u32[]{:S(2)}, u32[]{:S(2)}) %collective-permute-start.1) | collective-permute-done | bytes 4128 | tf_op jit(solution)/shard_map/ppermute | solution.py:478
  37.1 0.0 collective-permute-done
  37.1 0.0 copy-start.2
  37.2 0.0 copy-start
  37.2 0.0 copy-start.1
  37.2 19.9 %all_to_all.10 = f32[32,24,128]{2,1,0:T(8,128)S(1)} all-to-all(f32[32,24,128]{2,1,0:T(8,128)S(1)} %pack.1), channel_id=1, replica_groups=mesh['ctx'=32,'seq'=8] {'ctx'}, dimensions={0} | all-to-all | bytes 786432 | tf_op jit(solution)/shard_map/all_to_all | solution.py:489
  57.2 2.3 %collective-permute-start.3 = (f32[32,8,128]{2,1,0:T(8,128)S(1)}, f32[32,8,128]{2,1,0:T(8,128)S(1)}, u32[]{:S(2)}, u32[]{:S(2)}) collective-permute-start(f32[32,8,128]{2,1,0:T(8,128)S(1)} %slice.4), channel_id=1, source_target_pairs={{0,6},{1,7},{2,4},{3,5},{4,2},{5,3},{6,0},{7,1},{8,14},{9,15},{10,... | collective-permute-start | bytes 393224 | tf_op jit(solution)/shard_map/ppermute | solution.py:494
  59.5 0.0 copy-done.2
  59.5 0.0 copy-done.1
  59.5 3.9 %outputs.1 = (bf16[128,2048]{1,0:T(8,128)(2,1)}, bf16[128,2048]{1,0:T(8,128)(2,1)}, bf16[128,2048]{1,0:T(8,128)(2,1)}, bf16[128,2048]{1,0:T(8,128)(2,1)}) custom-call(bf16[128,2048]{1,0:T(8,128)(2,1)S(1)} %bitcast.21, bf16[128,2048]{1,0:T(8,128)(2,1)S(1)} %bitcast.24, bf16[128,2048]{1,0:T(8,128)(2,1)S(1)} %bitcast.27, bf16[128,2048]{1,0:T(8,128)(2,1)S(1)} %bitcast.30, ...), custom_call_target="tpu_custom_call" | custom-call | flops 16777216 | bytes 6291456 | tf_op jit(solution)/shard_map/outputs/pallas_call | solution.py:412
  63.4 0.1 collective-permute-done.3
  63.4 0.7 %slice_add_fusion = f32[32,8,128]{2,1,0:T(8,128)} fusion(f32[32,8,128]{2,1,0:T(8,128)S(1)} %collective-permute-done.3, f32[32,24,128]{2,1,0:T(8,128)S(1)} %all_to_all.10), kind=kLoop, calls=%fused_computation.1 | loop fusion | flops 32768 | bytes 393216 | tf_op jit(solution)/shard_map/add | solution.py:494
  (7 shorter events, 0.1 us)
Async XLA Ops:
  7.1 26.1 %all-to-all-start = ((f32[32,24,128]{2,1,0:T(8,128)}), f32[32,24,128]{2,1,0:T(8,128)S(1)}, u32[]{:S(2)}, u32[]{:S(2)}) async-start(f32[32,24,128]{2,1,0:T(8,128)} %bitcast.38), calls=%async_computation | async-start | bytes 786432 | tf_op jit(solution)/shard_map/all_to_all | solution.py:445
  18.5 14.7 %copy-start.4 = (f32[2048,16]{0,1:T(8,128)S(1)}, f32[2048,16]{0,1:T(8,128)}, u32[]{:S(2)}) copy-start(f32[2048,16]{0,1:T(8,128)} %param.11) | copy-start | bytes 393220
  18.5 14.7 %copy-start.5 = (f32[2048,16]{0,1:T(8,128)S(1)}, f32[2048,16]{0,1:T(8,128)}, u32[]{:S(2)}) copy-start(f32[2048,16]{0,1:T(8,128)} %param.10) | copy-start | bytes 393220
  33.2 26.2 %copy-start.3 = (bf16[1,128,2048]{2,1,0:T(8,128)(2,1)S(1)}, bf16[1,128,2048]{2,1,0:T(8,128)(2,1)}, u32[]{:S(2)}) copy-start(bf16[1,128,2048]{2,1,0:T(8,128)(2,1)} %param.9) | copy-start | bytes 1572868
  33.3 3.1 %collective-permute-start.2 = (f32[8,128]{1,0:T(8,128)S(1)}, f32[8,128]{1,0:T(8,128)S(1)}, u32[]{:S(2)}, u32[]{:S(2)}) collective-permute-start(f32[8,128]{1,0:T(8,128)S(1)} %get-tuple-element.28), channel_id=1, source_target_pairs={{0,3},{1,2},{2,1},{3,0},{4,7},{5,6},{6,5},{7,4},{8,11},{9,10},{10,... | collective-permute-start | bytes 12296 | tf_op jit(solution)/shard_map/ppermute | solution.py:478
  33.4 3.7 %collective-permute-start.1 = (f32[8,128]{1,0:T(8,128)S(1)}, f32[8,128]{1,0:T(8,128)S(1)}, u32[]{:S(2)}, u32[]{:S(2)}) collective-permute-start(f32[8,128]{1,0:T(8,128)S(1)} %get-tuple-element.28), channel_id=1, source_target_pairs={{0,2},{1,3},{2,0},{3,1},{4,6},{5,7},{6,4},{7,5},{8,10},{9,11},{10,... | collective-permute-start | bytes 12296 | tf_op jit(solution)/shard_map/ppermute | solution.py:478
  35.0 2.1 %collective-permute-start = (f32[8,128]{1,0:T(8,128)S(1)}, f32[8,128]{1,0:T(8,128)S(1)}, u32[]{:S(2)}, u32[]{:S(2)}) collective-permute-start(f32[8,128]{1,0:T(8,128)S(1)} %get-tuple-element.28), channel_id=1, source_target_pairs={{0,1},{1,0},{2,3},{3,2},{4,5},{5,4},{6,7},{7,6},{8,9},{9,8},{10,11... | collective-permute-start | bytes 12296 | tf_op jit(solution)/shard_map/ppermute | solution.py:478
  37.1 22.3 %copy-start.2 = (bf16[1,128,2048]{2,1,0:T(8,128)(2,1)S(1)}, bf16[1,128,2048]{2,1,0:T(8,128)(2,1)}, u32[]{:S(2)}) copy-start(bf16[1,128,2048]{2,1,0:T(8,128)(2,1)} %param.8) | copy-start | bytes 1572868
  37.2 22.3 %copy-start = (bf16[1,128,2048]{2,1,0:T(8,128)(2,1)S(1)}, bf16[1,128,2048]{2,1,0:T(8,128)(2,1)}, u32[]{:S(2)}) copy-start(bf16[1,128,2048]{2,1,0:T(8,128)(2,1)} %param.6) | copy-start | bytes 1572868
  37.2 22.3 %copy-start.1 = (bf16[1,128,2048]{2,1,0:T(8,128)(2,1)S(1)}, bf16[1,128,2048]{2,1,0:T(8,128)(2,1)}, u32[]{:S(2)}) copy-start(bf16[1,128,2048]{2,1,0:T(8,128)(2,1)} %param.7) | copy-start | bytes 1572868
  57.2 6.3 %collective-permute-start.3 = (f32[32,8,128]{2,1,0:T(8,128)S(1)}, f32[32,8,128]{2,1,0:T(8,128)S(1)}, u32[]{:S(2)}, u32[]{:S(2)}) collective-permute-start(f32[32,8,128]{2,1,0:T(8,128)S(1)} %slice.4), channel_id=1, source_target_pairs={{0,6},{1,7},{2,4},{3,5},{4,2},{5,3},{6,0},{7,1},{8,14},{9,15},{10,... | collective-permute-start | bytes 393224 | tf_op jit(solution)/shard_map/ppermute | solution.py:494

commit v6 on v5

--- a/solution.py
+++ b/solution.py
@@ -9,6 +9,7 @@
 
 LANES = 128
 SUBS = 8
+SPARE = 8
 MODES_TILE = 8
 F32 = jnp.float32
 GROUPS = 4
@@ -77,10 +78,11 @@
 
     def stores(group):
         part = pl.ds(firsts[group], STATE_BLOCKS[group])
+        rows = pl.ds(0, MODES_TILE * SUBS)
         return [
             pltpu.make_async_copy(packed_ref.at[:, part], packed_hbm.at[:, part], sent.at[0, group]),
-            pltpu.make_async_copy(before_ref.at[part], before_hbm.at[part], sent.at[1, group]),
-            pltpu.make_async_copy(after_ref.at[part], after_hbm.at[part], sent.at[2, group]),
+            pltpu.make_async_copy(before_ref.at[part, :, rows], before_hbm.at[part], sent.at[1, group]),
+            pltpu.make_async_copy(after_ref.at[part, :, rows], after_hbm.at[part], sent.at[2, group]),
         ]
 
     rates_fetch = pltpu.make_async_copy(rates_hbm, rates_ref, rates_arrived)
@@ -184,8 +186,8 @@
 
     def block(index, carry):
         lanes = pl.ds(pl.multiple_of(index * LANES, LANES), LANES)
-        u_ref[...] = key_ref[:, lanes].astype(F32) * value_ref[:, lanes].astype(F32)
-        a_ref[...] = cot_ref[:, lanes].astype(F32) * query_ref[:, lanes].astype(F32)
+        u_ref[0:tokens] = key_ref[:, lanes].astype(F32) * value_ref[:, lanes].astype(F32)
+        a_ref[0:tokens] = cot_ref[:, lanes].astype(F32) * query_ref[:, lanes].astype(F32)
         for half in range(modes // MODES_TILE):
             picked = slice(half * MODES_TILE, (half + 1) * MODES_TILE)
             rates = rates_ref[picked, lanes]
@@ -211,8 +213,8 @@
                     term = weight[m] * bwd[m]
                     total = term if total is None else total + term
                 g_ref[rows, :] = total
-        conv_ref[:, lanes] = y_ref[...]
-        grad_ref[:, lanes] = g_ref[...]
+        conv_ref[:, lanes] = y_ref[0:tokens]
+        grad_ref[:, lanes] = g_ref[0:tokens]
         return carry
 
     lax.fori_loop(0, width // LANES, block, 0)
@@ -372,8 +374,9 @@
     halves = modes // MODES_TILE
     there = pl.BlockSpec(memory_space=pltpu.HBM)
     border = jax.ShapeDtypeStruct((blocks, halves, MODES_TILE * SUBS, LANES), F32)
-    square = pltpu.VMEM((tokens, LANES), F32)
-    tile = pltpu.VMEM((MODES_TILE * SUBS, LANES), F32)
+    square = pltpu.VMEM((tokens + SPARE, LANES), F32)
+    tile = pltpu.VMEM((MODES_TILE * SUBS + SPARE, LANES), F32)
+    staged = pltpu.VMEM((blocks, halves, MODES_TILE * SUBS + SPARE, LANES), F32)
     signal_buffer = pltpu.VMEM((tokens, channels), signals[0].dtype)
     return pl.pallas_call(
         states_kernel,
@@ -384,13 +387,13 @@
         + [
             pltpu.VMEM((modes, channels), F32),
             pltpu.VMEM((halves, blocks, 3 * MODES_TILE, LANES), F32),
-            pltpu.VMEM(border.shape, F32),
-            pltpu.VMEM(border.shape, F32),
+            staged,
+            staged,
             pltpu.SemaphoreType.DMA(()),
             pltpu.SemaphoreType.DMA((4, len(STATE_BLOCKS))),
             pltpu.SemaphoreType.DMA((3, len(STATE_BLOCKS))),
-            pltpu.VMEM((SUBS * PITCH, LANES), F32),
-            pltpu.VMEM((SUBS * PITCH, LANES), F32),
+            pltpu.VMEM((SUBS * PITCH + 2 * SPARE, LANES), F32),
+            pltpu.VMEM((SUBS * PITCH + 2 * SPARE, LANES), F32),
             square,
             pltpu.VMEM((tokens // SUBS, LANES), F32),
             tile,
@@ -437,7 +440,7 @@
 
     here = pl.BlockSpec(memory_space=pltpu.VMEM)
     whole = jax.ShapeDtypeStruct((tokens, channels), F32)
-    square = pltpu.VMEM((tokens, LANES), F32)
+    square = pltpu.VMEM((tokens + 2 * SPARE, LANES), F32)
     small = pltpu.CompilerParams(vmem_limit_bytes=SMALL_VMEM)
 
     packed, before, after = states_call(signals, rates)

time: 64.7 us -> 64.7 us (level)
  no operation moved by 1% of the time
where the time goes in v6:
time: 64.7 us; the launch traced here: 64.1 us
  blocking collectives  19.9 us (31%)
  Pallas kernels  19 us (29%)
  starting transfers between devices  15.6 us (24%)
  waiting for transfers between devices  8.15 us (13%)
  between operations  0.73 us (1%)
  other arithmetic  0.68 us (1%)
    all_to_all x1, blocking collectives, on_device(): lax.all_to_all(repacked, 'ctx', split_axis=0, concat_axis=0, tiled=True)  19.9 us
    all_to_all x1, starting transfers between devices, on_device(): lax.all_to_all(packed.reshape(ctx_count, 3 * MODES_TILE, LANES), 'ctx', s...  11.4 us
    pallas_call x1, Pallas kernels, on_device(): pl.pallas_call(local_kernel, grid=(GROUPS,), in_specs=[signal_spec] * 4 +...  8.44 us
    pallas_call x1, Pallas kernels, states_call(): pl.pallas_call(states_kernel, in_specs=[there] * 5, out_specs=[there] * 3...  6.51 us
    all_to_all x1, waiting for transfers between devices, on_device(): lax.all_to_all(packed.reshape(ctx_count, 3 * MODES_TILE, LANES), 'ctx', s...  6.24 us
    pallas_call x1, Pallas kernels, outputs_call(): pl.pallas_call(output_kernel, in_specs=[here] * 5 + [there] * 2 + [here],...  3.9 us
    ppermute x1, starting transfers between devices, on_device(): lax.ppermute(tiles, 'seq', [(i, i ^ 6) for i in range(seq_count)])  2.29 us
    ppermute x3, starting transfers between devices, on_device(): lax.ppermute(part, 'seq', [(i, i ^ flip) for i in range(seq_count)])  1.94 us
  transfers between devices with their start and end apart: 5, of which 4 were waited for; matrix products, arithmetic and copies ran while one was open for 0% of the time, Pallas kernels for 19%

profile of v6, /device:TPU:32, one launch (start us, length us, event | category | flops | bytes accessed | tf_op | source)
XLA Modules:
  0.0 64.1 jit_solution(12821216353991256807)
XLA Ops:
  0.6 6.5 %states.1 = (f32[2,16,24,128]{3,2,1,0:T(8,128)}, f32[16,2,64,128]{3,2,1,0:T(8,128)}, f32[16,2,64,128]{3,2,1,0:T(8,128)}) custom-call(bf16[128,2048]{1,0:T(8,128)(2,1)} %bitcast.19, bf16[128,2048]{1,0:T(8,128)(2,1)} %bitcast.22, bf16[128,2048]{1,0:T(8,128)(2,1)} %bitcast.25, bf16[128,2048]{1,0:T(8,128)(2,1)} %bitcast.28, f32[16,2048]{1,0:T(8,128)} %bitcast.32), custom_call_target="tpu_custom_call" | custom-call | flops 25165824 | bytes 4194304 | tf_op jit(solution)/shard_map/states/pallas_call | solution.py:381
  7.2 11.4 %all-to-all-start = ((f32[32,24,128]{2,1,0:T(8,128)}), f32[32,24,128]{2,1,0:T(8,128)S(1)}, u32[]{:S(2)}, u32[]{:S(2)}) async-start(f32[32,24,128]{2,1,0:T(8,128)} %bitcast.38), calls=%async_computation | async-start | bytes 786432 | tf_op jit(solution)/shard_map/all_to_all | solution.py:448
  18.5 0.0 copy-start.4
  18.5 0.0 copy-start.5
  18.6 8.4 %local.1 = (f32[128,2048]{1,0:T(8,128)}, f32[128,2048]{1,0:T(8,128)}) custom-call(bf16[128,2048]{1,0:T(8,128)(2,1)} %bitcast.20, bf16[128,2048]{1,0:T(8,128)(2,1)} %bitcast.23, bf16[128,2048]{1,0:T(8,128)(2,1)} %bitcast.26, bf16[128,2048]{1,0:T(8,128)(2,1)} %bitcast.29, f32[16,2048]{1,0:T(8,128)} %bitcast.33, f32[16,2048]{1,0:T(8,128)} %bitcast.36, ...), custom_call_target="tpu_custom_call" | custom-call | flops 33554432 | bytes 6291456 | tf_op jit(solution)/shard_map/local/pallas_call | solution.py:456
  27.0 6.2 %all-to-all-done.states_ref = f32[32,24,128]{2,1,0:T(8,128)S(1)} async-done(((f32[32,24,128]{2,1,0:T(8,128)}), f32[32,24,128]{2,1,0:T(8,128)S(1)}, u32[]{:S(2)}, u32[]{:S(2)}) %all-to-all-start) | async-done | bytes 393248 | tf_op jit(solution)/shard_map/all_to_all | solution.py:448
  33.2 0.0 copy-done.4
  33.2 0.0 copy-done.5
  33.2 0.1 scan.1
  33.3 0.1 collective-permute-start.2
  33.4 1.6 %collective-permute-start.1 = (f32[8,128]{1,0:T(8,128)S(1)}, f32[8,128]{1,0:T(8,128)S(1)}, u32[]{:S(2)}, u32[]{:S(2)}) collective-permute-start(f32[8,128]{1,0:T(8,128)S(1)} %get-tuple-element.28), channel_id=1, source_target_pairs={{0,2},{1,3},{2,0},{3,1},{4,6},{5,7},{6,4},{7,5},{8,10},{9,11},{10,... | collective-permute-start | bytes 12296 | tf_op jit(solution)/shard_map/ppermute | solution.py:481
  35.0 0.3 collective-permute-start
  35.3 1.2 %collective-permute-done.2 = f32[8,128]{1,0:T(8,128)S(1)} collective-permute-done((f32[8,128]{1,0:T(8,128)S(1)}, f32[8,128]{1,0:T(8,128)S(1)}, u32[]{:S(2)}, u32[]{:S(2)}) %collective-permute-start.2) | collective-permute-done | bytes 4128 | tf_op jit(solution)/shard_map/ppermute | solution.py:481
  36.5 0.7 %collective-permute-done.1 = f32[8,128]{1,0:T(8,128)S(1)} collective-permute-done((f32[8,128]{1,0:T(8,128)S(1)}, f32[8,128]{1,0:T(8,128)S(1)}, u32[]{:S(2)}, u32[]{:S(2)}) %collective-permute-start.1) | collective-permute-done | bytes 4128 | tf_op jit(solution)/shard_map/ppermute | solution.py:481
  37.1 0.0 collective-permute-done
  37.2 0.0 copy-start.2
  37.2 0.0 copy-start
  37.2 0.0 copy-start.1
  37.2 19.9 %all_to_all.10 = f32[32,24,128]{2,1,0:T(8,128)S(1)} all-to-all(f32[32,24,128]{2,1,0:T(8,128)S(1)} %pack.1), channel_id=1, replica_groups=mesh['ctx'=32,'seq'=8] {'ctx'}, dimensions={0} | all-to-all | bytes 786432 | tf_op jit(solution)/shard_map/all_to_all | solution.py:492
  57.2 2.3 %collective-permute-start.3 = (f32[32,8,128]{2,1,0:T(8,128)S(1)}, f32[32,8,128]{2,1,0:T(8,128)S(1)}, u32[]{:S(2)}, u32[]{:S(2)}) collective-permute-start(f32[32,8,128]{2,1,0:T(8,128)S(1)} %slice.4), channel_id=1, source_target_pairs={{0,6},{1,7},{2,4},{3,5},{4,2},{5,3},{6,0},{7,1},{8,14},{9,15},{10,... | collective-permute-start | bytes 393224 | tf_op jit(solution)/shard_map/ppermute | solution.py:497
  59.5 0.0 copy-done
  59.5 3.9 %outputs.1 = (bf16[128,2048]{1,0:T(8,128)(2,1)}, bf16[128,2048]{1,0:T(8,128)(2,1)}, bf16[128,2048]{1,0:T(8,128)(2,1)}, bf16[128,2048]{1,0:T(8,128)(2,1)}) custom-call(bf16[128,2048]{1,0:T(8,128)(2,1)S(1)} %bitcast.21, bf16[128,2048]{1,0:T(8,128)(2,1)S(1)} %bitcast.24, bf16[128,2048]{1,0:T(8,128)(2,1)S(1)} %bitcast.27, bf16[128,2048]{1,0:T(8,128)(2,1)S(1)} %bitcast.30, ...), custom_call_target="tpu_custom_call" | custom-call | flops 16777216 | bytes 6291456 | tf_op jit(solution)/shard_map/outputs/pallas_call | solution.py:415
  63.4 0.1 collective-permute-done.3
  63.4 0.7 %slice_add_fusion = f32[32,8,128]{2,1,0:T(8,128)} fusion(f32[32,8,128]{2,1,0:T(8,128)S(1)} %collective-permute-done.3, f32[32,24,128]{2,1,0:T(8,128)S(1)} %all_to_all.10), kind=kLoop, calls=%fused_computation.1 | loop fusion | flops 32768 | bytes 393216 | tf_op jit(solution)/shard_map/add | solution.py:497
  (7 shorter events, 0.1 us)
Async XLA Ops:
  7.2 26.1 %all-to-all-start = ((f32[32,24,128]{2,1,0:T(8,128)}), f32[32,24,128]{2,1,0:T(8,128)S(1)}, u32[]{:S(2)}, u32[]{:S(2)}) async-start(f32[32,24,128]{2,1,0:T(8,128)} %bitcast.38), calls=%async_computation | async-start | bytes 786432 | tf_op jit(solution)/shard_map/all_to_all | solution.py:448
  18.5 14.7 %copy-start.4 = (f32[2048,16]{0,1:T(8,128)S(1)}, f32[2048,16]{0,1:T(8,128)}, u32[]{:S(2)}) copy-start(f32[2048,16]{0,1:T(8,128)} %param.11) | copy-start | bytes 393220
  18.5 14.7 %copy-start.5 = (f32[2048,16]{0,1:T(8,128)S(1)}, f32[2048,16]{0,1:T(8,128)}, u32[]{:S(2)}) copy-start(f32[2048,16]{0,1:T(8,128)} %param.10) | copy-start | bytes 393220
  33.2 26.2 %copy-start.3 = (bf16[1,128,2048]{2,1,0:T(8,128)(2,1)S(1)}, bf16[1,128,2048]{2,1,0:T(8,128)(2,1)}, u32[]{:S(2)}) copy-start(bf16[1,128,2048]{2,1,0:T(8,128)(2,1)} %param.9) | copy-start | bytes 1572868
  33.3 3.1 %collective-permute-start.2 = (f32[8,128]{1,0:T(8,128)S(1)}, f32[8,128]{1,0:T(8,128)S(1)}, u32[]{:S(2)}, u32[]{:S(2)}) collective-permute-start(f32[8,128]{1,0:T(8,128)S(1)} %get-tuple-element.28), channel_id=1, source_target_pairs={{0,3},{1,2},{2,1},{3,0},{4,7},{5,6},{6,5},{7,4},{8,11},{9,10},{10,... | collective-permute-start | bytes 12296 | tf_op jit(solution)/shard_map/ppermute | solution.py:481
  33.4 3.7 %collective-permute-start.1 = (f32[8,128]{1,0:T(8,128)S(1)}, f32[8,128]{1,0:T(8,128)S(1)}, u32[]{:S(2)}, u32[]{:S(2)}) collective-permute-start(f32[8,128]{1,0:T(8,128)S(1)} %get-tuple-element.28), channel_id=1, source_target_pairs={{0,2},{1,3},{2,0},{3,1},{4,6},{5,7},{6,4},{7,5},{8,10},{9,11},{10,... | collective-permute-start | bytes 12296 | tf_op jit(solution)/shard_map/ppermute | solution.py:481
  35.0 2.1 %collective-permute-start = (f32[8,128]{1,0:T(8,128)S(1)}, f32[8,128]{1,0:T(8,128)S(1)}, u32[]{:S(2)}, u32[]{:S(2)}) collective-permute-start(f32[8,128]{1,0:T(8,128)S(1)} %get-tuple-element.28), channel_id=1, source_target_pairs={{0,1},{1,0},{2,3},{3,2},{4,5},{5,4},{6,7},{7,6},{8,9},{9,8},{10,11... | collective-permute-start | bytes 12296 | tf_op jit(solution)/shard_map/ppermute | solution.py:481
  37.2 22.3 %copy-start.2 = (bf16[1,128,2048]{2,1,0:T(8,128)(2,1)S(1)}, bf16[1,128,2048]{2,1,0:T(8,128)(2,1)}, u32[]{:S(2)}) copy-start(bf16[1,128,2048]{2,1,0:T(8,128)(2,1)} %param.8) | copy-start | bytes 1572868
  37.2 22.3 %copy-start = (bf16[1,128,2048]{2,1,0:T(8,128)(2,1)S(1)}, bf16[1,128,2048]{2,1,0:T(8,128)(2,1)}, u32[]{:S(2)}) copy-start(bf16[1,128,2048]{2,1,0:T(8,128)(2,1)} %param.6) | copy-start | bytes 1572868
  37.2 22.3 %copy-start.1 = (bf16[1,128,2048]{2,1,0:T(8,128)(2,1)S(1)}, bf16[1,128,2048]{2,1,0:T(8,128)(2,1)}, u32[]{:S(2)}) copy-start(bf16[1,128,2048]{2,1,0:T(8,128)(2,1)} %param.7) | copy-start | bytes 1572868
  57.2 6.3 %collective-permute-start.3 = (f32[32,8,128]{2,1,0:T(8,128)S(1)}, f32[32,8,128]{2,1,0:T(8,128)S(1)}, u32[]{:S(2)}, u32[]{:S(2)}) collective-permute-start(f32[32,8,128]{2,1,0:T(8,128)S(1)} %slice.4), channel_id=1, source_target_pairs={{0,6},{1,7},{2,4},{3,5},{4,2},{5,3},{6,0},{7,1},{8,14},{9,15},{10,... | collective-permute-start | bytes 393224 | tf_op jit(solution)/shard_map/ppermute | solution.py:497

commit v7 on v6

--- a/solution.py
+++ b/solution.py
@@ -62,6 +62,7 @@
     lag_sum_ref,
     fwd_ref,
     bwd_ref,
+    mid_ref,
 ):
     tokens, width = query_ref.shape
     steps = tokens // SUBS
@@ -101,17 +102,19 @@
             a_ref[s * PITCH : s * PITCH + steps, :] = adjoint[s * steps : (s + 1) * steps]
         u = [u_ref[pl.ds(i, SUBS, stride=PITCH), :] for i in range(steps)]
         a = [a_ref[pl.ds(i, SUBS, stride=PITCH), :] for i in range(steps)]
-        for lag in range(steps):
-            total = a[lag] * u[0]
-            for i in range(1, steps - lag):
-                total = total + a[lag + i] * u[i]
+        middle = steps // 2
+        for lag in range(middle):
+            total = None
+            for start in (0, middle):
+                for i in range(start, start + middle - lag):
+                    term = a[lag + i] * u[i]
+                    total = term if total is None else total + term
             lag_ref[lag * SUBS : (lag + 1) * SUBS, :] = total
-        for group in range(steps // SUBS):
-            total = None
-            for s in range(SUBS):
-                term = lag_ref[pl.ds(group * SUBS * SUBS + s, SUBS, stride=SUBS), :]
-                total = term if total is None else total + term
-            lag_sum_ref[group * SUBS : (group + 1) * SUBS, :] = total
+        total = None
+        for s in range(SUBS):
+            term = lag_ref[pl.ds(s, middle, stride=SUBS), :]
+            total = term if total is None else total + term
+        lag_sum_ref[...] = total
         for half in range(modes // MODES_TILE):
             rates = rates_ref[half * MODES_TILE : (half + 1) * MODES_TILE, lanes]
             lam_tile = jnp.exp(-rates)
@@ -124,6 +127,9 @@
                 for m in range(MODES_TILE):
                     fwd[m] = lam[m] * fwd[m] + front
                     bwd[m] = lam[m] * bwd[m] + back
+                if i == middle - 1:
+                    for m in range(MODES_TILE):
+                        mid_ref[m * SUBS : (m + 1) * SUBS, :] = fwd[m] * bwd[m]
             for m in range(MODES_TILE):
                 fwd_ref[m * SUBS : (m + 1) * SUBS, :] = fwd[m]
                 bwd_ref[m * SUBS : (m + 1) * SUBS, :] = bwd[m]
@@ -133,13 +139,13 @@
             for s in range(SUBS):
                 rows = pl.ds(s, MODES_TILE, stride=SUBS)
                 before_ref[index, half, rows, :] = before
-                cross = cross + bwd_ref[rows, :] * before
+                cross = cross + bwd_ref[rows, :] * before + mid_ref[rows, :]
                 before = jump * before + fwd_ref[rows, :]
             for s in reversed(range(SUBS)):
                 rows = pl.ds(s, MODES_TILE, stride=SUBS)
                 after_ref[index, half, rows, :] = after
                 after = jump * after + bwd_ref[rows, :]
-            for lag in reversed(range(steps)):
+            for lag in reversed(range(middle)):
                 inner = inner * lam_tile + lag_sum_ref[lag : lag + 1, :]
             packed_ref[half, index, 0:MODES_TILE, :] = before
             packed_ref[half, index, MODES_TILE : 2 * MODES_TILE, :] = after
@@ -374,7 +380,6 @@
     halves = modes // MODES_TILE
     there = pl.BlockSpec(memory_space=pltpu.HBM)
     border = jax.ShapeDtypeStruct((blocks, halves, MODES_TILE * SUBS, LANES), F32)
-    square = pltpu.VMEM((tokens + SPARE, LANES), F32)
     tile = pltpu.VMEM((MODES_TILE * SUBS + SPARE, LANES), F32)
     staged = pltpu.VMEM((blocks, halves, MODES_TILE * SUBS + SPARE, LANES), F32)
     signal_buffer = pltpu.VMEM((tokens, channels), signals[0].dtype)
@@ -394,8 +399,9 @@
             pltpu.SemaphoreType.DMA((3, len(STATE_BLOCKS))),
             pltpu.VMEM((SUBS * PITCH + 2 * SPARE, LANES), F32),
             pltpu.VMEM((SUBS * PITCH + 2 * SPARE, LANES), F32),
-            square,
-            pltpu.VMEM((tokens // SUBS, LANES), F32),
+            tile,
+            pltpu.VMEM((tokens // SUBS // 2, LANES), F32),
+            tile,
             tile,
             tile,
         ],

time: 64.7 us -> 64.3 us (level)
  no operation moved by 1% of the time
where the time goes in v7:
time: 64.3 us; the launch traced here: 63.8 us
  blocking collectives  19.9 us (31%)
  Pallas kernels  18.6 us (29%)
  starting transfers between devices  15.6 us (24%)
  waiting for transfers between devices  8.15 us (13%)
  between operations  0.73 us (1%)
  other arithmetic  0.68 us (1%)
    all_to_all x1, blocking collectives, on_device(): lax.all_to_all(repacked, 'ctx', split_axis=0, concat_axis=0, tiled=True)  19.9 us
    all_to_all x1, starting transfers between devices, on_device(): lax.all_to_all(packed.reshape(ctx_count, 3 * MODES_TILE, LANES), 'ctx', s...  11.4 us
    pallas_call x1, Pallas kernels, on_device(): pl.pallas_call(local_kernel, grid=(GROUPS,), in_specs=[signal_spec] * 4 +...  8.44 us
    all_to_all x1, waiting for transfers between devices, on_device(): lax.all_to_all(packed.reshape(ctx_count, 3 * MODES_TILE, LANES), 'ctx', s...  6.24 us
    pallas_call x1, Pallas kernels, states_call(): pl.pallas_call(states_kernel, in_specs=[there] * 5, out_specs=[there] * 3...  6.17 us
    pallas_call x1, Pallas kernels, outputs_call(): pl.pallas_call(output_kernel, in_specs=[here] * 5 + [there] * 2 + [here],...  3.9 us
    ppermute x1, starting transfers between devices, on_device(): lax.ppermute(tiles, 'seq', [(i, i ^ 6) for i in range(seq_count)])  2.29 us
    ppermute x3, starting transfers between devices, on_device(): lax.ppermute(part, 'seq', [(i, i ^ flip) for i in range(seq_count)])  1.94 us
  transfers between devices with their start and end apart: 5, of which 4 were waited for; matrix products, arithmetic and copies ran while one was open for 0% of the time, Pallas kernels for 19%

profile of v7, /device:TPU:32, one launch (start us, length us, event | category | flops | bytes accessed | tf_op | source)
XLA Modules:
  0.0 63.8 jit_solution(9108910936502984886)
XLA Ops:
  0.6 6.2 %states.1 = (f32[2,16,24,128]{3,2,1,0:T(8,128)}, f32[16,2,64,128]{3,2,1,0:T(8,128)}, f32[16,2,64,128]{3,2,1,0:T(8,128)}) custom-call(bf16[128,2048]{1,0:T(8,128)(2,1)} %bitcast.19, bf16[128,2048]{1,0:T(8,128)(2,1)} %bitcast.22, bf16[128,2048]{1,0:T(8,128)(2,1)} %bitcast.25, bf16[128,2048]{1,0:T(8,128)(2,1)} %bitcast.28, f32[16,2048]{1,0:T(8,128)} %bitcast.32), custom_call_target="tpu_custom_call" | custom-call | flops 25165824 | bytes 4194304 | tf_op jit(solution)/shard_map/states/pallas_call | solution.py:386
  6.8 11.4 %all-to-all-start = ((f32[32,24,128]{2,1,0:T(8,128)}), f32[32,24,128]{2,1,0:T(8,128)S(1)}, u32[]{:S(2)}, u32[]{:S(2)}) async-start(f32[32,24,128]{2,1,0:T(8,128)} %bitcast.38), calls=%async_computation | async-start | bytes 786432 | tf_op jit(solution)/shard_map/all_to_all | solution.py:454
  18.2 0.0 copy-start.4
  18.2 0.0 copy-start.5
  18.2 8.4 %local.1 = (f32[128,2048]{1,0:T(8,128)}, f32[128,2048]{1,0:T(8,128)}) custom-call(bf16[128,2048]{1,0:T(8,128)(2,1)} %bitcast.20, bf16[128,2048]{1,0:T(8,128)(2,1)} %bitcast.23, bf16[128,2048]{1,0:T(8,128)(2,1)} %bitcast.26, bf16[128,2048]{1,0:T(8,128)(2,1)} %bitcast.29, f32[16,2048]{1,0:T(8,128)} %bitcast.33, f32[16,2048]{1,0:T(8,128)} %bitcast.36, ...), custom_call_target="tpu_custom_call" | custom-call | flops 33554432 | bytes 6291456 | tf_op jit(solution)/shard_map/local/pallas_call | solution.py:462
  26.7 6.2 %all-to-all-done.states_ref = f32[32,24,128]{2,1,0:T(8,128)S(1)} async-done(((f32[32,24,128]{2,1,0:T(8,128)}), f32[32,24,128]{2,1,0:T(8,128)S(1)}, u32[]{:S(2)}, u32[]{:S(2)}) %all-to-all-start) | async-done | bytes 393248 | tf_op jit(solution)/shard_map/all_to_all | solution.py:454
  32.9 0.0 copy-done.4
  32.9 0.1 scan.1
  33.0 0.1 collective-permute-start.2
  33.1 1.6 %collective-permute-start.1 = (f32[8,128]{1,0:T(8,128)S(1)}, f32[8,128]{1,0:T(8,128)S(1)}, u32[]{:S(2)}, u32[]{:S(2)}) collective-permute-start(f32[8,128]{1,0:T(8,128)S(1)} %get-tuple-element.28), channel_id=1, source_target_pairs={{0,2},{1,3},{2,0},{3,1},{4,6},{5,7},{6,4},{7,5},{8,10},{9,11},{10,... | collective-permute-start | bytes 12296 | tf_op jit(solution)/shard_map/ppermute | solution.py:487
  34.7 0.3 collective-permute-start
  35.0 1.2 %collective-permute-done.2 = f32[8,128]{1,0:T(8,128)S(1)} collective-permute-done((f32[8,128]{1,0:T(8,128)S(1)}, f32[8,128]{1,0:T(8,128)S(1)}, u32[]{:S(2)}, u32[]{:S(2)}) %collective-permute-start.2) | collective-permute-done | bytes 4128 | tf_op jit(solution)/shard_map/ppermute | solution.py:487
  36.1 0.7 %collective-permute-done.1 = f32[8,128]{1,0:T(8,128)S(1)} collective-permute-done((f32[8,128]{1,0:T(8,128)S(1)}, f32[8,128]{1,0:T(8,128)S(1)}, u32[]{:S(2)}, u32[]{:S(2)}) %collective-permute-start.1) | collective-permute-done | bytes 4128 | tf_op jit(solution)/shard_map/ppermute | solution.py:487
  36.8 0.0 collective-permute-done
  36.8 0.0 copy-start.2
  36.9 0.0 copy-start
  36.9 0.0 copy-start.1
  36.9 19.9 %all_to_all.10 = f32[32,24,128]{2,1,0:T(8,128)S(1)} all-to-all(f32[32,24,128]{2,1,0:T(8,128)S(1)} %pack.1), channel_id=1, replica_groups=mesh['ctx'=32,'seq'=8] {'ctx'}, dimensions={0} | all-to-all | bytes 786432 | tf_op jit(solution)/shard_map/all_to_all | solution.py:498
  56.8 2.3 %collective-permute-start.3 = (f32[32,8,128]{2,1,0:T(8,128)S(1)}, f32[32,8,128]{2,1,0:T(8,128)S(1)}, u32[]{:S(2)}, u32[]{:S(2)}) collective-permute-start(f32[32,8,128]{2,1,0:T(8,128)S(1)} %slice.4), channel_id=1, source_target_pairs={{0,6},{1,7},{2,4},{3,5},{4,2},{5,3},{6,0},{7,1},{8,14},{9,15},{10,... | collective-permute-start | bytes 393224 | tf_op jit(solution)/shard_map/ppermute | solution.py:503
  59.1 0.0 copy-done.2
  59.1 0.0 copy-done.1
  59.1 3.9 %outputs.1 = (bf16[128,2048]{1,0:T(8,128)(2,1)}, bf16[128,2048]{1,0:T(8,128)(2,1)}, bf16[128,2048]{1,0:T(8,128)(2,1)}, bf16[128,2048]{1,0:T(8,128)(2,1)}) custom-call(bf16[128,2048]{1,0:T(8,128)(2,1)S(1)} %bitcast.21, bf16[128,2048]{1,0:T(8,128)(2,1)S(1)} %bitcast.24, bf16[128,2048]{1,0:T(8,128)(2,1)S(1)} %bitcast.27, bf16[128,2048]{1,0:T(8,128)(2,1)S(1)} %bitcast.30, ...), custom_call_target="tpu_custom_call" | custom-call | flops 16777216 | bytes 6291456 | tf_op jit(solution)/shard_map/outputs/pallas_call | solution.py:421
  63.0 0.1 collective-permute-done.3
  63.1 0.7 %slice_add_fusion = f32[32,8,128]{2,1,0:T(8,128)} fusion(f32[32,8,128]{2,1,0:T(8,128)S(1)} %collective-permute-done.3, f32[32,24,128]{2,1,0:T(8,128)S(1)} %all_to_all.10), kind=kLoop, calls=%fused_computation.1 | loop fusion | flops 32768 | bytes 393216 | tf_op jit(solution)/shard_map/add | solution.py:503
  (7 shorter events, 0.1 us)
Async XLA Ops:
  6.8 26.1 %all-to-all-start = ((f32[32,24,128]{2,1,0:T(8,128)}), f32[32,24,128]{2,1,0:T(8,128)S(1)}, u32[]{:S(2)}, u32[]{:S(2)}) async-start(f32[32,24,128]{2,1,0:T(8,128)} %bitcast.38), calls=%async_computation | async-start | bytes 786432 | tf_op jit(solution)/shard_map/all_to_all | solution.py:454
  18.2 14.7 %copy-start.4 = (f32[2048,16]{0,1:T(8,128)S(1)}, f32[2048,16]{0,1:T(8,128)}, u32[]{:S(2)}) copy-start(f32[2048,16]{0,1:T(8,128)} %param.11) | copy-start | bytes 393220
  18.2 14.7 %copy-start.5 = (f32[2048,16]{0,1:T(8,128)S(1)}, f32[2048,16]{0,1:T(8,128)}, u32[]{:S(2)}) copy-start(f32[2048,16]{0,1:T(8,128)} %param.10) | copy-start | bytes 393220
  32.9 26.2 %copy-start.3 = (bf16[1,128,2048]{2,1,0:T(8,128)(2,1)S(1)}, bf16[1,128,2048]{2,1,0:T(8,128)(2,1)}, u32[]{:S(2)}) copy-start(bf16[1,128,2048]{2,1,0:T(8,128)(2,1)} %param.9) | copy-start | bytes 1572868
  33.0 3.1 %collective-permute-start.2 = (f32[8,128]{1,0:T(8,128)S(1)}, f32[8,128]{1,0:T(8,128)S(1)}, u32[]{:S(2)}, u32[]{:S(2)}) collective-permute-start(f32[8,128]{1,0:T(8,128)S(1)} %get-tuple-element.28), channel_id=1, source_target_pairs={{0,3},{1,2},{2,1},{3,0},{4,7},{5,6},{6,5},{7,4},{8,11},{9,10},{10,... | collective-permute-start | bytes 12296 | tf_op jit(solution)/shard_map/ppermute | solution.py:487
  33.1 3.7 %collective-permute-start.1 = (f32[8,128]{1,0:T(8,128)S(1)}, f32[8,128]{1,0:T(8,128)S(1)}, u32[]{:S(2)}, u32[]{:S(2)}) collective-permute-start(f32[8,128]{1,0:T(8,128)S(1)} %get-tuple-element.28), channel_id=1, source_target_pairs={{0,2},{1,3},{2,0},{3,1},{4,6},{5,7},{6,4},{7,5},{8,10},{9,11},{10,... | collective-permute-start | bytes 12296 | tf_op jit(solution)/shard_map/ppermute | solution.py:487
  34.7 2.1 %collective-permute-start = (f32[8,128]{1,0:T(8,128)S(1)}, f32[8,128]{1,0:T(8,128)S(1)}, u32[]{:S(2)}, u32[]{:S(2)}) collective-permute-start(f32[8,128]{1,0:T(8,128)S(1)} %get-tuple-element.28), channel_id=1, source_target_pairs={{0,1},{1,0},{2,3},{3,2},{4,5},{5,4},{6,7},{7,6},{8,9},{9,8},{10,11... | collective-permute-start | bytes 12296 | tf_op jit(solution)/shard_map/ppermute | solution.py:487
  36.8 22.3 %copy-start.2 = (bf16[1,128,2048]{2,1,0:T(8,128)(2,1)S(1)}, bf16[1,128,2048]{2,1,0:T(8,128)(2,1)}, u32[]{:S(2)}) copy-start(bf16[1,128,2048]{2,1,0:T(8,128)(2,1)} %param.8) | copy-start | bytes 1572868
  36.9 22.3 %copy-start = (bf16[1,128,2048]{2,1,0:T(8,128)(2,1)S(1)}, bf16[1,128,2048]{2,1,0:T(8,128)(2,1)}, u32[]{:S(2)}) copy-start(bf16[1,128,2048]{2,1,0:T(8,128)(2,1)} %param.6) | copy-start | bytes 1572868
  36.9 22.3 %copy-start.1 = (bf16[1,128,2048]{2,1,0:T(8,128)(2,1)S(1)}, bf16[1,128,2048]{2,1,0:T(8,128)(2,1)}, u32[]{:S(2)}) copy-start(bf16[1,128,2048]{2,1,0:T(8,128)(2,1)} %param.7) | copy-start | bytes 1572868
  56.8 6.3 %collective-permute-start.3 = (f32[32,8,128]{2,1,0:T(8,128)S(1)}, f32[32,8,128]{2,1,0:T(8,128)S(1)}, u32[]{:S(2)}, u32[]{:S(2)}) collective-permute-start(f32[32,8,128]{2,1,0:T(8,128)S(1)} %slice.4), channel_id=1, source_target_pairs={{0,6},{1,7},{2,4},{3,5},{4,2},{5,3},{6,0},{7,1},{8,14},{9,15},{10,... | collective-permute-start | bytes 393224 | tf_op jit(solution)/shard_map/ppermute | solution.py:503

commit v8 on v7

--- a/solution.py
+++ b/solution.py
@@ -319,28 +319,24 @@
 
     def entry(index, carry):
         lanes = pl.ds(pl.multiple_of(index * LANES, LANES), LANES)
-        for half in range(modes // MODES_TILE):
-            picked = slice(half * MODES_TILE, (half + 1) * MODES_TILE)
-            rates = rates_ref[picked, lanes]
-            row = rows_of(rates)
-            jump = rows_of(jnp.exp(rates * -float(SUBS)))
-            early = rows_of(entry_ref[half, index, 0:MODES_TILE, :])
-            late = rows_of(entry_ref[half, index, MODES_TILE : 2 * MODES_TILE, :])
-            fwd = [early[m] * jnp.exp(-row[m] * sub) for m in range(MODES_TILE)]
-            bwd = [late[m] * jnp.exp(-row[m] * (SUBS - 1 - sub)) for m in range(MODES_TILE)]
+        rates = [
+            rates_ref[half * MODES_TILE : (half + 1) * MODES_TILE, lanes]
+            for half in range(modes // MODES_TILE)
+        ]
+        for part, place, target in ((0, sub, y_ref), (1, SUBS - 1 - sub, g_ref)):
+            state, jump = [], []
+            for half, rate in enumerate(rates):
+                row = rows_of(rate)
+                jump += rows_of(jnp.exp(rate * -float(SUBS)))
+                start = rows_of(entry_ref[half, index, part * MODES_TILE : (part + 1) * MODES_TILE, :])
+                state += [start[m] * jnp.exp(-row[m] * place) for m in range(MODES_TILE)]
             for i in range(groups):
-                rows = slice(i * SUBS, (i + 1) * SUBS)
-                total = y_ref[rows, lanes] if half else None
-                for m in range(MODES_TILE):
-                    total = fwd[m] if total is None else total + fwd[m]
-                    fwd[m] = fwd[m] * jump[m]
-                y_ref[rows, lanes] = total
-                rows = slice((groups - 1 - i) * SUBS, (groups - i) * SUBS)
-                total = g_ref[rows, lanes] if half else None
-                for m in range(MODES_TILE):
-                    total = bwd[m] if total is None else total + bwd[m]
-                    bwd[m] = bwd[m] * jump[m]
-                g_ref[rows, lanes] = total
+                at = groups - 1 - i if part else i
+                total = state[0]
+                for term in state[1:]:
+                    total = total + term
+                target[at * SUBS : (at + 1) * SUBS, lanes] = total
+                state = [s * j for s, j in zip(state, jump, strict=True)]
         return carry
 
     def finish(index, carry):

time: 64.3 us -> 64.3 us (level)
  transfers between devices with their start and end apart: 5 -> 5, of which waited for: 4 -> 3; matrix products, arithmetic and copies ran while one was open for 0% -> 0% of each run, Pallas kernels for 19% -> 19%
where the time goes in v8:
time: 64.3 us; the launch traced here: 63.8 us
  blocking collectives  19.9 us (31%)
  Pallas kernels  18.7 us (29%)
  starting transfers between devices  15.6 us (24%)
  waiting for transfers between devices  8.1 us (13%)
  between operations  0.73 us (1%)
  other arithmetic  0.68 us (1%)
    all_to_all x1, blocking collectives, on_device(): lax.all_to_all(repacked, 'ctx', split_axis=0, concat_axis=0, tiled=True)  19.9 us
    all_to_all x1, starting transfers between devices, on_device(): lax.all_to_all(packed.reshape(ctx_count, 3 * MODES_TILE, LANES), 'ctx', s...  11.4 us
    pallas_call x1, Pallas kernels, on_device(): pl.pallas_call(local_kernel, grid=(GROUPS,), in_specs=[signal_spec] * 4 +...  8.44 us
    all_to_all x1, waiting for transfers between devices, on_device(): lax.all_to_all(packed.reshape(ctx_count, 3 * MODES_TILE, LANES), 'ctx', s...  6.24 us
    pallas_call x1, Pallas kernels, states_call(): pl.pallas_call(states_kernel, in_specs=[there] * 5, out_specs=[there] * 3...  6.17 us
    pallas_call x1, Pallas kernels, outputs_call(): pl.pallas_call(output_kernel, in_specs=[here] * 5 + [there] * 2 + [here],...  3.95 us
    ppermute x1, starting transfers between devices, on_device(): lax.ppermute(tiles, 'seq', [(i, i ^ 6) for i in range(seq_count)])  2.29 us
    ppermute x3, starting transfers between devices, on_device(): lax.ppermute(part, 'seq', [(i, i ^ flip) for i in range(seq_count)])  1.94 us
  transfers between devices with their start and end apart: 5, of which 3 were waited for; matrix products, arithmetic and copies ran while one was open for 0% of the time, Pallas kernels for 19%

profile of v8, /device:TPU:32, one launch (start us, length us, event | category | flops | bytes accessed | tf_op | source)
XLA Modules:
  0.0 63.8 jit_solution(12774241993958968753)
XLA Ops:
  0.6 6.2 %states.1 = (f32[2,16,24,128]{3,2,1,0:T(8,128)}, f32[16,2,64,128]{3,2,1,0:T(8,128)}, f32[16,2,64,128]{3,2,1,0:T(8,128)}) custom-call(bf16[128,2048]{1,0:T(8,128)(2,1)} %bitcast.19, bf16[128,2048]{1,0:T(8,128)(2,1)} %bitcast.22, bf16[128,2048]{1,0:T(8,128)(2,1)} %bitcast.25, bf16[128,2048]{1,0:T(8,128)(2,1)} %bitcast.28, f32[16,2048]{1,0:T(8,128)} %bitcast.32), custom_call_target="tpu_custom_call" | custom-call | flops 25165824 | bytes 4194304 | tf_op jit(solution)/shard_map/states/pallas_call | solution.py:382
  6.8 11.4 %all-to-all-start = ((f32[32,24,128]{2,1,0:T(8,128)}), f32[32,24,128]{2,1,0:T(8,128)S(1)}, u32[]{:S(2)}, u32[]{:S(2)}) async-start(f32[32,24,128]{2,1,0:T(8,128)} %bitcast.38), calls=%async_computation | async-start | bytes 786432 | tf_op jit(solution)/shard_map/all_to_all | solution.py:450
  18.2 0.0 copy-start.4
  18.2 0.0 copy-start.5
  18.2 8.4 %local.1 = (f32[128,2048]{1,0:T(8,128)}, f32[128,2048]{1,0:T(8,128)}) custom-call(bf16[128,2048]{1,0:T(8,128)(2,1)} %bitcast.20, bf16[128,2048]{1,0:T(8,128)(2,1)} %bitcast.23, bf16[128,2048]{1,0:T(8,128)(2,1)} %bitcast.26, bf16[128,2048]{1,0:T(8,128)(2,1)} %bitcast.29, f32[16,2048]{1,0:T(8,128)} %bitcast.33, f32[16,2048]{1,0:T(8,128)} %bitcast.36, ...), custom_call_target="tpu_custom_call" | custom-call | flops 33554432 | bytes 6291456 | tf_op jit(solution)/shard_map/local/pallas_call | solution.py:458
  26.7 6.2 %all-to-all-done.states_ref = f32[32,24,128]{2,1,0:T(8,128)S(1)} async-done(((f32[32,24,128]{2,1,0:T(8,128)}), f32[32,24,128]{2,1,0:T(8,128)S(1)}, u32[]{:S(2)}, u32[]{:S(2)}) %all-to-all-start) | async-done | bytes 393248 | tf_op jit(solution)/shard_map/all_to_all | solution.py:450
  32.9 0.0 copy-done.4
  32.9 0.0 copy-done.5
  32.9 0.1 scan.1
  33.0 0.1 collective-permute-start.2
  33.1 1.6 %collective-permute-start.1 = (f32[8,128]{1,0:T(8,128)S(1)}, f32[8,128]{1,0:T(8,128)S(1)}, u32[]{:S(2)}, u32[]{:S(2)}) collective-permute-start(f32[8,128]{1,0:T(8,128)S(1)} %get-tuple-element.28), channel_id=1, source_target_pairs={{0,2},{1,3},{2,0},{3,1},{4,6},{5,7},{6,4},{7,5},{8,10},{9,11},{10,... | collective-permute-start | bytes 12296 | tf_op jit(solution)/shard_map/ppermute | solution.py:483
  34.7 0.3 collective-permute-start
  35.0 1.2 %collective-permute-done.2 = f32[8,128]{1,0:T(8,128)S(1)} collective-permute-done((f32[8,128]{1,0:T(8,128)S(1)}, f32[8,128]{1,0:T(8,128)S(1)}, u32[]{:S(2)}, u32[]{:S(2)}) %collective-permute-start.2) | collective-permute-done | bytes 4128 | tf_op jit(solution)/shard_map/ppermute | solution.py:483
  36.1 0.7 %collective-permute-done.1 = f32[8,128]{1,0:T(8,128)S(1)} collective-permute-done((f32[8,128]{1,0:T(8,128)S(1)}, f32[8,128]{1,0:T(8,128)S(1)}, u32[]{:S(2)}, u32[]{:S(2)}) %collective-permute-start.1) | collective-permute-done | bytes 4128 | tf_op jit(solution)/shard_map/ppermute | solution.py:483
  36.8 0.0 collective-permute-done
  36.8 0.0 copy-start.2
  36.9 0.0 copy-start
  36.9 0.0 copy-start.1
  36.9 19.9 %all_to_all.10 = f32[32,24,128]{2,1,0:T(8,128)S(1)} all-to-all(f32[32,24,128]{2,1,0:T(8,128)S(1)} %pack.1), channel_id=1, replica_groups=mesh['ctx'=32,'seq'=8] {'ctx'}, dimensions={0} | all-to-all | bytes 786432 | tf_op jit(solution)/shard_map/all_to_all | solution.py:494
  56.8 2.3 %collective-permute-start.3 = (f32[32,8,128]{2,1,0:T(8,128)S(1)}, f32[32,8,128]{2,1,0:T(8,128)S(1)}, u32[]{:S(2)}, u32[]{:S(2)}) collective-permute-start(f32[32,8,128]{2,1,0:T(8,128)S(1)} %slice.4), channel_id=1, source_target_pairs={{0,6},{1,7},{2,4},{3,5},{4,2},{5,3},{6,0},{7,1},{8,14},{9,15},{10,... | collective-permute-start | bytes 393224 | tf_op jit(solution)/shard_map/ppermute | solution.py:499
  59.1 0.0 copy-done.2
  59.1 4.0 %outputs.1 = (bf16[128,2048]{1,0:T(8,128)(2,1)}, bf16[128,2048]{1,0:T(8,128)(2,1)}, bf16[128,2048]{1,0:T(8,128)(2,1)}, bf16[128,2048]{1,0:T(8,128)(2,1)}) custom-call(bf16[128,2048]{1,0:T(8,128)(2,1)S(1)} %bitcast.21, bf16[128,2048]{1,0:T(8,128)(2,1)S(1)} %bitcast.24, bf16[128,2048]{1,0:T(8,128)(2,1)S(1)} %bitcast.27, bf16[128,2048]{1,0:T(8,128)(2,1)S(1)} %bitcast.30, ...), custom_call_target="tpu_custom_call" | custom-call | flops 16777216 | bytes 6291456 | tf_op jit(solution)/shard_map/outputs/pallas_call | solution.py:417
  63.1 0.0 collective-permute-done.3
  63.1 0.7 %slice_add_fusion = f32[32,8,128]{2,1,0:T(8,128)} fusion(f32[32,8,128]{2,1,0:T(8,128)S(1)} %collective-permute-done.3, f32[32,24,128]{2,1,0:T(8,128)S(1)} %all_to_all.10), kind=kLoop, calls=%fused_computation.1 | loop fusion | flops 32768 | bytes 393216 | tf_op jit(solution)/shard_map/add | solution.py:499
  (7 shorter events, 0.1 us)
Async XLA Ops:
  6.8 26.1 %all-to-all-start = ((f32[32,24,128]{2,1,0:T(8,128)}), f32[32,24,128]{2,1,0:T(8,128)S(1)}, u32[]{:S(2)}, u32[]{:S(2)}) async-start(f32[32,24,128]{2,1,0:T(8,128)} %bitcast.38), calls=%async_computation | async-start | bytes 786432 | tf_op jit(solution)/shard_map/all_to_all | solution.py:450
  18.2 14.7 %copy-start.4 = (f32[2048,16]{0,1:T(8,128)S(1)}, f32[2048,16]{0,1:T(8,128)}, u32[]{:S(2)}) copy-start(f32[2048,16]{0,1:T(8,128)} %param.11) | copy-start | bytes 393220
  18.2 14.7 %copy-start.5 = (f32[2048,16]{0,1:T(8,128)S(1)}, f32[2048,16]{0,1:T(8,128)}, u32[]{:S(2)}) copy-start(f32[2048,16]{0,1:T(8,128)} %param.10) | copy-start | bytes 393220
  32.9 26.2 %copy-start.3 = (bf16[1,128,2048]{2,1,0:T(8,128)(2,1)S(1)}, bf16[1,128,2048]{2,1,0:T(8,128)(2,1)}, u32[]{:S(2)}) copy-start(bf16[1,128,2048]{2,1,0:T(8,128)(2,1)} %param.9) | copy-start | bytes 1572868
  33.0 3.1 %collective-permute-start.2 = (f32[8,128]{1,0:T(8,128)S(1)}, f32[8,128]{1,0:T(8,128)S(1)}, u32[]{:S(2)}, u32[]{:S(2)}) collective-permute-start(f32[8,128]{1,0:T(8,128)S(1)} %get-tuple-element.28), channel_id=1, source_target_pairs={{0,3},{1,2},{2,1},{3,0},{4,7},{5,6},{6,5},{7,4},{8,11},{9,10},{10,... | collective-permute-start | bytes 12296 | tf_op jit(solution)/shard_map/ppermute | solution.py:483
  33.1 3.7 %collective-permute-start.1 = (f32[8,128]{1,0:T(8,128)S(1)}, f32[8,128]{1,0:T(8,128)S(1)}, u32[]{:S(2)}, u32[]{:S(2)}) collective-permute-start(f32[8,128]{1,0:T(8,128)S(1)} %get-tuple-element.28), channel_id=1, source_target_pairs={{0,2},{1,3},{2,0},{3,1},{4,6},{5,7},{6,4},{7,5},{8,10},{9,11},{10,... | collective-permute-start | bytes 12296 | tf_op jit(solution)/shard_map/ppermute | solution.py:483
  34.7 2.1 %collective-permute-start = (f32[8,128]{1,0:T(8,128)S(1)}, f32[8,128]{1,0:T(8,128)S(1)}, u32[]{:S(2)}, u32[]{:S(2)}) collective-permute-start(f32[8,128]{1,0:T(8,128)S(1)} %get-tuple-element.28), channel_id=1, source_target_pairs={{0,1},{1,0},{2,3},{3,2},{4,5},{5,4},{6,7},{7,6},{8,9},{9,8},{10,11... | collective-permute-start | bytes 12296 | tf_op jit(solution)/shard_map/ppermute | solution.py:483
  36.8 22.3 %copy-start.2 = (bf16[1,128,2048]{2,1,0:T(8,128)(2,1)S(1)}, bf16[1,128,2048]{2,1,0:T(8,128)(2,1)}, u32[]{:S(2)}) copy-start(bf16[1,128,2048]{2,1,0:T(8,128)(2,1)} %param.8) | copy-start | bytes 1572868
  36.9 22.3 %copy-start = (bf16[1,128,2048]{2,1,0:T(8,128)(2,1)S(1)}, bf16[1,128,2048]{2,1,0:T(8,128)(2,1)}, u32[]{:S(2)}) copy-start(bf16[1,128,2048]{2,1,0:T(8,128)(2,1)} %param.6) | copy-start | bytes 1572868
  36.9 22.3 %copy-start.1 = (bf16[1,128,2048]{2,1,0:T(8,128)(2,1)S(1)}, bf16[1,128,2048]{2,1,0:T(8,128)(2,1)}, u32[]{:S(2)}) copy-start(bf16[1,128,2048]{2,1,0:T(8,128)(2,1)} %param.7) | copy-start | bytes 1572868
  56.8 6.3 %collective-permute-start.3 = (f32[32,8,128]{2,1,0:T(8,128)S(1)}, f32[32,8,128]{2,1,0:T(8,128)S(1)}, u32[]{:S(2)}, u32[]{:S(2)}) collective-permute-start(f32[32,8,128]{2,1,0:T(8,128)S(1)} %slice.4), channel_id=1, source_target_pairs={{0,6},{1,7},{2,4},{3,5},{4,2},{5,3},{6,0},{7,1},{8,14},{9,15},{10,... | collective-permute-start | bytes 393224 | tf_op jit(solution)/shard_map/ppermute | solution.py:499

commit v9 on v7

--- a/solution.py
+++ b/solution.py
@@ -12,7 +12,7 @@
 SPARE = 8
 MODES_TILE = 8
 F32 = jnp.float32
-GROUPS = 4
+LOCAL_STEPS = 2
 OUTPUT_COLUMNS = 2
 STATE_BLOCKS = (4, 4, 4, 4)
 AHEAD = 2
@@ -455,13 +455,13 @@
         packed.reshape(ctx_count, 3 * MODES_TILE, LANES), "ctx", split_axis=0, concat_axis=0, tiled=True
     )
 
-    per_step = blocks // GROUPS
+    per_step = blocks // LOCAL_STEPS
     signal_spec = pl.BlockSpec((tokens, per_step * LANES), lambda i: (0, i))
     mode_spec = pl.BlockSpec((modes, per_step * LANES), lambda i: (0, i))
     border_spec = pl.BlockSpec((per_step, halves, MODES_TILE * SUBS, LANES), lambda i: (i, 0, 0, 0))
     conv, grad = pl.pallas_call(
         local_kernel,
-        grid=(GROUPS,),
+        grid=(LOCAL_STEPS,),
         in_specs=[signal_spec] * 4 + [mode_spec] * 2 + [border_spec] * 2,
         out_specs=[signal_spec] * 2,
         out_shape=[whole] * 2,

time: 64.3 us -> 64.3 us (level)
  transfers between devices with their start and end apart: 5 -> 5, of which waited for: 4 -> 4; matrix products, arithmetic and copies ran while one was open for 0% -> 0% of each run, Pallas kernels for 19% -> 20%
where the time goes in v9:
time: 64.3 us; the launch traced here: 63.8 us
  blocking collectives  19.9 us (31%)
  Pallas kernels  19.2 us (30%)
  starting transfers between devices  15.6 us (24%)
  waiting for transfers between devices  7.57 us (12%)
  between operations  0.73 us (1%)
  other arithmetic  0.68 us (1%)
    all_to_all x1, blocking collectives, on_device(): lax.all_to_all(repacked, 'ctx', split_axis=0, concat_axis=0, tiled=True)  19.9 us
    all_to_all x1, starting transfers between devices, on_device(): lax.all_to_all(packed.reshape(ctx_count, 3 * MODES_TILE, LANES), 'ctx', s...  11.4 us
    pallas_call x1, Pallas kernels, on_device(): pl.pallas_call(local_kernel, grid=(LOCAL_STEPS,), in_specs=[signal_spec]...  9.02 us
    pallas_call x1, Pallas kernels, states_call(): pl.pallas_call(states_kernel, in_specs=[there] * 5, out_specs=[there] * 3...  6.17 us
    all_to_all x1, waiting for transfers between devices, on_device(): lax.all_to_all(packed.reshape(ctx_count, 3 * MODES_TILE, LANES), 'ctx', s...  5.66 us
    pallas_call x1, Pallas kernels, outputs_call(): pl.pallas_call(output_kernel, in_specs=[here] * 5 + [there] * 2 + [here],...  3.9 us
    ppermute x1, starting transfers between devices, on_device(): lax.ppermute(tiles, 'seq', [(i, i ^ 6) for i in range(seq_count)])  2.29 us
    ppermute x3, starting transfers between devices, on_device(): lax.ppermute(part, 'seq', [(i, i ^ flip) for i in range(seq_count)])  1.94 us
  transfers between devices with their start and end apart: 5, of which 4 were waited for; matrix products, arithmetic and copies ran while one was open for 0% of the time, Pallas kernels for 20%

profile of v9, /device:TPU:32, one launch (start us, length us, event | category | flops | bytes accessed | tf_op | source)
XLA Modules:
  0.0 63.8 jit_solution(18269667478992739409)
XLA Ops:
  0.6 6.2 %states.1 = (f32[2,16,24,128]{3,2,1,0:T(8,128)}, f32[16,2,64,128]{3,2,1,0:T(8,128)}, f32[16,2,64,128]{3,2,1,0:T(8,128)}) custom-call(bf16[128,2048]{1,0:T(8,128)(2,1)} %bitcast.19, bf16[128,2048]{1,0:T(8,128)(2,1)} %bitcast.22, bf16[128,2048]{1,0:T(8,128)(2,1)} %bitcast.25, bf16[128,2048]{1,0:T(8,128)(2,1)} %bitcast.28, f32[16,2048]{1,0:T(8,128)} %bitcast.32), custom_call_target="tpu_custom_call" | custom-call | flops 25165824 | bytes 4194304 | tf_op jit(solution)/shard_map/states/pallas_call | solution.py:386
  6.8 11.4 %all-to-all-start = ((f32[32,24,128]{2,1,0:T(8,128)}), f32[32,24,128]{2,1,0:T(8,128)S(1)}, u32[]{:S(2)}, u32[]{:S(2)}) async-start(f32[32,24,128]{2,1,0:T(8,128)} %bitcast.38), calls=%async_computation | async-start | bytes 786432 | tf_op jit(solution)/shard_map/all_to_all | solution.py:454
  18.2 0.0 copy-start.4
  18.2 0.0 copy-start.5
  18.2 9.0 %local.1 = (f32[128,2048]{1,0:T(8,128)}, f32[128,2048]{1,0:T(8,128)}) custom-call(bf16[128,2048]{1,0:T(8,128)(2,1)} %bitcast.20, bf16[128,2048]{1,0:T(8,128)(2,1)} %bitcast.23, bf16[128,2048]{1,0:T(8,128)(2,1)} %bitcast.26, bf16[128,2048]{1,0:T(8,128)(2,1)} %bitcast.29, f32[16,2048]{1,0:T(8,128)} %bitcast.33, f32[16,2048]{1,0:T(8,128)} %bitcast.36, ...), custom_call_target="tpu_custom_call" | custom-call | flops 33554432 | bytes 6291456 | tf_op jit(solution)/shard_map/local/pallas_call | solution.py:462
  27.2 5.7 %all-to-all-done.states_ref = f32[32,24,128]{2,1,0:T(8,128)S(1)} async-done(((f32[32,24,128]{2,1,0:T(8,128)}), f32[32,24,128]{2,1,0:T(8,128)S(1)}, u32[]{:S(2)}, u32[]{:S(2)}) %all-to-all-start) | async-done | bytes 393248 | tf_op jit(solution)/shard_map/all_to_all | solution.py:454
  32.9 0.0 copy-done.4
  32.9 0.1 scan.1
  33.0 0.1 collective-permute-start.2
  33.1 1.6 %collective-permute-start.1 = (f32[8,128]{1,0:T(8,128)S(1)}, f32[8,128]{1,0:T(8,128)S(1)}, u32[]{:S(2)}, u32[]{:S(2)}) collective-permute-start(f32[8,128]{1,0:T(8,128)S(1)} %get-tuple-element.28), channel_id=1, source_target_pairs={{0,2},{1,3},{2,0},{3,1},{4,6},{5,7},{6,4},{7,5},{8,10},{9,11},{10,... | collective-permute-start | bytes 12296 | tf_op jit(solution)/shard_map/ppermute | solution.py:487
  34.7 0.3 collective-permute-start
  35.0 1.2 %collective-permute-done.2 = f32[8,128]{1,0:T(8,128)S(1)} collective-permute-done((f32[8,128]{1,0:T(8,128)S(1)}, f32[8,128]{1,0:T(8,128)S(1)}, u32[]{:S(2)}, u32[]{:S(2)}) %collective-permute-start.2) | collective-permute-done | bytes 4128 | tf_op jit(solution)/shard_map/ppermute | solution.py:487
  36.1 0.7 %collective-permute-done.1 = f32[8,128]{1,0:T(8,128)S(1)} collective-permute-done((f32[8,128]{1,0:T(8,128)S(1)}, f32[8,128]{1,0:T(8,128)S(1)}, u32[]{:S(2)}, u32[]{:S(2)}) %collective-permute-start.1) | collective-permute-done | bytes 4128 | tf_op jit(solution)/shard_map/ppermute | solution.py:487
  36.8 0.0 collective-permute-done
  36.8 0.0 copy-start.2
  36.9 0.0 copy-start
  36.9 0.0 copy-start.1
  36.9 19.9 %all_to_all.10 = f32[32,24,128]{2,1,0:T(8,128)S(1)} all-to-all(f32[32,24,128]{2,1,0:T(8,128)S(1)} %pack.1), channel_id=1, replica_groups=mesh['ctx'=32,'seq'=8] {'ctx'}, dimensions={0} | all-to-all | bytes 786432 | tf_op jit(solution)/shard_map/all_to_all | solution.py:498
  56.8 2.3 %collective-permute-start.3 = (f32[32,8,128]{2,1,0:T(8,128)S(1)}, f32[32,8,128]{2,1,0:T(8,128)S(1)}, u32[]{:S(2)}, u32[]{:S(2)}) collective-permute-start(f32[32,8,128]{2,1,0:T(8,128)S(1)} %slice.4), channel_id=1, source_target_pairs={{0,6},{1,7},{2,4},{3,5},{4,2},{5,3},{6,0},{7,1},{8,14},{9,15},{10,... | collective-permute-start | bytes 393224 | tf_op jit(solution)/shard_map/ppermute | solution.py:503
  59.1 0.0 copy-done.2
  59.1 0.0 copy-done.1
  59.1 3.9 %outputs.1 = (bf16[128,2048]{1,0:T(8,128)(2,1)}, bf16[128,2048]{1,0:T(8,128)(2,1)}, bf16[128,2048]{1,0:T(8,128)(2,1)}, bf16[128,2048]{1,0:T(8,128)(2,1)}) custom-call(bf16[128,2048]{1,0:T(8,128)(2,1)S(1)} %bitcast.21, bf16[128,2048]{1,0:T(8,128)(2,1)S(1)} %bitcast.24, bf16[128,2048]{1,0:T(8,128)(2,1)S(1)} %bitcast.27, bf16[128,2048]{1,0:T(8,128)(2,1)S(1)} %bitcast.30, ...), custom_call_target="tpu_custom_call" | custom-call | flops 16777216 | bytes 6291456 | tf_op jit(solution)/shard_map/outputs/pallas_call | solution.py:421
  63.0 0.1 collective-permute-done.3
  63.1 0.7 %slice_add_fusion = f32[32,8,128]{2,1,0:T(8,128)} fusion(f32[32,8,128]{2,1,0:T(8,128)S(1)} %collective-permute-done.3, f32[32,24,128]{2,1,0:T(8,128)S(1)} %all_to_all.10), kind=kLoop, calls=%fused_computation.1 | loop fusion | flops 32768 | bytes 393216 | tf_op jit(solution)/shard_map/add | solution.py:503
  (7 shorter events, 0.1 us)
Async XLA Ops:
  6.8 26.1 %all-to-all-start = ((f32[32,24,128]{2,1,0:T(8,128)}), f32[32,24,128]{2,1,0:T(8,128)S(1)}, u32[]{:S(2)}, u32[]{:S(2)}) async-start(f32[32,24,128]{2,1,0:T(8,128)} %bitcast.38), calls=%async_computation | async-start | bytes 786432 | tf_op jit(solution)/shard_map/all_to_all | solution.py:454
  18.2 14.7 %copy-start.4 = (f32[2048,16]{0,1:T(8,128)S(1)}, f32[2048,16]{0,1:T(8,128)}, u32[]{:S(2)}) copy-start(f32[2048,16]{0,1:T(8,128)} %param.11) | copy-start | bytes 393220
  18.2 14.7 %copy-start.5 = (f32[2048,16]{0,1:T(8,128)S(1)}, f32[2048,16]{0,1:T(8,128)}, u32[]{:S(2)}) copy-start(f32[2048,16]{0,1:T(8,128)} %param.10) | copy-start | bytes 393220
  32.9 26.2 %copy-start.3 = (bf16[1,128,2048]{2,1,0:T(8,128)(2,1)S(1)}, bf16[1,128,2048]{2,1,0:T(8,128)(2,1)}, u32[]{:S(2)}) copy-start(bf16[1,128,2048]{2,1,0:T(8,128)(2,1)} %param.9) | copy-start | bytes 1572868
  33.0 3.1 %collective-permute-start.2 = (f32[8,128]{1,0:T(8,128)S(1)}, f32[8,128]{1,0:T(8,128)S(1)}, u32[]{:S(2)}, u32[]{:S(2)}) collective-permute-start(f32[8,128]{1,0:T(8,128)S(1)} %get-tuple-element.28), channel_id=1, source_target_pairs={{0,3},{1,2},{2,1},{3,0},{4,7},{5,6},{6,5},{7,4},{8,11},{9,10},{10,... | collective-permute-start | bytes 12296 | tf_op jit(solution)/shard_map/ppermute | solution.py:487
  33.1 3.7 %collective-permute-start.1 = (f32[8,128]{1,0:T(8,128)S(1)}, f32[8,128]{1,0:T(8,128)S(1)}, u32[]{:S(2)}, u32[]{:S(2)}) collective-permute-start(f32[8,128]{1,0:T(8,128)S(1)} %get-tuple-element.28), channel_id=1, source_target_pairs={{0,2},{1,3},{2,0},{3,1},{4,6},{5,7},{6,4},{7,5},{8,10},{9,11},{10,... | collective-permute-start | bytes 12296 | tf_op jit(solution)/shard_map/ppermute | solution.py:487
  34.7 2.1 %collective-permute-start = (f32[8,128]{1,0:T(8,128)S(1)}, f32[8,128]{1,0:T(8,128)S(1)}, u32[]{:S(2)}, u32[]{:S(2)}) collective-permute-start(f32[8,128]{1,0:T(8,128)S(1)} %get-tuple-element.28), channel_id=1, source_target_pairs={{0,1},{1,0},{2,3},{3,2},{4,5},{5,4},{6,7},{7,6},{8,9},{9,8},{10,11... | collective-permute-start | bytes 12296 | tf_op jit(solution)/shard_map/ppermute | solution.py:487
  36.8 22.3 %copy-start.2 = (bf16[1,128,2048]{2,1,0:T(8,128)(2,1)S(1)}, bf16[1,128,2048]{2,1,0:T(8,128)(2,1)}, u32[]{:S(2)}) copy-start(bf16[1,128,2048]{2,1,0:T(8,128)(2,1)} %param.8) | copy-start | bytes 1572868
  36.9 22.3 %copy-start = (bf16[1,128,2048]{2,1,0:T(8,128)(2,1)S(1)}, bf16[1,128,2048]{2,1,0:T(8,128)(2,1)}, u32[]{:S(2)}) copy-start(bf16[1,128,2048]{2,1,0:T(8,128)(2,1)} %param.6) | copy-start | bytes 1572868
  36.9 22.3 %copy-start.1 = (bf16[1,128,2048]{2,1,0:T(8,128)(2,1)S(1)}, bf16[1,128,2048]{2,1,0:T(8,128)(2,1)}, u32[]{:S(2)}) copy-start(bf16[1,128,2048]{2,1,0:T(8,128)(2,1)} %param.7) | copy-start | bytes 1572868
  56.8 6.3 %collective-permute-start.3 = (f32[32,8,128]{2,1,0:T(8,128)S(1)}, f32[32,8,128]{2,1,0:T(8,128)S(1)}, u32[]{:S(2)}, u32[]{:S(2)}) collective-permute-start(f32[32,8,128]{2,1,0:T(8,128)S(1)} %slice.4), channel_id=1, source_target_pairs={{0,6},{1,7},{2,4},{3,5},{4,2},{5,3},{6,0},{7,1},{8,14},{9,15},{10,... | collective-permute-start | bytes 393224 | tf_op jit(solution)/shard_map/ppermute | solution.py:503
